TPU v7x, 32 devices: a whole 2x2x4 slice. The times are simulated.
32 devices in a mesh: stream: 4 (over y, x), cross: 8 (over z, core).
Axes of the slice: x: 2, y: 2, z: 4, core: 2. Of those that a mesh axis runs over, the one named last changes fastest.
Arguments:
- velocity: bfloat16 [128, 3, 48, 64, 128], P(None, None, 'stream', 'cross'), may hold values from -40 to 40, as said below
- metric_x: float32 [48], P('stream'), may hold values from 0.5 to 2
- metric_y: float32 [64], P('cross'), may hold values from 0.5 to 2
- metric_z: float32 [128], replicated, may hold values from 0.5 to 2
Outputs:
- modes: bfloat16 [128, 4, 48, 64, 128], P(None, None, 'stream', 'cross')
- factor: float32 [128, 128], replicated
Inputs may be any that keep to these rules, and one draw needn't show every extreme that they name: velocity snapshots share a common part across snapshots.
All inputs are finite; a program needn't handle non-finite values.
Results may differ from a plain program's by a relative error of at most 0.0023.
The roundings to bfloat16 on the way count: a program that leaves them out, or rounds other values in their place, can miss the bound.
Values may be sent and summed in bfloat16 or wider, within the bound.
No kernel may reach another device: no remote copies, remote signals or barrier semaphores. Data moves between devices by JAX's collectives and lax.ppermute only.
A program may use at most 128 MiB of HBM per device.

v0:
```python
import jax
import jax.numpy as jnp
from jax import lax
from jax.sharding import PartitionSpec as P


def with_halo(cells, sides, width):
    for axis, dim in sides:
        count = lax.axis_size(axis)
        ends = count - 1
        head = lax.slice_in_dim(cells, 0, width, axis=dim)
        tail = lax.slice_in_dim(cells, cells.shape[dim] - width, cells.shape[dim], axis=dim)
        cells = jnp.concatenate(
            [
                lax.ppermute(tail, axis, [(i, (i + 1) % count) for i in range(ends)]),
                cells,
                lax.ppermute(head, axis, [((i + 1) % count, i) for i in range(ends)]),
            ],
            axis=dim,
        )
    return cells


def central(padded, axis):
    count = padded.shape[axis] - 4

    def part_at(offset):
        return lax.slice_in_dim(padded, offset, offset + count, axis=axis)

    return (8.0 * (part_at(3) - part_at(1)) - (part_at(4) - part_at(0))) / 12.0


def fields(along_x, along_y, interior, metric_x, metric_y, metric_z):

    def deriv_x(comp):
        return central(along_x[:, comp].astype(jnp.float32), 1) * metric_x[:, None, None]

    def deriv_y(comp):
        return central(along_y[:, comp].astype(jnp.float32), 2) * metric_y[:, None]

    def deriv_z(comp):
        inner = interior[:, comp].astype(jnp.float32)
        return central(jnp.pad(inner, ((0, 0), (0, 0), (0, 0), (2, 2))), 3) * metric_z

    vort_x = deriv_y(2) - deriv_z(1)
    vort_y = deriv_z(0) - deriv_x(2)
    vort_z = deriv_x(1) - deriv_y(0)
    dilatation = deriv_x(0) + deriv_y(1) + deriv_z(2)
    return jnp.stack([vort_x, vort_y, vort_z, dilatation], axis=1).astype(jnp.bfloat16)


def inner_products(flat):
    return lax.dot_general(flat, flat, (((1,), (1,)), ((), ())), preferred_element_type=jnp.float32)


def global_factor(flat, scale):
    local = inner_products(flat)
    gram = lax.psum(local, ("stream", "cross"))
    lower = jnp.linalg.cholesky(gram * scale)
    return lower


def shards(velocity, metric_x, metric_y, metric_z):
    snaps, comps, cells_x, cells_y, cells_z = velocity.shape
    groups = snaps // 8
    plain = velocity.reshape(groups, 8, comps, cells_x, cells_y, cells_z)
    stream_pad = with_halo(velocity, (("stream", 2),), 2)
    cross_pad = with_halo(velocity, (("cross", 3),), 2)
    stream_groups = stream_pad.reshape(groups, 8, comps, cells_x + 4, cells_y, cells_z)
    cross_groups = cross_pad.reshape(groups, 8, comps, cells_x, cells_y + 4, cells_z)

    def one_face_group(pieces):
        return fields(pieces[0], pieces[1], pieces[2], metric_x, metric_y, metric_z)

    stacked = lax.map(one_face_group, (stream_groups, cross_groups, plain))
    flat = stacked.reshape(snaps, 4 * cells_x * cells_y * cells_z)
    total_rows = (
        4.0 * cells_x * lax.axis_size("stream") * cells_y * lax.axis_size("cross") * cells_z
    )
    scale = 1.0 / total_rows
    lower = global_factor(flat, scale)
    identity = jnp.eye(snaps, dtype=jnp.float32)
    inverse = jax.scipy.linalg.solve_triangular(lower, identity, lower=True)
    basis = jnp.dot(inverse.astype(jnp.bfloat16), flat, preferred_element_type=jnp.float32).astype(
        jnp.bfloat16
    )
    return (basis.reshape(snaps, 4, cells_x, cells_y, cells_z), lower)


def solution(mesh):
    return jax.shard_map(
        shards,
        mesh=mesh,
        in_specs=(P(None, None, "stream", "cross", None), P("stream"), P("cross"), P()),
        out_specs=(P(None, None, "stream", "cross", None), P()),
        check_vma=False,
    )
```

profile of v0, /device:TPU:0, one launch (start us, length us, event | category | flops | bytes accessed | tf_op | source)
XLA Modules:
  0.0 423.0 jit_solution(14111133597748029114)
XLA Ops:
  7.2 4.1 fusion.49
  11.3 6.0 %collective-permute-start.2 = (bf16[128,3,2,8,128]{4,3,2,1,0:T(8,128)(2,1)}, bf16[128,3,2,8,128]{4,3,2,1,0:T(8,128)(2,1)}, u32[]{:S(2)}, u32[]{:S(2)}) collective-permute-start(bf16[128,3,2,8,128]{4,3,2,1,0:T(8,128)(2,1)} %get-tuple-element.143), channel_id=1, source_target_pairs={{0,8},{8,16},{16,24},{1,9},{9,17},{17,25},{2,10},{10,18},{18,26},{... | collective-permute-start | bytes 4718600 | tf_op jit(solution)/shard_map/ppermute | solution.py:15
  17.3 1.3 collective-permute-start.3
  18.6 11.0 %copy.14 = bf16[128,3,12,8,128]{4,0,3,2,1:T(8,128)(2,1)} copy(bf16[128,3,12,8,128]{4,3,2,1,0:T(8,128)(2,1)} %param.6) | data formatting | bytes 18874368 | tf_op args[0]
  29.5 6.5 %fusion.50 = (bf16[128,3,12,2,128]{4,0,3,2,1:T(8,128)(2,1)}, bf16[128,3,12,2,128]{4,0,3,2,1:T(8,128)(2,1)}) fusion(bf16[128,3,12,8,128]{4,0,3,2,1:T(8,128)(2,1)} %copy.14), kind=kLoop, calls=%fused_computation.102 | loop fusion | bytes 9437184 | tf_op jit(solution)/shard_map/slice | solution.py:12
  36.0 2.9 collective-permute-start
  38.9 1.3 collective-permute-start.1
  40.2 9.9 %collective-permute-done.2 = bf16[128,3,2,8,128]{4,3,2,1,0:T(8,128)(2,1)} collective-permute-done((bf16[128,3,2,8,128]{4,3,2,1,0:T(8,128)(2,1)}, bf16[128,3,2,8,128]{4,3,2,1,0:T(8,128)(2,1)}, u32[]{:S(2)}, u32[]{:S(2)}) %collective-permute-start.2) | collective-permute-done | bytes 1572896 | tf_op jit(solution)/shard_map/ppermute | solution.py:15
  50.1 35.7 %collective-permute-done.3 = bf16[128,3,2,8,128]{4,3,2,1,0:T(8,128)(2,1)} collective-permute-done((bf16[128,3,2,8,128]{4,3,2,1,0:T(8,128)(2,1)}, bf16[128,3,2,8,128]{4,3,2,1,0:T(8,128)(2,1)}, u32[]{:S(2)}, u32[]{:S(2)}) %collective-permute-start.3) | collective-permute-done | bytes 1572896 | tf_op jit(solution)/shard_map/ppermute | solution.py:17
  85.7 10.7 %pad_maximum_fusion = bf16[128,3,16,8,128]{4,3,2,1,0:T(8,128)(2,1)} fusion(bf16[128,3,2,8,128]{4,3,2,1,0:T(8,128)(2,1)} %collective-permute-done.3, bf16[128,3,12,8,128]{4,3,2,1,0:T(8,128)(2,1)} %param.6, bf16[128,3,2,8,128]{4,3,2,1,0:T(8,128)(2,1)} %collective-permute-done.2), kind=kLoop, calls=%fused_computation.88 | loop fusion | flops 12582912 | bytes 25165824 | tf_op jit(solution)/shard_map/concatenate | solution.py:13
  96.5 9.3 %maximum_bitcast_fusion = bf16[16,8,3,12,12,128]{5,1,0,4,3,2:T(8,128)(2,1)} fusion(bf16[128,3,12,2,128]{4,0,3,2,1:T(8,128)(2,1)} %collective-permute-done.1, bf16[128,3,12,8,128]{4,0,3,2,1:T(8,128)(2,1)S(1)} %bitcast.101, bf16[128,3,12,2,128]{4,0,3,2,1:T(8,128)(2,1)} %collective-permute-done), kind=kLoop, calls=%fused_computation.87 | loop fusion | flops 14155776 | bytes 28311552 | tf_op jit(solution)/shard_map/reshape | solution.py:70
  105.8 113.5 %while.12 = (s32[]{:T(128)}, bf16[16,8,4,12,8,128]{5,4,3,2,1,0:T(8,128)(2,1)}, bf16[16,8,3,12,12,128]{5,1,0,4,3,2:T(8,128)(2,1)}, f32[8]{0:T(128)S(1)}, bf16[16,...) while((s32[]{:T(128)}, ...), condition=%wide.region_1.2_spmd, body=%wide.region_0.1_spmd.sunk | while | flops 9594006 | bytes 30810576 | solution.py:75
  105.8 1.2 constant_dynamic-slice_fusion.10
  112.9 1.2 constant_dynamic-slice_fusion.10
  127.1 1.2 constant_dynamic-slice_fusion.10
  134.2 1.2 constant_dynamic-slice_fusion.10
  141.3 1.2 constant_dynamic-slice_fusion.10
  148.4 1.2 constant_dynamic-slice_fusion.10
  155.5 1.2 constant_dynamic-slice_fusion.10
  162.6 1.2 constant_dynamic-slice_fusion.10
  169.7 1.2 constant_dynamic-slice_fusion.10
  176.8 1.2 constant_dynamic-slice_fusion.10
  183.9 1.2 constant_dynamic-slice_fusion.10
  190.9 1.2 constant_dynamic-slice_fusion.10
  219.3 17.0 %reshape.128 = bf16[128,49152]{1,0:T(8,128)(2,1)} reshape(bf16[16,8,4,12,8,128]{5,4,3,2,1,0:T(8,128)(2,1)} %get-tuple-element.103) | data formatting | bytes 25165824 | tf_op jit(solution)/shard_map/reshape | solution.py:76
  236.4 12.2 %fusion.51 = f32[128,128]{0,1:T(8,128)} fusion(bf16[128,49152]{1,0:T(8,128)(2,1)} %reshape.128), kind=kOutput, calls=%fused_computation.103 | convolution fusion | flops 1610612736 | bytes 12648448 | tf_op jit(solution)/shard_map/dot_general | solution.py:53
  248.6 118.0 %all-reduce.5.cloned.1.call-done = f32[128,128]{0,1:T(8,128)} async-done(((f32[128,128]{0,1:T(8,128)}), f32[128,128]{0,1:T(8,128)}) %all-reduce.5.cloned.1.call-update) | async-done | bytes 65552 | tf_op jit(solution)/shard_map/psum | solution.py:58
  368.4 11.7 %cholesky.17 = f32[128,128]{1,0:T(8,128)S(1)} custom-call(f32[128,128]{1,0:T(8,128)S(1)} %fusion.48), custom_call_target="Cholesky" | custom-call | tf_op jit(solution)/shard_map/jit(cholesky)/cholesky | solution.py:59
  380.8 1.3 select_bitcast_fusion
  382.1 9.8 %custom-call.7 = f32[1,128,128]{1,2,0:T(8,128)S(1)} custom-call(f32[1,128,128]{2,1,0:T(8,128)S(1)} %get-tuple-element.128), custom_call_target="InvertDiagBlocksLowerTriangular" | custom-call | tf_op jit(solution)/shard_map/jit(_solve_triangular)/triangular_solve | solution.py:83
  392.1 12.5 %fusion.46 = bf16[16,8,384,128]{3,1,2,0:T(8,128)(2,1)} fusion(bf16[128,128]{1,0:T(8,128)(2,1)S(1)} %convolution_convert_fusion.1, bf16[128,49152]{1,0:T(8,128)(2,1)} %reshape.128), kind=kOutput, calls=%fused_computation.89 | convolution fusion | flops 1616904192 | bytes 25198592 | tf_op jit(solution)/shard_map/dot_general | solution.py:84
  404.6 11.6 %copy.26 = bf16[16,8,384,128]{3,2,1,0:T(8,128)(2,1)} copy(bf16[16,8,384,128]{3,1,2,0:T(8,128)(2,1)} %fusion.46) | data formatting | bytes 25165824
  (268 shorter events, 99.9 us)
Async XLA Ops:
  7.2 359.4 %all-reduce.5.cloned.1.call-start = ((), (), s32[]{:S(2)}) async-start(), calls=%async_computation | async-start | bytes 131072 | tf_op jit(solution)/shard_map/psum | solution.py:58
  11.3 38.8 %collective-permute-start.2 = (bf16[128,3,2,8,128]{4,3,2,1,0:T(8,128)(2,1)}, bf16[128,3,2,8,128]{4,3,2,1,0:T(8,128)(2,1)}, u32[]{:S(2)}, u32[]{:S(2)}) collective-permute-start(bf16[128,3,2,8,128]{4,3,2,1,0:T(8,128)(2,1)} %get-tuple-element.143), channel_id=1, source_target_pairs={{0,8},{8,16},{16,24},{1,9},{9,17},{17,25},{2,10},{10,18},{18,26},{... | collective-permute-start | bytes 4718600 | tf_op jit(solution)/shard_map/ppermute | solution.py:15
  17.3 68.5 %collective-permute-start.3 = (bf16[128,3,2,8,128]{4,3,2,1,0:T(8,128)(2,1)}, bf16[128,3,2,8,128]{4,3,2,1,0:T(8,128)(2,1)}, u32[]{:S(2)}, u32[]{:S(2)}) collective-permute-start(bf16[128,3,2,8,128]{4,3,2,1,0:T(8,128)(2,1)} %get-tuple-element.144), channel_id=1, source_target_pairs={{8,0},{16,8},{24,16},{9,1},{17,9},{25,17},{10,2},{18,10},{26,18},{... | collective-permute-start | bytes 4718600 | tf_op jit(solution)/shard_map/ppermute | solution.py:17
  36.0 60.4 %collective-permute-start = (bf16[128,3,12,2,128]{4,0,3,2,1:T(8,128)(2,1)}, bf16[128,3,12,2,128]{4,0,3,2,1:T(8,128)(2,1)}, u32[]{:S(2)}, u32[]{:S(2)}) collective-permute-start(bf16[128,3,12,2,128]{4,0,3,2,1:T(8,128)(2,1)} %get-tuple-element.145), channel_id=1, source_target_pairs={{0,1},{1,2},{2,3},{3,4},{4,5},{5,6},{6,7},{8,9},{9,10},{10,11},{11... | collective-permute-start | bytes 7077896 | tf_op jit(solution)/shard_map/ppermute | solution.py:15
  38.9 57.5 %collective-permute-start.1 = (bf16[128,3,12,2,128]{4,0,3,2,1:T(8,128)(2,1)}, bf16[128,3,12,2,128]{4,0,3,2,1:T(8,128)(2,1)}, u32[]{:S(2)}, u32[]{:S(2)}) collective-permute-start(bf16[128,3,12,2,128]{4,0,3,2,1:T(8,128)(2,1)} %get-tuple-element.146), channel_id=1, source_target_pairs={{1,0},{2,1},{3,2},{4,3},{5,4},{6,5},{7,6},{9,8},{10,9},{11,10},{12... | collective-permute-start | bytes 7077896 | tf_op jit(solution)/shard_map/ppermute | solution.py:17
  40.2 56.2 %slice-start = ((s8[9437184]{0:T(1024)(128)(4,1)}), s8[1048576]{0:T(1024)(128)(4,1)S(1)}, s32[]{:S(2)}) async-start(s8[9437184]{0:T(1024)(128)(4,1)} %bitcast.100), calls=%async_computation.1 | async-start | bytes 2097152
  40.2 56.2 %slice-start.1 = ((s8[9437184]{0:T(1024)(128)(4,1)}), s8[4194304]{0:T(1024)(128)(4,1)S(1)}, s32[]{:S(2)}) async-start(s8[9437184]{0:T(1024)(128)(4,1)} %bitcast.100), calls=%async_computation.2 | async-start | bytes 8388608
  40.2 56.2 %slice-start.2 = ((s8[9437184]{0:T(1024)(128)(4,1)}), s8[4194304]{0:T(1024)(128)(4,1)S(1)}, s32[]{:S(2)}) async-start(s8[9437184]{0:T(1024)(128)(4,1)} %bitcast.100), calls=%async_computation.3 | async-start | bytes 8388608
  96.4 9.4 %copy-start = (f32[8]{0:T(128)S(1)}, f32[8]{0:T(128)}, u32[]{:S(2)}) copy-start(f32[8]{0:T(128)} %param.8) | copy-start | bytes 100
  96.4 9.4 %copy-start.1 = (f32[128]{0:T(128)S(1)}, f32[128]{0:T(128)}, u32[]{:S(2)}) copy-start(f32[128]{0:T(128)} %param.9) | copy-start | bytes 1540
  96.4 9.4 %copy-start.2 = (f32[12]{0:T(128)S(1)}, f32[12]{0:T(128)}, u32[]{:S(2)}) copy-start(f32[12]{0:T(128)} %param.7) | copy-start | bytes 148
Sparse Core Ops, SparseCore 0:
  248.7 117.8 all-reduce.4
where the time goes:
time: 428 us; the launch traced here: 423 us
  waiting for transfers between devices  164 us (38%)
  local copies, waits for them, and re-layouts  112 us (26%)
  other arithmetic  95.3 us (22%)
  matrix products  24.9 us (6%)
  between operations  14.2 us (3%)
  starting transfers between devices  11.5 us (3%)
    psum x1, waiting for transfers between devices, global_factor(): gram = lax.psum(local, ('stream', 'cross'))  118 us
    squeeze x32, local copies, waits for them, and re-layouts, shards(): stacked = lax.map(one_face_group, (stream_groups, cross_groups, plain))  37.1 us
    ppermute x2, waiting for transfers between devices, with_halo(): lax.ppermute(head, axis, [((i + 1) % count, i) for i in range(ends)])  35.7 us
    dynamic_slice x32, local copies, waits for them, and re-layouts, shards(): stacked = lax.map(one_face_group, (stream_groups, cross_groups, plain))  24 us
    unnamed x14, local copies, waits for them, and re-layouts  22.6 us
    another operation x48, other arithmetic, fields(): jnp.stack([vort_x, vort_y, vort_z, dilatation], axis=1).astype(jnp.bfloat16)  21.8 us
    reshape x1, local copies, waits for them, and re-layouts, shards(): flat = stacked.reshape(snaps, 4 * cells_x * cells_y * cells_z)  17 us
    dynamic_update_slice x16, other arithmetic, shards(): stacked = lax.map(one_face_group, (stream_groups, cross_groups, plain))  15 us
  transfers between devices with their start and end apart: 5, of which 3 were waited for; matrix products, arithmetic and copies ran while one was open for 7% of the time, Pallas kernels for 0%

commit v1 on v0

v1 whole, which is shorter than its diff:
```python
import functools

import jax
import jax.numpy as jnp
from jax import lax
from jax.experimental import pallas as pl
from jax.experimental.pallas import tpu as pltpu
from jax.sharding import PartitionSpec as P

F32, BF16 = jnp.float32, jnp.bfloat16
VMEM_LIMIT = 56 * 1024 * 1024


def params():
    return pltpu.CompilerParams(vmem_limit_bytes=VMEM_LIMIT)


def planes_kernel(cells_ref, out_ref, rows):
    snaps, _, layers, cells_y, cells_z = cells_ref.shape
    for layer in range(layers):
        rows[...] = cells_ref[:, 0, layer].astype(F32).reshape(snaps * cells_y, cells_z)
        for y in range(cells_y):
            out_ref[0, layer, y] = rows[pl.ds(y, snaps, stride=cells_y), :].astype(BF16)


def planes(velocity, picks, width):
    snaps, comps, _, cells_y, cells_z = velocity.shape
    first, count, step = picks
    return pl.pallas_call(
        planes_kernel,
        grid=(comps, count),
        in_specs=[
            pl.BlockSpec(
                (snaps, 1, width, cells_y, cells_z), lambda c, i: (0, c, first + step * i, 0, 0)
            )
        ],
        out_specs=pl.BlockSpec(
            (1, width, cells_y, snaps, cells_z), lambda c, i: (c, i, 0, 0, 0)
        ),
        out_shape=jax.ShapeDtypeStruct((comps, count * width, cells_y, snaps, cells_z), BF16),
        scratch_shapes=[pltpu.VMEM((snaps * cells_y, cells_z), F32)],
        compiler_params=params(),
    )(velocity)


ROWS = 16


def layer_fields(ring, slots, rz, low, high, metric_x, metric_y_ref, metric_z, out_ref):
    cells_y, snaps, cells_z = ring.shape[2:]
    back2, back1, here, fore1, fore2 = slots

    def some_rows(step, _):
        at = pl.ds(pl.multiple_of(step * ROWS, ROWS), ROWS)

        def row(comp, y):
            if y < 0:
                return low[comp, 0, y + 2, at, :].astype(F32)
            if y >= cells_y:
                return high[comp, 0, y - cells_y, at, :].astype(F32)
            return ring[here, comp, y, at, :]

        window = [[row(c, y) for y in range(-2, 2)] for c in range(3)]
        for y in range(cells_y):
            for c in range(3):
                window[c].append(row(c, y + 2))

            def along_x(c):
                near = ring[fore1, c, y, at, :] - ring[back1, c, y, at, :]
                far = ring[fore2, c, y, at, :] - ring[back2, c, y, at, :]
                return (8.0 * near - far) * metric_x

            def along_y(c):
                w = window[c]
                return (8.0 * (w[3] - w[1]) - (w[4] - w[0])) * metric_y_ref[y]

            def along_z(c):
                return rz[c, y, at, :] * metric_z

            outs = (
                along_y(2) - along_z(1),
                along_z(0) - along_x(2),
                along_x(1) - along_y(0),
                along_x(0) + along_y(1) + along_z(2),
            )
            for f, value in enumerate(outs):
                lane = (f * cells_y + y) * cells_z
                out_ref[0, at, lane : lane + cells_z] = value.astype(BF16)
            for c in range(3):
                window[c] = window[c][1:]
        return 0

    lax.fori_loop(0, snaps // ROWS, some_rows, 0)


def fields_kernel(span, pick, n_layers, mx_ref, my_ref, mz_ref, taps_ref, *rest):
    layer_refs = rest[:n_layers]
    low_ref, high_ref, out_ref, gram_ref, ring, rz_ring = rest[n_layers:]
    i = pl.program_id(0)
    j = lax.rem(i, span)
    cells_y, snaps, cells_z = ring.shape[2:]

    @pl.when(i == 0)
    def _():
        gram_ref[...] = jnp.zeros_like(gram_ref)

    def take(ref):
        block = ref[:, 0]
        ring[lax.rem(j, 5)] = block.astype(F32)

        @pl.when((j >= 2) & (j < span - 2))
        def _():
            flat = block.reshape(3 * cells_y * snaps, cells_z)
            rz_ring[lax.rem(j, 3)] = jnp.dot(
                flat, taps_ref[...], preferred_element_type=F32
            ).reshape(3, cells_y, snaps, cells_z)

    which = pick(i)
    for k, ref in enumerate(layer_refs):
        pl.when(which == k)(functools.partial(take, ref))

    @pl.when(j >= 4)
    def _():
        slots = [lax.rem(j + 1 + k, 5) for k in range(5)]
        layer_fields(
            ring,
            slots,
            rz_ring.at[lax.rem(j - 2, 3)],
            low_ref,
            high_ref,
            mx_ref[i],
            my_ref,
            mz_ref[...],
            out_ref,
        )
        done = out_ref[0]
        gram_ref[...] += lax.dot_general(
            done, done, (((1,), (1,)), ((), ())), preferred_element_type=F32
        )


def fields(sources, pick, maps, segments, span, center, low, high, metric_x, metric_y, metric_z):
    comps, _, cells_y, snaps, cells_z = sources[0].shape
    taps = jnp.zeros((cells_z, cells_z), F32)
    for shift, weight in ((1, 8.0), (-1, -8.0), (2, -1.0), (-2, 1.0)):
        taps = taps + weight * jnp.eye(cells_z, k=-shift, dtype=F32)
    steps = segments * span
    lanes = 4 * cells_y * cells_z
    kept = span - 4

    def out_index(i):
        return (i // span) * kept + jnp.maximum(lax.rem(i, span) - 4, 0)

    halo_spec = pl.BlockSpec((comps, 1, 2, snaps, cells_z), lambda i: (0, center(i), 0, 0, 0))
    return pl.pallas_call(
        functools.partial(fields_kernel, span, pick, len(sources)),
        grid=(steps,),
        in_specs=[
            pl.BlockSpec(memory_space=pltpu.SMEM),
            pl.BlockSpec(memory_space=pltpu.SMEM),
            pl.BlockSpec((1, cells_z), lambda i: (0, 0)),
            pl.BlockSpec((cells_z, cells_z), lambda i: (0, 0)),
        ]
        + [
            pl.BlockSpec(
                (comps, 1, cells_y, snaps, cells_z),
                functools.partial(lambda m, i: (0, m(i), 0, 0, 0), m),
            )
            for m in maps
        ]
        + [halo_spec, halo_spec],
        out_specs=[
            pl.BlockSpec((1, snaps, lanes), lambda i: (out_index(i), 0, 0)),
            pl.BlockSpec((snaps, snaps), lambda i: (0, 0)),
        ],
        out_shape=[
            jax.ShapeDtypeStruct((segments * kept, snaps, lanes), BF16),
            jax.ShapeDtypeStruct((snaps, snaps), F32),
        ],
        scratch_shapes=[
            pltpu.VMEM((5, comps, cells_y, snaps, cells_z), F32),
            pltpu.VMEM((3, comps, cells_y, snaps, cells_z), F32),
        ],
        compiler_params=params(),
    )(
        metric_x[jnp.array([center(i) for i in range(steps)])] / 12.0,
        metric_y / 12.0,
        metric_z[None, :] / 12.0,
        taps.astype(BF16),
        *sources,
        low,
        high,
    )


def modes_kernel(pick, n_sources, inverse_ref, *rest):
    sources, (out_ref, rows) = rest[:n_sources], rest[n_sources:]
    snaps, comps, _, cells_y, cells_z = out_ref.shape
    width = cells_y * cells_z
    which = pick(pl.program_id(0))

    def take(ref):
        for f in range(comps):
            whole = jnp.dot(
                inverse_ref[...], ref[0, :, f * width : (f + 1) * width], preferred_element_type=F32
            )
            for y in range(cells_y):
                rows[pl.ds(y, snaps, stride=cells_y), :] = whole[:, y * cells_z : (y + 1) * cells_z]
            out_ref[:, f, 0] = rows[...].reshape(snaps, cells_y, cells_z).astype(BF16)

    for k, ref in enumerate(sources):
        pl.when(which == k)(functools.partial(take, ref))


def modes(inverse, sources, pick, maps, cells_x, cells_y, cells_z):
    snaps = inverse.shape[0]
    lanes = sources[0].shape[2]
    return pl.pallas_call(
        functools.partial(modes_kernel, pick, len(sources)),
        grid=(cells_x,),
        in_specs=[pl.BlockSpec((snaps, snaps), lambda i: (0, 0))]
        + [
            pl.BlockSpec((1, snaps, lanes), functools.partial(lambda m, i: (m(i), 0, 0), m))
            for m in maps
        ],
        out_specs=pl.BlockSpec((snaps, 4, 1, cells_y, cells_z), lambda i: (0, 0, i, 0, 0)),
        out_shape=jax.ShapeDtypeStruct((snaps, 4, cells_x, cells_y, cells_z), BF16),
        scratch_shapes=[pltpu.VMEM((snaps * cells_y, cells_z), F32)],
        compiler_params=params(),
    )(inverse, *sources)


def total(local):
    for axis in ("cross", "stream"):
        count = lax.axis_size(axis)
        if count & (count - 1):
            local = lax.psum(local, axis)
            continue
        step = 1
        while step < count:
            local = local + lax.ppermute(local, axis, [(i, i ^ step) for i in range(count)])
            step *= 2
    return local


def shift(cells, axis, way):
    count = lax.axis_size(axis)
    pairs = [(i, i + way) for i in range(count) if 0 <= i + way < count]
    return lax.ppermute(cells, axis, pairs)


def shards(velocity, metric_x, metric_y, metric_z):
    snaps, comps, cells_x, cells_y, cells_z = velocity.shape
    edges = planes(velocity, (0, 2, cells_x // 2 - 1), 2)
    before = shift(edges[:, 2:], "stream", 1)
    after = shift(edges[:, :2], "stream", -1)
    cells = planes(velocity, (0, cells_x // 2, 1), 2)
    low = shift(cells[:, :, cells_y - 2 :], "cross", 1)
    high = shift(cells[:, :, :2], "cross", -1)

    inner, inner_gram = fields(
        [cells],
        lambda i: 0,
        [lambda i: i],
        1,
        cells_x,
        lambda i: jnp.clip(i - 2, 0, cells_x - 1),
        low,
        high,
        metric_x,
        metric_y,
        metric_z,
    )
    outer, outer_gram = fields(
        [before, cells, after],
        lambda i: jnp.where(i < 2, 0, jnp.where(i < 10, 1, 2)),
        [
            lambda i: jnp.minimum(i, 1),
            lambda i: jnp.where(i < 6, jnp.maximum(i - 2, 0), jnp.minimum(i - 6 + cells_x - 4, cells_x - 1)),
            lambda i: jnp.maximum(i - 10, 0),
        ],
        2,
        6,
        lambda i: jnp.where(i < 6, jnp.maximum(i - 4, 0), jnp.maximum(i - 10, 0) + cells_x - 2),
        low,
        high,
        metric_x,
        metric_y,
        metric_z,
    )
    everywhere = (
        4.0 * cells_x * lax.axis_size("stream") * cells_y * lax.axis_size("cross") * cells_z
    )
    gram = total(inner_gram + outer_gram)
    lower = jnp.linalg.cholesky(gram * (1.0 / everywhere))
    inverse = jax.scipy.linalg.solve_triangular(lower, jnp.eye(snaps, dtype=F32), lower=True)
    basis = modes(
        inverse.astype(BF16),
        [inner, outer],
        lambda i: jnp.where((i >= 2) & (i < cells_x - 2), 0, 1),
        [
            lambda i: jnp.clip(i - 2, 0, cells_x - 5),
            lambda i: jnp.where(i < cells_x - 2, jnp.minimum(i, 1), i - (cells_x - 4)),
        ],
        cells_x,
        cells_y,
        cells_z,
    )
    return basis, lower


def solution(mesh):
    return jax.shard_map(
        shards,
        mesh=mesh,
        in_specs=(P(None, None, "stream", "cross", None), P("stream"), P("cross"), P()),
        out_specs=(P(None, None, "stream", "cross", None), P()),
        check_vma=False,
    )
```

time: 428 us -> 189 us (0.44)
  waiting for transfers between devices: 164 us -> 17.1 us
  local copies, waits for them, and re-layouts: 112 us -> 15.1 us
  Pallas kernels: 0 us -> 72.4 us
  other arithmetic: 95.3 us -> 26.4 us
  starting transfers between devices: 11.5 us -> 54.8 us
  matrix products: 24.9 us -> 0.87 us
  between operations: 14.2 us -> 0.8 us
    psum x1 -> x0, waiting for transfers between devices: 118 us -> none  [global_factor(): gram = lax.psum(local, ('stream', 'cross'))]
    pallas_call x0 -> x5, Pallas kernels: none -> 72.4 us  [the longest x2 35.8 us: fields(): pl.pallas_call(functools.partial(fields_kernel, span, pick, len(sources))...]
    ppermute x4 -> x9, starting transfers between devices: 11.4 us -> 54.8 us  [the longest x5 41.2 us: total(): lax.ppermute(local, axis, [(i, i ^ step) for i in range(count)])]
    squeeze x32 -> x0, local copies, waits for them, and re-layouts: 37.1 us -> none  [shards(): stacked = lax.map(one_face_group, (stream_groups, cross_groups, plain))]
    ppermute x4 -> x9, waiting for transfers between devices: 45.5 us -> 17.1 us  [the longest x5 11 us: total(): lax.ppermute(local, axis, [(i, i ^ step) for i in range(count)])]
    dot_general x2 -> x0, matrix products: 24.7 us -> none  [the longest x1 12.5 us: shards(): jnp.dot(inverse.astype(jnp.bfloat16), flat, preferred_element_type=jnp.fl...]
    dynamic_slice x32 -> x0, local copies, waits for them, and re-layouts: 24 us -> none  [shards(): stacked = lax.map(one_face_group, (stream_groups, cross_groups, plain))]
    another operation x53 -> x5, other arithmetic: 45.2 us -> 23.5 us  [the longest x3 12.4 us: shards(): lower = jnp.linalg.cholesky(gram * (1.0 / everywhere))]
  transfers between devices with their start and end apart: 5 -> 9, of which waited for: 3 -> 7; matrix products, arithmetic and copies ran while one was open for 7% -> 5% of each run, Pallas kernels for 0% -> 14%
where the time goes in v1:
time: 189 us; the launch traced here: 188 us
  Pallas kernels  72.4 us (38%)
  starting transfers between devices  54.8 us (29%)
  other arithmetic  26.4 us (14%)
  waiting for transfers between devices  17.1 us (9%)
  local copies, waits for them, and re-layouts  15.1 us (8%)
    ppermute x5, starting transfers between devices, total(): lax.ppermute(local, axis, [(i, i ^ step) for i in range(count)])  41.2 us
    pallas_call x2, Pallas kernels, fields(): pl.pallas_call(functools.partial(fields_kernel, span, pick, len(sources))...  35.8 us
    pallas_call x2, Pallas kernels, planes(): pl.pallas_call(planes_kernel, grid=(comps, count), in_specs=[pl.BlockSpec...  21 us
    pallas_call x1, Pallas kernels, modes(): pl.pallas_call(functools.partial(modes_kernel, pick, len(sources)), grid=...  15.6 us
    ppermute x4, starting transfers between devices, shift(): return lax.ppermute(cells, axis, pairs)  13.6 us
    another operation x3, other arithmetic, shards(): lower = jnp.linalg.cholesky(gram * (1.0 / everywhere))  12.4 us
    another operation x2, other arithmetic, shards(): jax.scipy.linalg.solve_triangular(lower, jnp.eye(snaps, dtype=F32), lower...  11.1 us
    ppermute x5, waiting for transfers between devices, total(): lax.ppermute(local, axis, [(i, i ^ step) for i in range(count)])  11 us
  transfers between devices with their start and end apart: 9, of which 7 were waited for; matrix products, arithmetic and copies ran while one was open for 5% of the time, Pallas kernels for 14%

profile of v1, /device:TPU:0, one launch (start us, length us, event | category | flops | bytes accessed | tf_op | source)
XLA Modules:
  0.0 187.6 jit_solution(9890047794556585950)
XLA Ops:
  0.6 15.1 %shard_map.59.rest_0_.rest_1_ = bf16[3,12,8,128,128]{4,3,2,1,0:T(8,128)(2,1)} custom-call(bf16[128,3,12,8,128]{4,3,2,1,0:T(8,128)(2,1)} %cells_ref.3), custom_call_target="tpu_custom_call" | custom-call | tf_op jit(solution)/shard_map/pallas_call | solution.py:29
  15.8 6.4 %fusion.2 = (bf16[3,12,2,128,128]{4,3,2,1,0:T(8,128)(2,1)}, bf16[3,12,2,128,128]{4,3,2,1,0:T(8,128)(2,1)}) fusion(bf16[3,12,8,128,128]{4,3,2,1,0:T(8,128)(2,1)} %shard_map.59.rest_0_.rest_1_), kind=kLoop, calls=%fused_computation.28 | loop fusion | bytes 9437184 | tf_op jit(solution)/shard_map/slice | solution.py:259
  22.2 1.3 collective-permute-start.1
  23.5 4.4 %collective-permute-start = (bf16[3,12,2,128,128]{4,3,2,1,0:T(8,128)(2,1)}, bf16[3,12,2,128,128]{4,3,2,1,0:T(8,128)(2,1)}, u32[]{:S(2)}, u32[]{:S(2)}) collective-permute-start(bf16[3,12,2,128,128]{4,3,2,1,0:T(8,128)(2,1)} %get-tuple-element.13), channel_id=1, source_target_pairs={{0,1},{1,2},{2,3},{3,4},{4,5},{5,6},{6,7},{8,9},{9,10},{10,11},{11... | collective-permute-start | bytes 7077896 | tf_op jit(solution)/shard_map/ppermute | solution.py:249
  27.9 5.9 %shard_map.61 = bf16[3,4,8,128,128]{4,3,2,1,0:T(8,128)(2,1)} custom-call(bf16[128,3,12,8,128]{4,3,2,1,0:T(8,128)(2,1)} %cells_ref.3), custom_call_target="tpu_custom_call" | custom-call | tf_op jit(solution)/shard_map/pallas_call | solution.py:29
  33.8 4.1 %fusion.3 = (bf16[3,2,8,128,128]{4,3,2,1,0:T(8,128)(2,1)}, bf16[3,2,8,128,128]{4,3,2,1,0:T(8,128)(2,1)}) fusion(bf16[3,4,8,128,128]{4,3,2,1,0:T(8,128)(2,1)} %shard_map.61), kind=kLoop, calls=%fused_computation.29 | loop fusion | bytes 6291456 | tf_op jit(solution)/shard_map/slice | solution.py:256
  37.9 1.3 collective-permute-start.3
  39.2 6.7 %collective-permute-start.2 = (bf16[3,2,8,128,128]{4,3,2,1,0:T(8,128)(2,1)}, bf16[3,2,8,128,128]{4,3,2,1,0:T(8,128)(2,1)}, u32[]{:S(2)}, u32[]{:S(2)}) collective-permute-start(bf16[3,2,8,128,128]{4,3,2,1,0:T(8,128)(2,1)} %get-tuple-element.15), channel_id=1, source_target_pairs={{0,8},{8,16},{16,24},{1,9},{9,17},{17,25},{2,10},{10,18},{18,26},{... | collective-permute-start | bytes 4718600 | tf_op jit(solution)/shard_map/ppermute | solution.py:249
  45.9 0.7 gather_fusion
  46.6 0.7 gather_fusion.1
  49.4 0.7 add_convert_fusion.taps_ref
  50.1 1.4 copy-done.1
  51.5 20.3 %shard_map.60 = (bf16[8,128,4096]{2,1,0:T(8,128)(2,1)}, f32[128,128]{1,0:T(8,128)}) custom-call(f32[12]{0:T(128)} %broadcast_multiply_fusion.2.mx_ref, f32[8]{0:T(128)} %broadcast_multiply_fusion.my_ref, f32[1,128]{1,0:T(1,128)} %multiply_bitcast_fusion.mz_ref, bf16[128,128]{1,0:T(8,128)(2,1)} %add_convert_fusion.taps_ref, ...), custom_call_target="tpu_custom_call" | custom-call | tf_op jit(solution)/shard_map/pallas_call | solution.py:155
  71.8 0.9 copy.9
  72.8 5.5 %collective-permute-done.3.rest_2_ = bf16[3,2,8,128,128]{4,3,2,1,0:T(8,128)(2,1)} collective-permute-done((bf16[3,2,8,128,128]{4,3,2,1,0:T(8,128)(2,1)}, bf16[3,2,8,128,128]{4,3,2,1,0:T(8,128)(2,1)}, u32[]{:S(2)}, u32[]{:S(2)}) %collective-permute-start.3) | collective-permute-done | bytes 1572896 | tf_op jit(solution)/shard_map/ppermute | solution.py:249
  78.9 15.4 %shard_map.62 = (bf16[4,128,4096]{2,1,0:T(8,128)(2,1)}, f32[128,128]{1,0:T(8,128)}) custom-call(f32[12]{0:T(128)} %broadcast_multiply_fusion.1.mx_ref, f32[8]{0:T(128)} %broadcast_multiply_fusion.my_ref, f32[1,128]{1,0:T(1,128)} %multiply_bitcast_fusion.mz_ref, bf16[128,128]{1,0:T(8,128)(2,1)} %add_convert_fusion.taps_ref, ...), custom_call_target="tpu_custom_call" | custom-call | tf_op jit(solution)/shard_map/pallas_call | solution.py:155
  94.3 0.9 copy.10
  95.3 1.2 collective-permute-done.4
  96.6 1.6 collective-permute-start.5
  98.2 2.7 %collective-permute-done.5 = f32[128,128]{0,1:T(8,128)S(1)} collective-permute-done((f32[128,128]{0,1:T(8,128)S(1)}, f32[128,128]{0,1:T(8,128)S(1)}, u32[]{:S(2)}, u32[]{:S(2)}) %collective-permute-start.5) | collective-permute-done | bytes 65568 | tf_op jit(solution)/shard_map/ppermute | solution.py:241
  100.9 2.6 %collective-permute-start.6 = (f32[128,128]{0,1:T(8,128)S(1)}, f32[128,128]{0,1:T(8,128)S(1)}, u32[]{:S(2)}, u32[]{:S(2)}) collective-permute-start(f32[128,128]{0,1:T(8,128)S(1)} %add.89), channel_id=1, source_target_pairs={{0,4},{1,5},{2,6},{3,7},{4,0},{5,1},{6,2},{7,3},{8,12},{9,13},{10,... | collective-permute-start | bytes 196616 | tf_op jit(solution)/shard_map/ppermute | solution.py:241
  103.6 2.6 %collective-permute-done.6 = f32[128,128]{0,1:T(8,128)S(1)} collective-permute-done((f32[128,128]{0,1:T(8,128)S(1)}, f32[128,128]{0,1:T(8,128)S(1)}, u32[]{:S(2)}, u32[]{:S(2)}) %collective-permute-start.6) | collective-permute-done | bytes 65568 | tf_op jit(solution)/shard_map/ppermute | solution.py:241
  106.2 32.1 %collective-permute-start.7 = (f32[128,128]{0,1:T(8,128)S(1)}, f32[128,128]{0,1:T(8,128)S(1)}, u32[]{:S(2)}, u32[]{:S(2)}) collective-permute-start(f32[128,128]{0,1:T(8,128)S(1)} %add.90), channel_id=1, source_target_pairs={{0,8},{8,0},{16,24},{24,16},{1,9},{9,1},{17,25},{25,17},{2,10},{10... | collective-permute-start | bytes 196616 | tf_op jit(solution)/shard_map/ppermute | solution.py:241
  138.3 2.2 %collective-permute-done.7 = f32[128,128]{0,1:T(8,128)S(1)} collective-permute-done((f32[128,128]{0,1:T(8,128)S(1)}, f32[128,128]{0,1:T(8,128)S(1)}, u32[]{:S(2)}, u32[]{:S(2)}) %collective-permute-start.7) | collective-permute-done | bytes 65568 | tf_op jit(solution)/shard_map/ppermute | solution.py:241
  140.6 4.7 %collective-permute-start.8 = (f32[128,128]{0,1:T(8,128)S(1)}, f32[128,128]{0,1:T(8,128)S(1)}, u32[]{:S(2)}, u32[]{:S(2)}) collective-permute-start(f32[128,128]{0,1:T(8,128)S(1)} %add.91), channel_id=1, source_target_pairs={{0,16},{8,24},{16,0},{24,8},{1,17},{9,25},{17,1},{25,9},{2,18},{10... | collective-permute-start | bytes 196616 | tf_op jit(solution)/shard_map/ppermute | solution.py:241
  145.3 2.2 %collective-permute-done.8 = f32[128,128]{0,1:T(8,128)S(1)} collective-permute-done((f32[128,128]{0,1:T(8,128)S(1)}, f32[128,128]{0,1:T(8,128)S(1)}, u32[]{:S(2)}, u32[]{:S(2)}) %collective-permute-start.8) | collective-permute-done | bytes 65568 | tf_op jit(solution)/shard_map/ppermute | solution.py:241
  147.7 11.7 %cholesky.16 = f32[128,128]{1,0:T(8,128)S(1)} custom-call(f32[128,128]{1,0:T(8,128)S(1)} %fusion.1), custom_call_target="Cholesky" | custom-call | tf_op jit(solution)/shard_map/jit(cholesky)/cholesky | solution.py:295
  159.4 0.6 compare_reduce_fusion
  160.0 1.3 select_bitcast_fusion
  161.3 9.8 %custom-call.7 = f32[1,128,128]{1,2,0:T(8,128)S(1)} custom-call(f32[1,128,128]{2,1,0:T(8,128)S(1)} %get-tuple-element.10), custom_call_target="InvertDiagBlocksLowerTriangular" | custom-call | tf_op jit(solution)/shard_map/jit(_solve_triangular)/triangular_solve | solution.py:296
  171.1 0.9 convolution_convert_fusion.inverse_ref
  172.0 15.6 %shard_map.63 = bf16[128,4,12,8,128]{4,3,2,1,0:T(8,128)(2,1)} custom-call(bf16[128,128]{1,0:T(8,128)(2,1)} %convolution_convert_fusion.inverse_ref, bf16[8,128,4096]{2,1,0:T(8,128)(2,1)} %get-tuple-element.8.rest_0_, bf16[4,128,4096]{2,1,0:T(8,128)(2,1)} %get-tuple-element.9.rest_1_), custom_call_target="tpu_custom_call" | custom-call | tf_op jit(solution)/shard_map/pallas_call | solution.py:218
  (32 shorter events, 3.1 us)
Async XLA Ops:
  0.6 45.2 %copy-start = (f32[12]{0:T(128)S(1)}, f32[12]{0:T(128)}, u32[]{:S(2)}) copy-start(f32[12]{0:T(128)} %param.5) | copy-start | bytes 148
  22.2 27.9 %collective-permute-start.1 = (bf16[3,12,2,128,128]{4,3,2,1,0:T(8,128)(2,1)}, bf16[3,12,2,128,128]{4,3,2,1,0:T(8,128)(2,1)S(1)}, u32[]{:S(2)}, u32[]{:S(2)}) collective-permute-start(bf16[3,12,2,128,128]{4,3,2,1,0:T(8,128)(2,1)} %get-tuple-element.12), channel_id=1, source_target_pairs={{1,0},{2,1},{3,2},{4,3},{5,4},{6,5},{7,6},{9,8},{10,9},{11,10},{12... | collective-permute-start | bytes 7077896 | tf_op jit(solution)/shard_map/ppermute | solution.py:249
  23.5 26.7 %collective-permute-start = (bf16[3,12,2,128,128]{4,3,2,1,0:T(8,128)(2,1)}, bf16[3,12,2,128,128]{4,3,2,1,0:T(8,128)(2,1)}, u32[]{:S(2)}, u32[]{:S(2)}) collective-permute-start(bf16[3,12,2,128,128]{4,3,2,1,0:T(8,128)(2,1)} %get-tuple-element.13), channel_id=1, source_target_pairs={{0,1},{1,2},{2,3},{3,4},{4,5},{5,6},{6,7},{8,9},{9,10},{10,11},{11... | collective-permute-start | bytes 7077896 | tf_op jit(solution)/shard_map/ppermute | solution.py:249
  33.8 12.0 %copy-start.2 = (s32[12]{0:T(128)S(1)}, s32[12]{0:T(128)}, u32[]{:S(2)}) copy-start(s32[12]{0:T(128)} %constant.145) | copy-start | bytes 148
  33.8 12.7 %copy-start.3 = (s32[12]{0:T(128)S(1)}, s32[12]{0:T(128)}, u32[]{:S(2)}) copy-start(s32[12]{0:T(128)} %constant.146) | copy-start | bytes 148
  33.8 13.4 %copy-start.4 = (f32[8]{0:T(128)S(1)}, f32[8]{0:T(128)}, u32[]{:S(2)}) copy-start(f32[8]{0:T(128)} %param.6) | copy-start | bytes 100
  33.8 13.9 %copy-start.5 = (f32[128]{0:T(128)S(1)}, f32[128]{0:T(128)}, u32[]{:S(2)}) copy-start(f32[128]{0:T(128)} %param.7) | copy-start | bytes 1540
  37.9 40.3 %collective-permute-start.3 = (bf16[3,2,8,128,128]{4,3,2,1,0:T(8,128)(2,1)}, bf16[3,2,8,128,128]{4,3,2,1,0:T(8,128)(2,1)}, u32[]{:S(2)}, u32[]{:S(2)}) collective-permute-start(bf16[3,2,8,128,128]{4,3,2,1,0:T(8,128)(2,1)} %get-tuple-element.14), channel_id=1, source_target_pairs={{8,0},{16,8},{24,16},{9,1},{17,9},{25,17},{10,2},{18,10},{26,18},{... | collective-permute-start | bytes 4718600 | tf_op jit(solution)/shard_map/ppermute | solution.py:249
  39.2 39.7 %collective-permute-start.2 = (bf16[3,2,8,128,128]{4,3,2,1,0:T(8,128)(2,1)}, bf16[3,2,8,128,128]{4,3,2,1,0:T(8,128)(2,1)}, u32[]{:S(2)}, u32[]{:S(2)}) collective-permute-start(bf16[3,2,8,128,128]{4,3,2,1,0:T(8,128)(2,1)} %get-tuple-element.15), channel_id=1, source_target_pairs={{0,8},{8,16},{16,24},{1,9},{9,17},{17,25},{2,10},{10,18},{18,26},{... | collective-permute-start | bytes 4718600 | tf_op jit(solution)/shard_map/ppermute | solution.py:249
  50.1 1.4 copy-start.1
  95.3 1.3 collective-permute-start.4
  96.6 4.3 %collective-permute-start.5 = (f32[128,128]{0,1:T(8,128)S(1)}, f32[128,128]{0,1:T(8,128)S(1)}, u32[]{:S(2)}, u32[]{:S(2)}) collective-permute-start(f32[128,128]{0,1:T(8,128)S(1)} %add.88), channel_id=1, source_target_pairs={{0,2},{1,3},{2,0},{3,1},{4,6},{5,7},{6,4},{7,5},{8,10},{9,11},{10,... | collective-permute-start | bytes 196616 | tf_op jit(solution)/shard_map/ppermute | solution.py:241
  100.9 5.2 %collective-permute-start.6 = (f32[128,128]{0,1:T(8,128)S(1)}, f32[128,128]{0,1:T(8,128)S(1)}, u32[]{:S(2)}, u32[]{:S(2)}) collective-permute-start(f32[128,128]{0,1:T(8,128)S(1)} %add.89), channel_id=1, source_target_pairs={{0,4},{1,5},{2,6},{3,7},{4,0},{5,1},{6,2},{7,3},{8,12},{9,13},{10,... | collective-permute-start | bytes 196616 | tf_op jit(solution)/shard_map/ppermute | solution.py:241
  106.2 34.4 %collective-permute-start.7 = (f32[128,128]{0,1:T(8,128)S(1)}, f32[128,128]{0,1:T(8,128)S(1)}, u32[]{:S(2)}, u32[]{:S(2)}) collective-permute-start(f32[128,128]{0,1:T(8,128)S(1)} %add.90), channel_id=1, source_target_pairs={{0,8},{8,0},{16,24},{24,16},{1,9},{9,1},{17,25},{25,17},{2,10},{10... | collective-permute-start | bytes 196616 | tf_op jit(solution)/shard_map/ppermute | solution.py:241
  140.6 6.9 %collective-permute-start.8 = (f32[128,128]{0,1:T(8,128)S(1)}, f32[128,128]{0,1:T(8,128)S(1)}, u32[]{:S(2)}, u32[]{:S(2)}) collective-permute-start(f32[128,128]{0,1:T(8,128)S(1)} %add.91), channel_id=1, source_target_pairs={{0,16},{8,24},{16,0},{24,8},{1,17},{9,25},{17,1},{25,9},{2,18},{10... | collective-permute-start | bytes 196616 | tf_op jit(solution)/shard_map/ppermute | solution.py:241

commit v2 on v0

v2 whole, which is shorter than its diff:
```python
import functools

import jax
import jax.numpy as jnp
from jax import lax
from jax.experimental import pallas as pl
from jax.experimental.pallas import tpu as pltpu
from jax.sharding import PartitionSpec as P

F32, BF16 = jnp.float32, jnp.bfloat16
VMEM_LIMIT = 56 * 1024 * 1024
PITCH = 9
ROWS = 16
HBM = pl.BlockSpec(memory_space=pl.ANY)
SMEM = pl.BlockSpec(memory_space=pltpu.SMEM)
VMEM = pl.BlockSpec(memory_space=pltpu.VMEM)
PARAMS = pltpu.CompilerParams(vmem_limit_bytes=VMEM_LIMIT)
SHORT = pl.CostEstimate(flops=1024, bytes_accessed=1024, transcendentals=0)
DMA = pltpu.SemaphoreType.DMA


def turn(tile, rows, ys, put):
    snaps, cells_y, cells_z = tile.shape
    wide = tile.astype(F32)
    for s in range(snaps):
        rows[pl.ds(s * PITCH, cells_y), :] = wide[s]
    for y in ys:
        put(y, rows[pl.ds(y, snaps, stride=PITCH), :].astype(BF16))


def edges_kernel(
    velocity, near, far1, far2, first, last, tiles, inner, ends, sides, rows, *sems
):
    end_in, inner_in, end_out, side_out = sems
    snaps, comps, cells_x, cells_y, _ = velocity.shape
    odd = lax.rem(lax.axis_index("stream"), 2)
    firsts = ((1 - odd) * (cells_x - 2), odd * (cells_x - 2))
    half = cells_y // 2
    between = cells_x - 4
    order = [(side, c) for side in (1, 0) for c in range(comps)]

    def end_read(side, c):
        return pltpu.make_async_copy(
            velocity.at[:, c, pl.ds(firsts[side], 2)], tiles.at[side, c], end_in.at[side, c]
        )

    def inner_read(c):
        return pltpu.make_async_copy(
            velocity.at[:, c, pl.ds(2, between)], inner.at[c], inner_in.at[c]
        )

    def side_writes(c, x):
        return [
            pltpu.make_async_copy(sides.at[k, c, x], ref.at[c, x], side_out.at[k, c, x])
            for k, ref in enumerate((first, last))
        ]

    def put_side(c, x, y, plane):
        if y < 2:
            sides[0, c, x, y] = plane
        elif y >= cells_y - 2:
            sides[1, c, x, y - cells_y + 2] = plane

    for side, c in order:
        end_read(side, c).start()
    for c in range(comps):
        inner_read(c).start()
    writes = []
    for side, c in order:
        end_read(side, c).wait()

        def one_end(layer, _):
            x = firsts[side] + layer

            def put(y, plane):
                ends[side, c, layer, y] = plane
                put_side(c, x, y, plane)

            turn(tiles[side, c, :, layer], rows, range(cells_y), put)
            for w in side_writes(c, x):
                w.start()
            return 0

        lax.fori_loop(0, 2, one_end, 0)
        if side == 0:
            parts = [(ends.at[0, c], near.at[c])]
        else:
            parts = [
                (ends.at[1, c, :, pl.ds(0, half)], far1.at[c]),
                (ends.at[1, c, :, pl.ds(half, half)], far2.at[c]),
            ]
        for src, dst in parts:
            writes.append(pltpu.make_async_copy(src, dst, end_out.at[len(writes)]))
            writes[-1].start()

    for c in range(comps):
        inner_read(c).wait()

        def one_inner(n, _):
            turn(
                inner[c, :, n],
                rows,
                (0, 1, cells_y - 2, cells_y - 1),
                functools.partial(put_side, c, n + 2),
            )
            for w in side_writes(c, n + 2):
                w.start()
            return 0

        lax.fori_loop(0, between, one_inner, 0)

    for w in writes:
        w.wait()

    def finish(n, _):
        for w in side_writes(n // cells_x, lax.rem(n, cells_x)):
            w.wait()
        return 0

    lax.fori_loop(0, comps * cells_x, finish, 0)


def edges(velocity):
    snaps, comps, cells_x, cells_y, cells_z = velocity.shape
    shape = lambda layers, rows: jax.ShapeDtypeStruct((comps, layers, rows, snaps, cells_z), BF16)
    return pl.pallas_call(
        edges_kernel,
        in_specs=[HBM],
        out_specs=[HBM] * 5,
        out_shape=[shape(2, cells_y)] + [shape(2, cells_y // 2)] * 2 + [shape(cells_x, 2)] * 2,
        scratch_shapes=[
            pltpu.VMEM((2, comps, snaps, 2, cells_y, cells_z), BF16),
            pltpu.VMEM((comps, snaps, cells_x - 4, cells_y, cells_z), BF16),
            pltpu.VMEM((2, comps, 2, cells_y, snaps, cells_z), BF16),
            pltpu.VMEM((2, comps, cells_x, 2, snaps, cells_z), BF16),
            pltpu.VMEM((snaps * PITCH, cells_z), F32),
            DMA((2, comps)),
            DMA((comps,)),
            DMA((3 * comps,)),
            DMA((2, comps, cells_x)),
        ],
        compiler_params=PARAMS,
    )(velocity)


def planes_kernel(velocity, cells, taken, turned, rows, in_sems, out_sems):
    snaps, comps, cells_x, cells_y, cells_z = velocity.shape

    def read(c, x):
        return pltpu.make_async_copy(velocity.at[:, c, x], taken.at[c, x], in_sems.at[c, x])

    def write(c, x):
        return pltpu.make_async_copy(turned.at[c, x], cells.at[c, x], out_sems.at[c, x])

    def each(work):
        def step(n, _):
            work(n // cells_x, lax.rem(n, cells_x))
            return 0

        lax.fori_loop(0, comps * cells_x, step, 0)

    def one(c, x):
        read(c, x).wait()

        def put(y, plane):
            turned[c, x, y] = plane

        turn(taken[c, x], rows, range(cells_y), put)
        write(c, x).start()

    each(lambda c, x: read(c, x).start())
    each(one)
    each(lambda c, x: write(c, x).wait())


def planes(velocity):
    snaps, comps, cells_x, cells_y, cells_z = velocity.shape
    return pl.pallas_call(
        planes_kernel,
        in_specs=[HBM],
        out_specs=HBM,
        out_shape=jax.ShapeDtypeStruct((comps, cells_x, cells_y, snaps, cells_z), BF16),
        scratch_shapes=[
            pltpu.VMEM((comps, cells_x, snaps, cells_y, cells_z), BF16),
            pltpu.VMEM((comps, cells_x, cells_y, snaps, cells_z), BF16),
            pltpu.VMEM((snaps * PITCH, cells_z), F32),
            DMA((comps, cells_x)),
            DMA((comps, cells_x)),
        ],
        compiler_params=PARAMS,
    )(velocity)


def layer_fields(ys, ring, slots, rz, low, high, metric_x, metric_y_ref, metric_z, out_ref):
    cells_y, snaps, cells_z = ring.shape[2:]
    back2, back1, here, fore1, fore2 = slots

    def some_rows(step, _):
        at = pl.ds(pl.multiple_of(step * ROWS, ROWS), ROWS)
        held = {}

        def row(comp, y):
            if (comp, y) not in held:
                if y < 0:
                    held[comp, y] = low[comp, y + 2, at, :].astype(F32)
                elif y >= cells_y:
                    held[comp, y] = high[comp, y - cells_y, at, :].astype(F32)
                else:
                    held[comp, y] = ring[here, comp, y, at, :]
            return held[comp, y]

        for n, y in enumerate(ys):

            def along_x(c):
                near = ring[fore1, c, y, at, :] - ring[back1, c, y, at, :]
                far = ring[fore2, c, y, at, :] - ring[back2, c, y, at, :]
                return (8.0 * near - far) * metric_x

            def along_y(c):
                near = row(c, y + 1) - row(c, y - 1)
                far = row(c, y + 2) - row(c, y - 2)
                return (8.0 * near - far) * metric_y_ref[y]

            def along_z(c):
                return rz[c, y, at, :] * metric_z

            outs = (
                along_y(2) - along_z(1),
                along_z(0) - along_x(2),
                along_x(1) - along_y(0),
                along_x(0) + along_y(1) + along_z(2),
            )
            for f, value in enumerate(outs):
                lane = (f * len(ys) + n) * cells_z
                out_ref[at, lane : lane + cells_z] = value.astype(BF16)
        return 0

    lax.fori_loop(0, snaps // ROWS, some_rows, 0)


def runs(ys):
    found = []
    for y in ys:
        if found and found[-1][1] == y:
            found[-1][1] = y + 1
        else:
            found.append([y, y + 1])
    return found


def fields_kernel(reads, centers, ys, mx_ref, my_ref, mz_ref, taps_ref, *rest):
    n = len(rest) - 12
    sources, (low, high, out, gram_ref) = rest[:n], rest[n : n + 4]
    layers, lows, highs, ring, rz_ring, done, in_sems, out_sems = rest[n + 4 :]
    comps, cells_y, snaps, cells_z = ring.shape[1:]
    steps = len(centers)
    kept = [i for i in range(steps) if centers[i] is not None]
    lowest, highest = min(ys) < 2, max(ys) >= cells_y - 2

    def whichever(i, start):
        for m, (src, rows, cond) in enumerate(reads[i](sources)):
            copy = pltpu.make_async_copy(src, layers.at[i, :, rows], in_sems.at[0, i, m])
            if cond is None:
                getattr(copy, "start" if start else "wait")()
            else:
                pl.when(cond)(copy.start if start else copy.wait)

    def sides(k):
        x = centers[kept[k]]
        copies = []
        if lowest:
            copies.append(pltpu.make_async_copy(low.at[:, x], lows.at[k], in_sems.at[1, k, 0]))
        if highest:
            copies.append(pltpu.make_async_copy(high.at[:, x], highs.at[k], in_sems.at[2, k, 0]))
        return copies

    for i in range(steps):
        whichever(i, True)
        if centers[i] is not None:
            for copy in sides(kept.index(i)):
                copy.start()

    gram_ref[...] = jnp.zeros_like(gram_ref)
    writes = []
    for i in range(steps):
        whichever(i, False)
        ring[i % 5] = layers[i].astype(F32)
        if i + 2 < steps and centers[i + 2] is not None:
            for a, b in runs(ys):
                flat = layers[i, :, a:b].reshape(comps * (b - a) * snaps, cells_z)
                rz_ring[i % 3, :, a:b] = jnp.dot(
                    flat, taps_ref[...], preferred_element_type=F32
                ).reshape(comps, b - a, snaps, cells_z)
        if centers[i] is None:
            continue
        k = kept.index(i)
        for copy in sides(k):
            copy.wait()
        layer_fields(
            ys,
            ring,
            [(i + 1 + s) % 5 for s in range(5)],
            rz_ring.at[(i - 2) % 3],
            lows.at[k],
            highs.at[k],
            mx_ref[centers[i]],
            my_ref,
            mz_ref[...],
            done.at[k],
        )
        writes.append(pltpu.make_async_copy(done.at[k], out.at[k], out_sems.at[k]))
        writes[-1].start()
        gram_ref[...] += lax.dot_general(
            done[k], done[k], (((1,), (1,)), ((), ())), preferred_element_type=F32
        )
    for w in writes:
        w.wait()


def fields(sources, reads, centers, ys, low, high, metrics):
    comps, _, cells_y, snaps, cells_z = sources[0].shape
    steps = len(centers)
    kept = sum(c is not None for c in centers)
    lanes = 4 * len(ys) * cells_z
    return pl.pallas_call(
        functools.partial(fields_kernel, reads, centers, ys),
        in_specs=[SMEM, SMEM, VMEM, VMEM] + [HBM] * (len(sources) + 2),
        out_specs=[HBM, VMEM],
        out_shape=[
            jax.ShapeDtypeStruct((kept, snaps, lanes), BF16),
            jax.ShapeDtypeStruct((snaps, snaps), F32),
        ],
        scratch_shapes=[
            pltpu.VMEM((steps, comps, cells_y, snaps, cells_z), BF16),
            pltpu.VMEM((kept, comps, 2, snaps, cells_z), BF16),
            pltpu.VMEM((kept, comps, 2, snaps, cells_z), BF16),
            pltpu.VMEM((5, comps, cells_y, snaps, cells_z), F32),
            pltpu.VMEM((3, comps, cells_y, snaps, cells_z), F32),
            pltpu.VMEM((kept, snaps, lanes), BF16),
            DMA((3, steps, 3)),
            DMA((kept,)),
        ],
        compiler_params=PARAMS,
    )(*metrics, *sources, low, high)


def modes_kernel(places, inverse_ref, *rest):
    n = len(rest) - 6
    sources, (out, held, made, rows, in_sems, out_sems) = rest[:n], rest[n:]
    snaps, comps, _, cells_y, cells_z = out.shape

    def reads(x):
        copies, lane = [], 0
        for m, (source, layer, ys) in enumerate(places[x]):
            lanes = pl.ds(lane, comps * len(ys) * cells_z)
            lane += comps * len(ys) * cells_z
            copies.append(
                pltpu.make_async_copy(
                    sources[source].at[layer], held.at[x, :, lanes], in_sems.at[x, m]
                )
            )
        return copies

    for x in range(len(places)):
        for copy in reads(x):
            copy.start()
    writes = []
    for x in range(len(places)):
        for copy in reads(x):
            copy.wait()
        for f in range(comps):
            lane = 0
            for _, _, ys in places[x]:
                width = len(ys) * cells_z
                at = lane + f * width
                lane += comps * width
                whole = jnp.dot(
                    inverse_ref[...], held[x, :, at : at + width], preferred_element_type=F32
                )
                for k, y in enumerate(ys):
                    rows[f % 2, pl.ds(y, snaps, stride=PITCH), :] = whole[
                        :, k * cells_z : (k + 1) * cells_z
                    ]
            for s in range(snaps):
                made[x, s, f] = rows[f % 2, pl.ds(s * PITCH, cells_y), :].astype(BF16)
        writes.append(pltpu.make_async_copy(made.at[x], out.at[:, :, x], out_sems.at[x]))
        writes[-1].start()
    for w in writes:
        w.wait()


def modes(inverse, sources, places, cells_y, cells_z):
    snaps = inverse.shape[0]
    cells_x = len(places)
    return pl.pallas_call(
        functools.partial(modes_kernel, places),
        in_specs=[VMEM] + [HBM] * len(sources),
        out_specs=HBM,
        out_shape=jax.ShapeDtypeStruct((snaps, 4, cells_x, cells_y, cells_z), BF16),
        scratch_shapes=[
            pltpu.VMEM((cells_x, snaps, 4 * cells_y * cells_z), BF16),
            pltpu.VMEM((cells_x, snaps, 4, cells_y, cells_z), BF16),
            pltpu.VMEM((2, snaps * PITCH, cells_z), F32),
            DMA((cells_x, 2)),
            DMA((cells_x,)),
        ],
        compiler_params=PARAMS,
    )(inverse, *sources)


def total(local):
    for axis in ("cross", "stream"):
        count = lax.axis_size(axis)
        if count & (count - 1):
            local = lax.psum(local, axis)
            continue
        step = 1
        while step < count:
            local = local + lax.ppermute(local, axis, [(i, i ^ step) for i in range(count)])
            step *= 2
    return local


def shift(cells, axis, way):
    count = lax.axis_size(axis)
    pairs = [(i, i + way) for i in range(count) if 0 <= i + way < count]
    return lax.ppermute(cells, axis, pairs)


def both_ways(pairs):
    return [p for a, b in pairs for p in ((a, b), (b, a))]


def far_exchange(far2):
    count = lax.axis_size("stream")
    direct = both_ways([(i, i + 1) for i in range(1, count - 1, 2)])
    if count == 4:
        half_way = lax.ppermute(far2, "stream", [(1, 3), (2, 0)])
        return half_way, lambda cells: lax.ppermute(cells, "stream", [(3, 2), (0, 1)]), direct
    return far2, lambda cells: lax.ppermute(cells, "stream", direct), direct


def shards(velocity, metric_x, metric_y, metric_z):
    snaps, comps, cells_x, cells_y, cells_z = velocity.shape
    count = lax.axis_size("stream")
    near, far1, far2, first, last = edges(velocity)
    after_edges, _ = lax.optimization_barrier((velocity, near))
    half_way, second_hop, direct = far_exchange(far2)
    near = lax.ppermute(near, "stream", both_ways([(i, i + 1) for i in range(0, count - 1, 2)]))
    far1 = lax.ppermute(far1, "stream", direct)
    low = shift(last, "cross", 1)
    high = shift(first, "cross", -1)
    cells = planes(after_edges)
    half_way, cells = lax.optimization_barrier((half_way, cells))
    far2 = second_hop(half_way)

    taps = jnp.zeros((cells_z, cells_z), F32)
    for step, weight in ((1, 8.0), (-1, -8.0), (2, -1.0), (-2, 1.0)):
        taps = taps + weight * jnp.eye(cells_z, k=-step, dtype=F32)
    metrics = (metric_x / 12.0, metric_y / 12.0, metric_z[None, :] / 12.0, taps.astype(BF16))
    whole, half = slice(0, cells_y), cells_y // 2

    def local(layer):
        return lambda refs: [(refs[0].at[:, layer], whole, None)]

    def halo(layer, of_near):
        def read(refs):
            odd = lax.rem(lax.axis_index("stream"), 2)
            is_near = (odd == 1) == of_near
            is_far = jnp.logical_not(is_near)
            return [
                (refs[1].at[:, layer], whole, is_near),
                (refs[2].at[:, layer], slice(0, half), is_far),
                (refs[3].at[:, layer], slice(half, cells_y), is_far),
            ]

        return read

    rows = tuple(range(cells_y))
    rows_in, rows_out = rows[2:-2], rows[:2] + rows[-2:]
    walk = ([local(i) for i in range(cells_x)], [None] * 4 + list(range(2, cells_x - 2)))
    middle, middle_gram = fields([cells], *walk, rows_in, first, last, metrics)
    sides, sides_gram = fields([cells], *walk, rows_out, low, high, metrics)
    outer, outer_gram = fields(
        [cells, near, far1, far2],
        [halo(0, True), halo(1, True)]
        + [local(i) for i in (*range(4), *range(cells_x - 4, cells_x))]
        + [halo(0, False), halo(1, False)],
        [None] * 4 + [0, 1] + [None] * 4 + [cells_x - 2, cells_x - 1],
        rows,
        low,
        high,
        metrics,
    )
    everywhere = (
        4.0 * cells_x * lax.axis_size("stream") * cells_y * lax.axis_size("cross") * cells_z
    )
    gram = total(middle_gram + sides_gram + outer_gram)
    lower = jnp.linalg.cholesky(gram * (1.0 / everywhere))
    inverse = jax.scipy.linalg.solve_triangular(lower, jnp.eye(snaps, dtype=F32), lower=True)
    places = [
        [(2, x if x < 2 else x - cells_x + 4, rows)]
        if x < 2 or x >= cells_x - 2
        else [(0, x - 2, rows_in), (1, x - 2, rows_out)]
        for x in range(cells_x)
    ]
    basis = modes(inverse.astype(BF16), [middle, sides, outer], places, cells_y, cells_z)
    return basis, lower


def solution(mesh):
    return jax.shard_map(
        shards,
        mesh=mesh,
        in_specs=(P(None, None, "stream", "cross", None), P("stream"), P("cross"), P()),
        out_specs=(P(None, None, "stream", "cross", None), P()),
        check_vma=False,
    )
```

time: 428 us -> 145 us (0.34); the launches traced: 423 us -> 145 us
  waiting for transfers between devices: 164 us -> 22.9 us
  local copies, waits for them, and re-layouts: 112 us -> 5.08 us
  other arithmetic: 95.3 us -> 25.9 us
  Pallas kernels: 0 us -> 68.5 us
  matrix products: 24.9 us -> 0.86 us
  between operations: 14.2 us -> 1.05 us
  starting transfers between devices: 11.5 us -> 20.4 us
    psum x1 -> x0, waiting for transfers between devices: 118 us -> none  [global_factor(): gram = lax.psum(local, ('stream', 'cross'))]
    pallas_call x0 -> x6, Pallas kernels: none -> 68.5 us  [the longest x3 42 us: fields(): pl.pallas_call(functools.partial(fields_kernel, reads, centers, ys), in_s...]
    squeeze x32 -> x0, local copies, waits for them, and re-layouts: 37.1 us -> none  [shards(): stacked = lax.map(one_face_group, (stream_groups, cross_groups, plain))]
    dot_general x2 -> x0, matrix products: 24.7 us -> none  [the longest x1 12.5 us: shards(): jnp.dot(inverse.astype(jnp.bfloat16), flat, preferred_element_type=jnp.fl...]
    dynamic_slice x32 -> x0, local copies, waits for them, and re-layouts: 24 us -> none  [shards(): stacked = lax.map(one_face_group, (stream_groups, cross_groups, plain))]
    ppermute x4 -> x11, waiting for transfers between devices: 45.5 us -> 22.9 us  [the longest x5 16.6 us: total(): lax.ppermute(local, axis, [(i, i ^ step) for i in range(count)])]
    another operation x53 -> x5, other arithmetic: 45.2 us -> 23.5 us  [the longest x3 12.4 us: shards(): lower = jnp.linalg.cholesky(gram * (1.0 / everywhere))]
    unnamed x14 -> x10, local copies, waits for them, and re-layouts: 22.6 us -> 2.2 us
  transfers between devices with their start and end apart: 5 -> 11, of which waited for: 3 -> 6; matrix products, arithmetic and copies ran while one was open for 7% -> 3% of each run, Pallas kernels for 0% -> 25%
where the time goes in v2:
time: 145 us
  Pallas kernels  68.5 us (47%)
  other arithmetic  25.9 us (18%)
  waiting for transfers between devices  22.9 us (16%)
  starting transfers between devices  20.4 us (14%)
  local copies, waits for them, and re-layouts  5.08 us (4%)
    pallas_call x3, Pallas kernels, fields(): pl.pallas_call(functools.partial(fields_kernel, reads, centers, ys), in_s...  42 us
    ppermute x5, waiting for transfers between devices, total(): lax.ppermute(local, axis, [(i, i ^ step) for i in range(count)])  16.6 us
    another operation x3, other arithmetic, shards(): lower = jnp.linalg.cholesky(gram * (1.0 / everywhere))  12.4 us
    another operation x2, other arithmetic, shards(): jax.scipy.linalg.solve_triangular(lower, jnp.eye(snaps, dtype=F32), lower...  11.1 us
    pallas_call x1, Pallas kernels, modes(): pl.pallas_call(functools.partial(modes_kernel, places), in_specs=[VMEM] +...  10.3 us
    pallas_call x1, Pallas kernels, edges(): pl.pallas_call(edges_kernel, in_specs=[HBM], out_specs=[HBM] * 5, out_sha...  8.11 us
    pallas_call x1, Pallas kernels, planes(): pl.pallas_call(planes_kernel, in_specs=[HBM], out_specs=HBM, out_shape=ja...  8.1 us
    ppermute x1, waiting for transfers between devices, far_exchange(): half_way = lax.ppermute(far2, 'stream', [(1, 3), (2, 0)])  6.29 us
  transfers between devices with their start and end apart: 11, of which 6 were waited for; matrix products, arithmetic and copies ran while one was open for 3% of the time, Pallas kernels for 25%

profile of v2, /device:TPU:0, one launch (start us, length us, event | category | flops | bytes accessed | tf_op | source)
XLA Modules:
  0.0 144.8 jit_solution(7498521453407311362)
XLA Ops:
  0.6 8.1 %shard_map.59 = (bf16[3,2,8,128,128]{4,3,2,1,0:T(8,128)(2,1)}, bf16[3,2,4,128,128]{4,3,2,1,0:T(8,128)(2,1)}, bf16[3,2,4,128,128]{4,3,2,1,0:T(8,128)(2,1)}, bf16[...) custom-call(bf16[128,3,12,8,128]{4,3,2,1,0:T(8,128)(2,1)} %velocity.2), custom_call_target="tpu_custom_call" | custom-call | tf_op jit(solution)/shard_map/pallas_call | solution.py:126
  8.7 1.3 collective-permute-start.2
  10.0 4.4 %collective-permute-start.1 = (bf16[3,12,2,128,128]{4,3,2,1,0:T(8,128)(2,1)}, bf16[3,12,2,128,128]{4,3,2,1,0:T(8,128)(2,1)}, u32[]{:S(2)}, u32[]{:S(2)}) collective-permute-start(bf16[3,12,2,128,128]{4,3,2,1,0:T(8,128)(2,1)} %get-tuple-element.21.rest_2_), channel_id=1, source_target_pairs={{0,1},{1,2},{2,3},{3,4},{4,5},{5,6},{6,7},{8,9},{9,10},{10,11},{11... | collective-permute-start | bytes 7077896 | tf_op jit(solution)/shard_map/ppermute | solution.py:427
  14.5 1.3 collective-permute-start
  15.8 5.8 %collective-permute-start.3 = (bf16[3,2,8,128,128]{4,3,2,1,0:T(8,128)(2,1)}, bf16[3,2,8,128,128]{4,3,2,1,0:T(8,128)(2,1)}, u32[]{:S(2)}, u32[]{:S(2)}) collective-permute-start(bf16[3,2,8,128,128]{4,3,2,1,0:T(8,128)(2,1)} %get-tuple-element.17), channel_id=1, source_target_pairs={{0,8},{8,0},{16,24},{24,16},{1,9},{9,1},{17,25},{25,17},{2,10},{10... | collective-permute-start | bytes 4718600 | tf_op jit(solution)/shard_map/ppermute | solution.py:449
  21.6 0.8 collective-permute-start.4
  22.4 8.1 %shard_map.60.rest_0_ = bf16[3,12,8,128,128]{4,3,2,1,0:T(8,128)(2,1)} custom-call(bf16[128,3,12,8,128]{4,3,2,1,0:T(8,128)(2,1)} %velocity.2), custom_call_target="tpu_custom_call" | custom-call | tf_op jit(solution)/shard_map/pallas_call | solution.py:178
  31.1 6.3 %collective-permute-done = bf16[3,2,4,128,128]{4,3,2,1,0:T(8,128)(2,1)} collective-permute-done((bf16[3,2,4,128,128]{4,3,2,1,0:T(8,128)(2,1)}, bf16[3,2,4,128,128]{4,3,2,1,0:T(8,128)(2,1)}, u32[]{:S(2)}, u32[]{:S(2)}) %collective-permute-start) | collective-permute-done | bytes 786464 | tf_op jit(solution)/shard_map/ppermute | solution.py:438
  37.4 3.2 %collective-permute-start.5 = (bf16[3,2,4,128,128]{4,3,2,1,0:T(8,128)(2,1)}, bf16[3,2,4,128,128]{4,3,2,1,0:T(8,128)(2,1)}, u32[]{:S(2)}, u32[]{:S(2)}) collective-permute-start(bf16[3,2,4,128,128]{4,3,2,1,0:T(8,128)(2,1)} %collective-permute-done), channel_id=1, source_target_pairs={{24,16},{0,8},{25,17},{1,9},{26,18},{2,10},{27,19},{3,11},{28,20},... | collective-permute-start | bytes 2359304 | tf_op jit(solution)/shard_map/ppermute | solution.py:439
  41.1 0.6 multiply_bitcast_fusion.mz_ref
  41.7 0.7 add_convert_fusion.taps_ref
  42.4 14.3 %shard_map.61 = (bf16[8,128,2048]{2,1,0:T(8,128)(2,1)}, f32[128,128]{1,0:T(8,128)}) custom-call(f32[12]{0:T(128)} %broadcast_multiply_fusion.1.mx_ref, f32[8]{0:T(128)} %broadcast_multiply_fusion.my_ref, f32[1,128]{1,0:T(1,128)} %multiply_bitcast_fusion.mz_ref, bf16[128,128]{1,0:T(8,128)(2,1)} %add_convert_fusion.taps_ref, ...), custom_call_target="tpu_custom_call" | custom-call | tf_op jit(solution)/shard_map/pallas_call | solution.py:325
  56.7 0.9 copy.6
  57.7 1.3 copy-done
  59.1 14.4 %shard_map.62 = (bf16[8,128,2048]{2,1,0:T(8,128)(2,1)}, f32[128,128]{1,0:T(8,128)}) custom-call(f32[12]{0:T(128)} %broadcast_multiply_fusion.1.mx_ref, f32[8]{0:T(128)} %broadcast_multiply_fusion.my_ref, f32[1,128]{1,0:T(1,128)} %multiply_bitcast_fusion.mz_ref, bf16[128,128]{1,0:T(8,128)(2,1)} %add_convert_fusion.taps_ref, ...), custom_call_target="tpu_custom_call" | custom-call | tf_op jit(solution)/shard_map/pallas_call | solution.py:325
  73.5 0.9 copy.7
  74.5 0.8 copy-done.1
  75.3 13.2 %shard_map.63 = (bf16[4,128,4096]{2,1,0:T(8,128)(2,1)}, f32[128,128]{1,0:T(8,128)}) custom-call(f32[12]{0:T(128)} %broadcast_multiply_fusion.1.mx_ref, f32[8]{0:T(128)} %broadcast_multiply_fusion.my_ref, f32[1,128]{1,0:T(1,128)} %multiply_bitcast_fusion.mz_ref, bf16[128,128]{1,0:T(8,128)(2,1)} %add_convert_fusion.taps_ref, ...), custom_call_target="tpu_custom_call" | custom-call | tf_op jit(solution)/shard_map/pallas_call | solution.py:325
  88.6 0.9 copy.8
  89.6 1.2 collective-permute-done.6
  90.9 1.2 collective-permute-start.7
  92.1 3.1 %collective-permute-done.7 = f32[128,128]{0,1:T(8,128)S(1)} collective-permute-done((f32[128,128]{0,1:T(8,128)S(1)}, f32[128,128]{0,1:T(8,128)S(1)}, u32[]{:S(2)}, u32[]{:S(2)}) %collective-permute-start.7) | collective-permute-done | bytes 65568 | tf_op jit(solution)/shard_map/ppermute | solution.py:419
  95.2 2.2 %collective-permute-start.8 = (f32[128,128]{0,1:T(8,128)S(1)}, f32[128,128]{0,1:T(8,128)S(1)}, u32[]{:S(2)}, u32[]{:S(2)}) collective-permute-start(f32[128,128]{0,1:T(8,128)S(1)} %add.112), channel_id=1, source_target_pairs={{0,4},{1,5},{2,6},{3,7},{4,0},{5,1},{6,2},{7,3},{8,12},{9,13},{10,... | collective-permute-start | bytes 196616 | tf_op jit(solution)/shard_map/ppermute | solution.py:419
  97.4 3.7 %collective-permute-done.8 = f32[128,128]{0,1:T(8,128)S(1)} collective-permute-done((f32[128,128]{0,1:T(8,128)S(1)}, f32[128,128]{0,1:T(8,128)S(1)}, u32[]{:S(2)}, u32[]{:S(2)}) %collective-permute-start.8) | collective-permute-done | bytes 65568 | tf_op jit(solution)/shard_map/ppermute | solution.py:419
  101.2 4.3 %collective-permute-done.9 = f32[128,128]{0,1:T(8,128)S(1)} collective-permute-done((f32[128,128]{0,1:T(8,128)S(1)}, f32[128,128]{0,1:T(8,128)S(1)}, u32[]{:S(2)}, u32[]{:S(2)}) %collective-permute-start.9) | collective-permute-done | bytes 65568 | tf_op jit(solution)/shard_map/ppermute | solution.py:419
  105.6 4.3 %collective-permute-done.10 = f32[128,128]{0,1:T(8,128)S(1)} collective-permute-done((f32[128,128]{0,1:T(8,128)S(1)}, f32[128,128]{0,1:T(8,128)S(1)}, u32[]{:S(2)}, u32[]{:S(2)}) %collective-permute-start.10) | collective-permute-done | bytes 65568 | tf_op jit(solution)/shard_map/ppermute | solution.py:419
  110.0 11.7 %cholesky.16 = f32[128,128]{1,0:T(8,128)S(1)} custom-call(f32[128,128]{1,0:T(8,128)S(1)} %fusion.1), custom_call_target="Cholesky" | custom-call | tf_op jit(solution)/shard_map/jit(cholesky)/cholesky | solution.py:499
  121.7 0.6 compare_reduce_fusion
  122.4 1.3 select_bitcast_fusion
  123.6 9.8 %custom-call.7 = f32[1,128,128]{1,2,0:T(8,128)S(1)} custom-call(f32[1,128,128]{2,1,0:T(8,128)S(1)} %get-tuple-element.30), custom_call_target="InvertDiagBlocksLowerTriangular" | custom-call | tf_op jit(solution)/shard_map/jit(_solve_triangular)/triangular_solve | solution.py:500
  133.5 0.9 convolution_convert_fusion.inverse_ref
  134.3 10.3 %shard_map.64 = bf16[128,4,12,8,128]{4,3,2,1,0:T(8,128)(2,1)} custom-call(bf16[128,128]{1,0:T(8,128)(2,1)} %convolution_convert_fusion.inverse_ref, bf16[8,128,2048]{2,1,0:T(8,128)(2,1)} %get-tuple-element.27.rest_0_, bf16[8,128,2048]{2,1,0:T(8,128)(2,1)} %get-tuple-element.28.rest_1_, bf16[4,128,4096]{2,1,0:T(8,128)(2,1)} %get-tuple-element.29.rest_2_), custom_call_target="tpu_custom_call" | custom-call | tf_op jit(solution)/shard_map/pallas_call | solution.py:395
  (29 shorter events, 1.5 us)
Async XLA Ops:
  8.7 48.9 %collective-permute-start.2 = (bf16[3,12,2,128,128]{4,3,2,1,0:T(8,128)(2,1)}, bf16[3,12,2,128,128]{4,3,2,1,0:T(8,128)(2,1)S(1)}, u32[]{:S(2)}, u32[]{:S(2)}) collective-permute-start(bf16[3,12,2,128,128]{4,3,2,1,0:T(8,128)(2,1)} %get-tuple-element.20.rest_1_), channel_id=1, source_target_pairs={{1,0},{2,1},{3,2},{4,3},{5,4},{6,5},{7,6},{9,8},{10,9},{11,10},{12... | collective-permute-start | bytes 7077896 | tf_op jit(solution)/shard_map/ppermute | solution.py:427
  10.0 47.7 %collective-permute-start.1 = (bf16[3,12,2,128,128]{4,3,2,1,0:T(8,128)(2,1)}, bf16[3,12,2,128,128]{4,3,2,1,0:T(8,128)(2,1)}, u32[]{:S(2)}, u32[]{:S(2)}) collective-permute-start(bf16[3,12,2,128,128]{4,3,2,1,0:T(8,128)(2,1)} %get-tuple-element.21.rest_2_), channel_id=1, source_target_pairs={{0,1},{1,2},{2,3},{3,4},{4,5},{5,6},{6,7},{8,9},{9,10},{10,11},{11... | collective-permute-start | bytes 7077896 | tf_op jit(solution)/shard_map/ppermute | solution.py:427
  14.5 22.9 %collective-permute-start = (bf16[3,2,4,128,128]{4,3,2,1,0:T(8,128)(2,1)}, bf16[3,2,4,128,128]{4,3,2,1,0:T(8,128)(2,1)}, u32[]{:S(2)}, u32[]{:S(2)}) collective-permute-start(bf16[3,2,4,128,128]{4,3,2,1,0:T(8,128)(2,1)} %get-tuple-element.16), channel_id=1, source_target_pairs={{8,24},{16,0},{9,25},{17,1},{10,26},{18,2},{11,27},{19,3},{12,28},... | collective-permute-start | bytes 2359304 | tf_op jit(solution)/shard_map/ppermute | solution.py:438
  15.8 58.7 %collective-permute-start.3 = (bf16[3,2,8,128,128]{4,3,2,1,0:T(8,128)(2,1)}, bf16[3,2,8,128,128]{4,3,2,1,0:T(8,128)(2,1)}, u32[]{:S(2)}, u32[]{:S(2)}) collective-permute-start(bf16[3,2,8,128,128]{4,3,2,1,0:T(8,128)(2,1)} %get-tuple-element.17), channel_id=1, source_target_pairs={{0,8},{8,0},{16,24},{24,16},{1,9},{9,1},{17,25},{25,17},{2,10},{10... | collective-permute-start | bytes 4718600 | tf_op jit(solution)/shard_map/ppermute | solution.py:449
  21.6 9.0 %copy-start.2 = (f32[12]{0:T(128)S(1)}, f32[12]{0:T(128)}, u32[]{:S(2)}) copy-start(f32[12]{0:T(128)} %param.5) | copy-start | bytes 148
  21.6 19.0 %copy-start.3 = (f32[8]{0:T(128)S(1)}, f32[8]{0:T(128)}, u32[]{:S(2)}) copy-start(f32[8]{0:T(128)} %param.6) | copy-start | bytes 100
  21.6 19.5 %copy-start.4 = (f32[128]{0:T(128)S(1)}, f32[128]{0:T(128)}, u32[]{:S(2)}) copy-start(f32[128]{0:T(128)} %param.7) | copy-start | bytes 1540
  21.6 52.9 %collective-permute-start.4 = (bf16[3,2,4,128,128]{4,3,2,1,0:T(8,128)(2,1)}, bf16[3,2,4,128,128]{4,3,2,1,0:T(8,128)(2,1)S(1)}, u32[]{:S(2)}, u32[]{:S(2)}) collective-permute-start(bf16[3,2,4,128,128]{4,3,2,1,0:T(8,128)(2,1)} %get-tuple-element.24), channel_id=1, source_target_pairs={{8,16},{16,8},{9,17},{17,9},{10,18},{18,10},{11,19},{19,11},{12,20... | collective-permute-start | bytes 2359304 | tf_op jit(solution)/shard_map/ppermute | solution.py:450
  37.4 37.1 %collective-permute-start.5 = (bf16[3,2,4,128,128]{4,3,2,1,0:T(8,128)(2,1)}, bf16[3,2,4,128,128]{4,3,2,1,0:T(8,128)(2,1)}, u32[]{:S(2)}, u32[]{:S(2)}) collective-permute-start(bf16[3,2,4,128,128]{4,3,2,1,0:T(8,128)(2,1)} %collective-permute-done), channel_id=1, source_target_pairs={{24,16},{0,8},{25,17},{1,9},{26,18},{2,10},{27,19},{3,11},{28,20},... | collective-permute-start | bytes 2359304 | tf_op jit(solution)/shard_map/ppermute | solution.py:439
  57.7 1.4 copy-start
  74.5 0.9 copy-start.1
  89.5 1.3 collective-permute-start.6
  90.9 4.3 %collective-permute-start.7 = (f32[128,128]{0,1:T(8,128)S(1)}, f32[128,128]{0,1:T(8,128)S(1)}, u32[]{:S(2)}, u32[]{:S(2)}) collective-permute-start(f32[128,128]{0,1:T(8,128)S(1)} %add.111), channel_id=1, source_target_pairs={{0,2},{1,3},{2,0},{3,1},{4,6},{5,7},{6,4},{7,5},{8,10},{9,11},{10,... | collective-permute-start | bytes 196616 | tf_op jit(solution)/shard_map/ppermute | solution.py:419
  95.2 5.9 %collective-permute-start.8 = (f32[128,128]{0,1:T(8,128)S(1)}, f32[128,128]{0,1:T(8,128)S(1)}, u32[]{:S(2)}, u32[]{:S(2)}) collective-permute-start(f32[128,128]{0,1:T(8,128)S(1)} %add.112), channel_id=1, source_target_pairs={{0,4},{1,5},{2,6},{3,7},{4,0},{5,1},{6,2},{7,3},{8,12},{9,13},{10,... | collective-permute-start | bytes 196616 | tf_op jit(solution)/shard_map/ppermute | solution.py:419
  101.2 4.3 %collective-permute-start.9 = (f32[128,128]{0,1:T(8,128)S(1)}, f32[128,128]{0,1:T(8,128)S(1)}, u32[]{:S(2)}, u32[]{:S(2)}) collective-permute-start(f32[128,128]{0,1:T(8,128)S(1)} %add.113), channel_id=1, source_target_pairs={{0,8},{8,0},{16,24},{24,16},{1,9},{9,1},{17,25},{25,17},{2,10},{10... | collective-permute-start | bytes 196616 | tf_op jit(solution)/shard_map/ppermute | solution.py:419
  105.5 4.3 %collective-permute-start.10 = (f32[128,128]{0,1:T(8,128)S(1)}, f32[128,128]{0,1:T(8,128)S(1)}, u32[]{:S(2)}, u32[]{:S(2)}) collective-permute-start(f32[128,128]{0,1:T(8,128)S(1)} %add.114), channel_id=1, source_target_pairs={{0,16},{8,24},{16,0},{24,8},{1,17},{9,25},{17,1},{25,9},{2,18},{10... | collective-permute-start | bytes 196616 | tf_op jit(solution)/shard_map/ppermute | solution.py:419

commit v3 on v2

--- a/solution.py
+++ b/solution.py
@@ -344,9 +344,73 @@
     )(*metrics, *sources, low, high)
 
 
-def modes_kernel(places, inverse_ref, *rest):
-    n = len(rest) - 6
-    sources, (out, held, made, rows, in_sems, out_sems) = rest[:n], rest[n:]
+def factorize(rows, panel):
+    eight, n = rows[0].shape
+    shape = (eight, n)
+    sub = lax.broadcasted_iota(jnp.int32, shape, 0)
+    lane = lax.broadcasted_iota(jnp.int32, shape, 1)
+    rows = list(rows)
+    eyes = [jnp.where(lane == sub + eight * j, 1.0, 0.0).astype(F32) for j in range(len(rows))]
+    uppers, inverses = [], []
+
+    def spread(block, r):
+        return jnp.broadcast_to(block[r : r + 1], shape)
+
+    def join(parts):
+        out = parts[0]
+        for r in range(1, eight):
+            out = jnp.where(sub == r, parts[r], out)
+        return out
+
+    for first in range(0, len(rows), panel):
+        rest = first + panel
+        for j in range(first, rest):
+            at = eight * j
+            left = {
+                (r, c): jnp.broadcast_to(rows[j][r : r + 1, at + c : at + c + 1], shape)
+                for r in range(eight)
+                for c in range(r + 1)
+            }
+            upper = [spread(rows[j], r) for r in range(eight)]
+            inverse = [spread(eyes[j], r) for r in range(eight)]
+            for c in range(eight):
+                root = lax.rsqrt(left[c, c])
+                column = {r: left[r, c] * root for r in range(c + 1, eight)}
+                for k in range(c + 1, eight):
+                    for r in range(k, eight):
+                        left[r, k] = left[r, k] - column[r] * column[k]
+                upper[c] = upper[c] * root
+                inverse[c] = inverse[c] * root
+                for r in range(c + 1, eight):
+                    upper[r] = upper[r] - column[r] * upper[c]
+                    inverse[r] = inverse[r] - column[r] * inverse[c]
+            for k in range(j + 1, rest):
+                own = lane == sub + eight * k
+                turned = [
+                    jnp.sum(jnp.where(own, u, 0.0), axis=1, keepdims=True) for u in upper
+                ]
+                rows[k] = rows[k] - sum(t * u for t, u in zip(turned, upper))
+                eyes[k] = eyes[k] - sum(t * v for t, v in zip(turned, inverse))
+            uppers.append(join(upper))
+            inverses.append(join(inverse))
+        if rest < len(rows):
+            u = jnp.concatenate(uppers[first:rest], axis=0)
+            v = jnp.concatenate(inverses[first:rest], axis=0)
+            below = u.T[eight * rest :]
+            dot = functools.partial(
+                jnp.dot, precision=lax.Precision.HIGHEST, preferred_element_type=F32
+            )
+            du, dv = dot(below, u), dot(below, v)
+            for k in range(rest, len(rows)):
+                o = slice(eight * (k - rest), eight * (k - rest + 1))
+                rows[k] = rows[k] - du[o]
+                eyes[k] = eyes[k] - dv[o]
+    return jnp.concatenate(uppers, axis=0), jnp.concatenate(inverses, axis=0)
+
+
+def modes_kernel(places, scale, gram_ref, more_ref, *rest):
+    n = len(rest) - 7
+    sources, (out, lower_ref, held, made, rows, in_sems, out_sems) = rest[:n], rest[n:]
     snaps, comps, _, cells_y, cells_z = out.shape
 
     def reads(x):
@@ -364,6 +428,19 @@
     for x in range(len(places)):
         for copy in reads(x):
             copy.start()
+
+    upper, inverse = factorize(
+        [
+            (gram_ref[r : r + 8, :] + more_ref[r : r + 8, :]) * scale
+            for r in range(0, snaps, 8)
+        ],
+        4,
+    )
+    r = lax.broadcasted_iota(jnp.int32, (snaps, snaps), 0)
+    c = lax.broadcasted_iota(jnp.int32, (snaps, snaps), 1)
+    lower_ref[...] = jnp.where(r >= c, upper.T, 0.0)
+    inverse = inverse.astype(BF16)
+
     writes = []
     for x in range(len(places)):
         for copy in reads(x):
@@ -374,9 +451,7 @@
                 width = len(ys) * cells_z
                 at = lane + f * width
                 lane += comps * width
-                whole = jnp.dot(
-                    inverse_ref[...], held[x, :, at : at + width], preferred_element_type=F32
-                )
+                whole = jnp.dot(inverse, held[x, :, at : at + width], preferred_element_type=F32)
                 for k, y in enumerate(ys):
                     rows[f % 2, pl.ds(y, snaps, stride=PITCH), :] = whole[
                         :, k * cells_z : (k + 1) * cells_z
@@ -389,14 +464,17 @@
         w.wait()
 
 
-def modes(inverse, sources, places, cells_y, cells_z):
-    snaps = inverse.shape[0]
+def modes(gram, more, scale, sources, places, cells_y, cells_z):
+    snaps = gram.shape[0]
     cells_x = len(places)
     return pl.pallas_call(
-        functools.partial(modes_kernel, places),
-        in_specs=[VMEM] + [HBM] * len(sources),
-        out_specs=HBM,
-        out_shape=jax.ShapeDtypeStruct((snaps, 4, cells_x, cells_y, cells_z), BF16),
+        functools.partial(modes_kernel, places, scale),
+        in_specs=[VMEM, VMEM] + [HBM] * len(sources),
+        out_specs=[HBM, VMEM],
+        out_shape=[
+            jax.ShapeDtypeStruct((snaps, 4, cells_x, cells_y, cells_z), BF16),
+            jax.ShapeDtypeStruct((snaps, snaps), F32),
+        ],
         scratch_shapes=[
             pltpu.VMEM((cells_x, snaps, 4 * cells_y * cells_z), BF16),
             pltpu.VMEM((cells_x, snaps, 4, cells_y, cells_z), BF16),
@@ -405,20 +483,19 @@
             DMA((cells_x,)),
         ],
         compiler_params=PARAMS,
-    )(inverse, *sources)
+    )(gram, more, *sources)
 
 
 def total(local):
+    steps = []
     for axis in ("cross", "stream"):
         count = lax.axis_size(axis)
-        if count & (count - 1):
-            local = lax.psum(local, axis)
-            continue
-        step = 1
-        while step < count:
-            local = local + lax.ppermute(local, axis, [(i, i ^ step) for i in range(count)])
-            step *= 2
-    return local
+        steps += [(axis, count, 1 << k) for k in range((count - 1).bit_length())]
+    more = jnp.zeros_like(local)
+    for axis, count, step in steps:
+        local = local + more
+        more = lax.ppermute(local, axis, [(i, i ^ step) for i in range(count)])
+    return local, more
 
 
 def shift(cells, axis, way):
@@ -495,17 +572,15 @@
     everywhere = (
         4.0 * cells_x * lax.axis_size("stream") * cells_y * lax.axis_size("cross") * cells_z
     )
-    gram = total(middle_gram + sides_gram + outer_gram)
-    lower = jnp.linalg.cholesky(gram * (1.0 / everywhere))
-    inverse = jax.scipy.linalg.solve_triangular(lower, jnp.eye(snaps, dtype=F32), lower=True)
+    gram, more = total(middle_gram + sides_gram + outer_gram)
     places = [
         [(2, x if x < 2 else x - cells_x + 4, rows)]
         if x < 2 or x >= cells_x - 2
         else [(0, x - 2, rows_in), (1, x - 2, rows_out)]
         for x in range(cells_x)
     ]
-    basis = modes(inverse.astype(BF16), [middle, sides, outer], places, cells_y, cells_z)
-    return basis, lower
+    sources = [middle, sides, outer]
+    return tuple(modes(gram, more, 1.0 / everywhere, sources, places, cells_y, cells_z))
 
 
 def solution(mesh):

time: 145 us -> 126 us (0.87)
  other arithmetic: 25.9 us -> 3.28 us
  Pallas kernels: 68.5 us -> 73.8 us
  waiting for transfers between devices: 22.9 us -> 19.7 us
  starting transfers between devices: 20.4 us -> 22 us
    another operation x5 -> x0, other arithmetic: 23.5 us -> none  [the longest x3 12.4 us: shards(): lower = jnp.linalg.cholesky(gram * (1.0 / everywhere))]
    pallas_call x1, Pallas kernels: 10.3 us -> 15.6 us  [modes(): pl.pallas_call(functools.partial(modes_kernel, places, scale), in_specs=[...]
    unnamed x10 -> x24, local copies, waits for them, and re-layouts: 2.2 us -> 5.68 us
    pallas_call x3 -> x0, local copies, waits for them, and re-layouts: 2.79 us -> none  [fields(): pl.pallas_call(functools.partial(fields_kernel, reads, centers, ys), in_s...]
    ppermute x5, waiting for transfers between devices: 16.6 us -> 14.6 us  [total(): more = lax.ppermute(local, axis, [(i, i ^ step) for i in range(count)])]
  transfers between devices with their start and end apart: 11 -> 11, of which waited for: 6 -> 6; matrix products, arithmetic and copies ran while one was open for 3% -> 2% of each run, Pallas kernels for 25% -> 29%
where the time goes in v3:
time: 126 us; the launch traced here: 125 us
  Pallas kernels  73.8 us (59%)
  starting transfers between devices  22 us (17%)
  waiting for transfers between devices  19.7 us (16%)
  local copies, waits for them, and re-layouts  5.68 us (5%)
  other arithmetic  3.28 us (3%)
    pallas_call x3, Pallas kernels, fields(): pl.pallas_call(functools.partial(fields_kernel, reads, centers, ys), in_s...  42 us
    pallas_call x1, Pallas kernels, modes(): pl.pallas_call(functools.partial(modes_kernel, places, scale), in_specs=[...  15.6 us
    ppermute x5, waiting for transfers between devices, total(): more = lax.ppermute(local, axis, [(i, i ^ step) for i in range(count)])  14.6 us
    pallas_call x1, Pallas kernels, edges(): pl.pallas_call(edges_kernel, in_specs=[HBM], out_specs=[HBM] * 5, out_sha...  8.11 us
    pallas_call x1, Pallas kernels, planes(): pl.pallas_call(planes_kernel, in_specs=[HBM], out_specs=HBM, out_shape=ja...  8.1 us
    ppermute x1, starting transfers between devices, shards(): lax.ppermute(near, 'stream', both_ways([(i, i + 1) for i in range(0, coun...  5.83 us
    unnamed x24, local copies, waits for them, and re-layouts  5.68 us
    ppermute x1, waiting for transfers between devices, far_exchange(): half_way = lax.ppermute(far2, 'stream', [(1, 3), (2, 0)])  5.09 us
  transfers between devices with their start and end apart: 11, of which 6 were waited for; matrix products, arithmetic and copies ran while one was open for 2% of the time, Pallas kernels for 29%

profile of v3, /device:TPU:0, one launch (start us, length us, event | category | flops | bytes accessed | tf_op | source)
XLA Modules:
  0.0 125.5 jit_solution(17064589418421964806)
XLA Ops:
  0.6 8.1 %shard_map.59 = (bf16[3,2,8,128,128]{4,3,2,1,0:T(8,128)(2,1)}, bf16[3,2,4,128,128]{4,3,2,1,0:T(8,128)(2,1)}, bf16[3,2,4,128,128]{4,3,2,1,0:T(8,128)(2,1)}, bf16[...) custom-call(bf16[128,3,12,8,128]{4,3,2,1,0:T(8,128)(2,1)} %velocity.2), custom_call_target="tpu_custom_call" | custom-call | tf_op jit(solution)/shard_map/pallas_call | solution.py:126
  8.7 1.3 %collective-permute-start.2 = (bf16[3,12,2,128,128]{4,3,2,1,0:T(8,128)(2,1)}, bf16[3,12,2,128,128]{4,3,2,1,0:T(8,128)(2,1)S(1)}, u32[]{:S(2)}, u32[]{:S(2)}) collective-permute-start(bf16[3,12,2,128,128]{4,3,2,1,0:T(8,128)(2,1)} %get-tuple-element.20.rest_1_), channel_id=1, source_target_pairs={{1,0},{2,1},{3,2},{4,3},{5,4},{6,5},{7,6},{9,8},{10,9},{11,10},{12... | collective-permute-start | bytes 7077896 | tf_op jit(solution)/shard_map/ppermute | solution.py:504
  10.0 3.2 %collective-permute-start.1 = (bf16[3,12,2,128,128]{4,3,2,1,0:T(8,128)(2,1)}, bf16[3,12,2,128,128]{4,3,2,1,0:T(8,128)(2,1)S(1)}, u32[]{:S(2)}, u32[]{:S(2)}) collective-permute-start(bf16[3,12,2,128,128]{4,3,2,1,0:T(8,128)(2,1)} %get-tuple-element.21.rest_2_), channel_id=1, source_target_pairs={{0,1},{1,2},{2,3},{3,4},{4,5},{5,6},{6,7},{8,9},{9,10},{10,11},{11... | collective-permute-start | bytes 7077896 | tf_op jit(solution)/shard_map/ppermute | solution.py:504
  13.2 1.3 %collective-permute-start = (bf16[3,2,4,128,128]{4,3,2,1,0:T(8,128)(2,1)}, bf16[3,2,4,128,128]{4,3,2,1,0:T(8,128)(2,1)}, u32[]{:S(2)}, u32[]{:S(2)}) collective-permute-start(bf16[3,2,4,128,128]{4,3,2,1,0:T(8,128)(2,1)} %get-tuple-element.16), channel_id=1, source_target_pairs={{8,24},{16,0},{9,25},{17,1},{10,26},{18,2},{11,27},{19,3},{12,28},... | collective-permute-start | bytes 2359304 | tf_op jit(solution)/shard_map/ppermute | solution.py:515
  14.5 5.8 %collective-permute-start.3 = (bf16[3,2,8,128,128]{4,3,2,1,0:T(8,128)(2,1)}, bf16[3,2,8,128,128]{4,3,2,1,0:T(8,128)(2,1)S(1)}, u32[]{:S(2)}, u32[]{:S(2)}) collective-permute-start(bf16[3,2,8,128,128]{4,3,2,1,0:T(8,128)(2,1)} %get-tuple-element.17), channel_id=1, source_target_pairs={{0,8},{8,0},{16,24},{24,16},{1,9},{9,1},{17,25},{25,17},{2,10},{10... | collective-permute-start | bytes 4718600 | tf_op jit(solution)/shard_map/ppermute | solution.py:526
  20.4 0.8 collective-permute-start.4
  21.2 8.1 %shard_map.60.rest_0_ = bf16[3,12,8,128,128]{4,3,2,1,0:T(8,128)(2,1)} custom-call(bf16[128,3,12,8,128]{4,3,2,1,0:T(8,128)(2,1)} %velocity.2), custom_call_target="tpu_custom_call" | custom-call | tf_op jit(solution)/shard_map/pallas_call | solution.py:178
  29.3 0.5 broadcast_multiply_fusion.1.mx_ref
  29.9 5.1 %collective-permute-done = bf16[3,2,4,128,128]{4,3,2,1,0:T(8,128)(2,1)} collective-permute-done((bf16[3,2,4,128,128]{4,3,2,1,0:T(8,128)(2,1)}, bf16[3,2,4,128,128]{4,3,2,1,0:T(8,128)(2,1)}, u32[]{:S(2)}, u32[]{:S(2)}) %collective-permute-start) | collective-permute-done | bytes 786464 | tf_op jit(solution)/shard_map/ppermute | solution.py:515
  35.0 4.6 %collective-permute-start.5 = (bf16[3,2,4,128,128]{4,3,2,1,0:T(8,128)(2,1)}, bf16[3,2,4,128,128]{4,3,2,1,0:T(8,128)(2,1)S(1)}, u32[]{:S(2)}, u32[]{:S(2)}) collective-permute-start(bf16[3,2,4,128,128]{4,3,2,1,0:T(8,128)(2,1)} %collective-permute-done), channel_id=1, source_target_pairs={{24,16},{0,8},{25,17},{1,9},{26,18},{2,10},{27,19},{3,11},{28,20},... | collective-permute-start | bytes 2359304 | tf_op jit(solution)/shard_map/ppermute | solution.py:516
  39.6 0.5 broadcast_multiply_fusion.my_ref
  40.1 0.6 multiply_bitcast_fusion.mz_ref
  40.7 0.7 add_convert_fusion.taps_ref
  41.4 14.3 %shard_map.61 = (bf16[8,128,2048]{2,1,0:T(8,128)(2,1)}, f32[128,128]{1,0:T(8,128)}) custom-call(f32[12]{0:T(128)} %broadcast_multiply_fusion.1.mx_ref, f32[8]{0:T(128)} %broadcast_multiply_fusion.my_ref, f32[1,128]{1,0:T(1,128)} %multiply_bitcast_fusion.mz_ref, bf16[128,128]{1,0:T(8,128)(2,1)} %add_convert_fusion.taps_ref, ...), custom_call_target="tpu_custom_call" | custom-call | tf_op jit(solution)/shard_map/pallas_call | solution.py:325
  55.8 1.4 %copy-done = bf16[3,12,2,128,128]{4,3,2,1,0:T(8,128)(2,1)} copy-done((bf16[3,12,2,128,128]{4,3,2,1,0:T(8,128)(2,1)}, bf16[3,12,2,128,128]{4,3,2,1,0:T(8,128)(2,1)S(1)}, u32[]{:S(2)}) %copy-start) | copy-done | bytes 2359320
  57.2 1.4 %copy-done.1 = bf16[3,12,2,128,128]{4,3,2,1,0:T(8,128)(2,1)} copy-done((bf16[3,12,2,128,128]{4,3,2,1,0:T(8,128)(2,1)}, bf16[3,12,2,128,128]{4,3,2,1,0:T(8,128)(2,1)S(1)}, u32[]{:S(2)}) %copy-start.1) | copy-done | bytes 2359320
  58.5 14.5 %shard_map.62 = (bf16[8,128,2048]{2,1,0:T(8,128)(2,1)}, f32[128,128]{1,0:T(8,128)}) custom-call(f32[12]{0:T(128)} %broadcast_multiply_fusion.1.mx_ref, f32[8]{0:T(128)} %broadcast_multiply_fusion.my_ref, f32[1,128]{1,0:T(1,128)} %multiply_bitcast_fusion.mz_ref, bf16[128,128]{1,0:T(8,128)(2,1)} %add_convert_fusion.taps_ref, ...), custom_call_target="tpu_custom_call" | custom-call | tf_op jit(solution)/shard_map/pallas_call | solution.py:325
  73.1 0.9 copy-done.3
  73.9 0.5 copy-done.2
  74.5 0.9 copy-done.4
  75.4 13.2 %shard_map.63 = (bf16[4,128,4096]{2,1,0:T(8,128)(2,1)}, f32[128,128]{1,0:T(8,128)}) custom-call(f32[12]{0:T(128)} %broadcast_multiply_fusion.1.mx_ref, f32[8]{0:T(128)} %broadcast_multiply_fusion.my_ref, f32[1,128]{1,0:T(1,128)} %multiply_bitcast_fusion.mz_ref, bf16[128,128]{1,0:T(8,128)(2,1)} %add_convert_fusion.taps_ref, ...), custom_call_target="tpu_custom_call" | custom-call | tf_op jit(solution)/shard_map/pallas_call | solution.py:325
  88.6 0.9 add_add_fusion
  89.6 1.2 collective-permute-done.6
  90.8 1.3 %collective-permute-start.7 = (f32[128,128]{1,0:T(8,128)S(1)}, f32[128,128]{1,0:T(8,128)S(1)}, u32[]{:S(2)}, u32[]{:S(2)}) collective-permute-start(f32[128,128]{1,0:T(8,128)S(1)} %add.96), channel_id=1, source_target_pairs={{0,2},{1,3},{2,0},{3,1},{4,6},{5,7},{6,4},{7,5},{8,10},{9,11},{10,... | collective-permute-start | bytes 196616 | tf_op jit(solution)/shard_map/ppermute | solution.py:497
  92.2 3.0 %collective-permute-done.7 = f32[128,128]{1,0:T(8,128)S(1)} collective-permute-done((f32[128,128]{1,0:T(8,128)S(1)}, f32[128,128]{1,0:T(8,128)S(1)}, u32[]{:S(2)}, u32[]{:S(2)}) %collective-permute-start.7) | collective-permute-done | bytes 65568 | tf_op jit(solution)/shard_map/ppermute | solution.py:497
  95.2 2.4 %collective-permute-start.8 = (f32[128,128]{1,0:T(8,128)S(1)}, f32[128,128]{1,0:T(8,128)S(1)}, u32[]{:S(2)}, u32[]{:S(2)}) collective-permute-start(f32[128,128]{1,0:T(8,128)S(1)} %add.97), channel_id=1, source_target_pairs={{0,4},{1,5},{2,6},{3,7},{4,0},{5,1},{6,2},{7,3},{8,12},{9,13},{10,... | collective-permute-start | bytes 196616 | tf_op jit(solution)/shard_map/ppermute | solution.py:497
  97.5 2.9 %collective-permute-done.8 = f32[128,128]{1,0:T(8,128)S(1)} collective-permute-done((f32[128,128]{1,0:T(8,128)S(1)}, f32[128,128]{1,0:T(8,128)S(1)}, u32[]{:S(2)}, u32[]{:S(2)}) %collective-permute-start.8) | collective-permute-done | bytes 65568 | tf_op jit(solution)/shard_map/ppermute | solution.py:497
  100.5 4.2 %collective-permute-done.9 = f32[128,128]{1,0:T(8,128)S(1)} collective-permute-done((f32[128,128]{1,0:T(8,128)S(1)}, f32[128,128]{1,0:T(8,128)S(1)}, u32[]{:S(2)}, u32[]{:S(2)}) %collective-permute-start.9) | collective-permute-done | bytes 65568 | tf_op jit(solution)/shard_map/ppermute | solution.py:497
  104.8 1.1 collective-permute-start.10
  105.8 3.3 %collective-permute-done.10.more_ref = f32[128,128]{1,0:T(8,128)S(1)} collective-permute-done((f32[128,128]{1,0:T(8,128)S(1)}, f32[128,128]{1,0:T(8,128)S(1)}, u32[]{:S(2)}, u32[]{:S(2)}) %collective-permute-start.10) | collective-permute-done | bytes 65568 | tf_op jit(solution)/shard_map/ppermute | solution.py:497
  109.1 0.6 copy-done.6
  109.7 15.6 %shard_map.64 = (bf16[128,4,12,8,128]{4,3,2,1,0:T(8,128)(2,1)}, f32[128,128]{1,0:T(8,128)}) custom-call(f32[128,128]{1,0:T(8,128)} %copy-done.5, f32[128,128]{1,0:T(8,128)} %copy-done.6, bf16[8,128,2048]{2,1,0:T(8,128)(2,1)} %get-tuple-element.27.rest_0_, bf16[8,128,2048]{2,1,0:T(8,128)(2,1)} %get-tuple-element.28.rest_1_, ...), custom_call_target="tpu_custom_call" | custom-call | tf_op jit(solution)/shard_map/pallas_call | solution.py:470
  (31 shorter events, 0.3 us)
Async XLA Ops:
  8.7 47.0 %collective-permute-start.2 = (bf16[3,12,2,128,128]{4,3,2,1,0:T(8,128)(2,1)}, bf16[3,12,2,128,128]{4,3,2,1,0:T(8,128)(2,1)S(1)}, u32[]{:S(2)}, u32[]{:S(2)}) collective-permute-start(bf16[3,12,2,128,128]{4,3,2,1,0:T(8,128)(2,1)} %get-tuple-element.20.rest_1_), channel_id=1, source_target_pairs={{1,0},{2,1},{3,2},{4,3},{5,4},{6,5},{7,6},{9,8},{10,9},{11,10},{12... | collective-permute-start | bytes 7077896 | tf_op jit(solution)/shard_map/ppermute | solution.py:504
  10.0 45.7 %collective-permute-start.1 = (bf16[3,12,2,128,128]{4,3,2,1,0:T(8,128)(2,1)}, bf16[3,12,2,128,128]{4,3,2,1,0:T(8,128)(2,1)S(1)}, u32[]{:S(2)}, u32[]{:S(2)}) collective-permute-start(bf16[3,12,2,128,128]{4,3,2,1,0:T(8,128)(2,1)} %get-tuple-element.21.rest_2_), channel_id=1, source_target_pairs={{0,1},{1,2},{2,3},{3,4},{4,5},{5,6},{6,7},{8,9},{9,10},{10,11},{11... | collective-permute-start | bytes 7077896 | tf_op jit(solution)/shard_map/ppermute | solution.py:504
  13.2 21.7 %collective-permute-start = (bf16[3,2,4,128,128]{4,3,2,1,0:T(8,128)(2,1)}, bf16[3,2,4,128,128]{4,3,2,1,0:T(8,128)(2,1)}, u32[]{:S(2)}, u32[]{:S(2)}) collective-permute-start(bf16[3,2,4,128,128]{4,3,2,1,0:T(8,128)(2,1)} %get-tuple-element.16), channel_id=1, source_target_pairs={{8,24},{16,0},{9,25},{17,1},{10,26},{18,2},{11,27},{19,3},{12,28},... | collective-permute-start | bytes 2359304 | tf_op jit(solution)/shard_map/ppermute | solution.py:515
  14.5 58.5 %collective-permute-start.3 = (bf16[3,2,8,128,128]{4,3,2,1,0:T(8,128)(2,1)}, bf16[3,2,8,128,128]{4,3,2,1,0:T(8,128)(2,1)S(1)}, u32[]{:S(2)}, u32[]{:S(2)}) collective-permute-start(bf16[3,2,8,128,128]{4,3,2,1,0:T(8,128)(2,1)} %get-tuple-element.17), channel_id=1, source_target_pairs={{0,8},{8,0},{16,24},{24,16},{1,9},{9,1},{17,25},{25,17},{2,10},{10... | collective-permute-start | bytes 4718600 | tf_op jit(solution)/shard_map/ppermute | solution.py:526
  20.4 9.0 %copy-start.9 = (f32[12]{0:T(128)S(1)}, f32[12]{0:T(128)}, u32[]{:S(2)}) copy-start(f32[12]{0:T(128)} %param.5) | copy-start | bytes 148
  20.4 19.2 %copy-start.10 = (f32[8]{0:T(128)S(1)}, f32[8]{0:T(128)}, u32[]{:S(2)}) copy-start(f32[8]{0:T(128)} %param.6) | copy-start | bytes 100
  20.4 19.7 %copy-start.11 = (f32[128]{0:T(128)S(1)}, f32[128]{0:T(128)}, u32[]{:S(2)}) copy-start(f32[128]{0:T(128)} %param.7) | copy-start | bytes 1540
  20.4 52.7 %collective-permute-start.4 = (bf16[3,2,4,128,128]{4,3,2,1,0:T(8,128)(2,1)}, bf16[3,2,4,128,128]{4,3,2,1,0:T(8,128)(2,1)S(1)}, u32[]{:S(2)}, u32[]{:S(2)}) collective-permute-start(bf16[3,2,4,128,128]{4,3,2,1,0:T(8,128)(2,1)} %get-tuple-element.24), channel_id=1, source_target_pairs={{8,16},{16,8},{9,17},{17,9},{10,18},{18,10},{11,19},{19,11},{12,20... | collective-permute-start | bytes 2359304 | tf_op jit(solution)/shard_map/ppermute | solution.py:527
  35.0 38.1 %collective-permute-start.5 = (bf16[3,2,4,128,128]{4,3,2,1,0:T(8,128)(2,1)}, bf16[3,2,4,128,128]{4,3,2,1,0:T(8,128)(2,1)S(1)}, u32[]{:S(2)}, u32[]{:S(2)}) collective-permute-start(bf16[3,2,4,128,128]{4,3,2,1,0:T(8,128)(2,1)} %collective-permute-done), channel_id=1, source_target_pairs={{24,16},{0,8},{25,17},{1,9},{26,18},{2,10},{27,19},{3,11},{28,20},... | collective-permute-start | bytes 2359304 | tf_op jit(solution)/shard_map/ppermute | solution.py:516
  55.8 1.4 %copy-start = (bf16[3,12,2,128,128]{4,3,2,1,0:T(8,128)(2,1)}, bf16[3,12,2,128,128]{4,3,2,1,0:T(8,128)(2,1)S(1)}, u32[]{:S(2)}) copy-start(bf16[3,12,2,128,128]{4,3,2,1,0:T(8,128)(2,1)S(1)} %collective-permute-done.2.rest_2_.rest_5_) | copy-start | bytes 7077892
  57.2 1.4 %copy-start.1 = (bf16[3,12,2,128,128]{4,3,2,1,0:T(8,128)(2,1)}, bf16[3,12,2,128,128]{4,3,2,1,0:T(8,128)(2,1)S(1)}, u32[]{:S(2)}) copy-start(bf16[3,12,2,128,128]{4,3,2,1,0:T(8,128)(2,1)S(1)} %collective-permute-done.1.rest_1_.rest_4_) | copy-start | bytes 7077892
  73.0 15.6 %copy-start.7 = (f32[128,128]{1,0:T(8,128)S(1)}, f32[128,128]{1,0:T(8,128)}, u32[]{:S(2)}) copy-start(f32[128,128]{1,0:T(8,128)} %get-tuple-element.22) | copy-start | bytes 196612
  73.0 15.6 %copy-start.8 = (f32[128,128]{1,0:T(8,128)S(1)}, f32[128,128]{1,0:T(8,128)}, u32[]{:S(2)}) copy-start(f32[128,128]{1,0:T(8,128)} %get-tuple-element.23) | copy-start | bytes 196612
  73.0 0.9 copy-start.3
  73.1 1.4 %copy-start.2 = (bf16[3,2,8,128,128]{4,3,2,1,0:T(8,128)(2,1)}, bf16[3,2,8,128,128]{4,3,2,1,0:T(8,128)(2,1)S(1)}, u32[]{:S(2)}) copy-start(bf16[3,2,8,128,128]{4,3,2,1,0:T(8,128)(2,1)S(1)} %collective-permute-done.3.rest_1_) | copy-start | bytes 4718596
  74.5 0.9 copy-start.4
  89.5 1.3 %collective-permute-start.6 = (f32[128,128]{1,0:T(8,128)S(1)}, f32[128,128]{1,0:T(8,128)S(1)}, u32[]{:S(2)}, u32[]{:S(2)}) collective-permute-start(f32[128,128]{1,0:T(8,128)S(1)} %add_add_fusion), channel_id=1, source_target_pairs={{0,1},{1,0},{2,3},{3,2},{4,5},{5,4},{6,7},{7,6},{8,9},{9,8},{10,11... | collective-permute-start | bytes 196616 | tf_op jit(solution)/shard_map/ppermute | solution.py:497
  90.8 4.3 %collective-permute-start.7 = (f32[128,128]{1,0:T(8,128)S(1)}, f32[128,128]{1,0:T(8,128)S(1)}, u32[]{:S(2)}, u32[]{:S(2)}) collective-permute-start(f32[128,128]{1,0:T(8,128)S(1)} %add.96), channel_id=1, source_target_pairs={{0,2},{1,3},{2,0},{3,1},{4,6},{5,7},{6,4},{7,5},{8,10},{9,11},{10,... | collective-permute-start | bytes 196616 | tf_op jit(solution)/shard_map/ppermute | solution.py:497
  95.2 5.2 %collective-permute-start.8 = (f32[128,128]{1,0:T(8,128)S(1)}, f32[128,128]{1,0:T(8,128)S(1)}, u32[]{:S(2)}, u32[]{:S(2)}) collective-permute-start(f32[128,128]{1,0:T(8,128)S(1)} %add.97), channel_id=1, source_target_pairs={{0,4},{1,5},{2,6},{3,7},{4,0},{5,1},{6,2},{7,3},{8,12},{9,13},{10,... | collective-permute-start | bytes 196616 | tf_op jit(solution)/shard_map/ppermute | solution.py:497
  100.4 4.3 %collective-permute-start.9 = (f32[128,128]{1,0:T(8,128)S(1)}, f32[128,128]{1,0:T(8,128)S(1)}, u32[]{:S(2)}, u32[]{:S(2)}) collective-permute-start(f32[128,128]{1,0:T(8,128)S(1)} %add.98), channel_id=1, source_target_pairs={{0,8},{8,0},{16,24},{24,16},{1,9},{9,1},{17,25},{25,17},{2,10},{10... | collective-permute-start | bytes 196616 | tf_op jit(solution)/shard_map/ppermute | solution.py:497
  104.8 4.3 %copy-start.5 = (f32[128,128]{1,0:T(8,128)}, f32[128,128]{1,0:T(8,128)S(1)}, u32[]{:S(2)}) copy-start(f32[128,128]{1,0:T(8,128)S(1)} %add.99.gram_ref) | copy-start | bytes 196612
  104.8 4.3 %collective-permute-start.10 = (f32[128,128]{1,0:T(8,128)S(1)}, f32[128,128]{1,0:T(8,128)S(1)}, u32[]{:S(2)}, u32[]{:S(2)}) collective-permute-start(f32[128,128]{1,0:T(8,128)S(1)} %add.99.gram_ref), channel_id=1, source_target_pairs={{0,16},{8,24},{16,0},{24,8},{1,17},{9,25},{17,1},{25,9},{2,18},{10... | collective-permute-start | bytes 196616 | tf_op jit(solution)/shard_map/ppermute | solution.py:497
  109.1 0.6 copy-start.6

commit v4 on v3

--- a/solution.py
+++ b/solution.py
@@ -8,15 +8,17 @@
 from jax.sharding import PartitionSpec as P
 
 F32, BF16 = jnp.float32, jnp.bfloat16
-VMEM_LIMIT = 56 * 1024 * 1024
 PITCH = 9
 ROWS = 16
+SLOTS = 4
 HBM = pl.BlockSpec(memory_space=pl.ANY)
 SMEM = pl.BlockSpec(memory_space=pltpu.SMEM)
 VMEM = pl.BlockSpec(memory_space=pltpu.VMEM)
-PARAMS = pltpu.CompilerParams(vmem_limit_bytes=VMEM_LIMIT)
-SHORT = pl.CostEstimate(flops=1024, bytes_accessed=1024, transcendentals=0)
 DMA = pltpu.SemaphoreType.DMA
+
+
+def limit(mib):
+    return pltpu.CompilerParams(vmem_limit_bytes=mib * 1024 * 1024)
 
 
 def turn(tile, rows, ys, put):
@@ -139,7 +141,7 @@
             DMA((3 * comps,)),
             DMA((2, comps, cells_x)),
         ],
-        compiler_params=PARAMS,
+        compiler_params=limit(60),
     )(velocity)
 
 
@@ -187,29 +189,28 @@
             DMA((comps, cells_x)),
             DMA((comps, cells_x)),
         ],
-        compiler_params=PARAMS,
+        compiler_params=limit(60),
     )(velocity)
 
 
-def layer_fields(ys, ring, slots, rz, low, high, metric_x, metric_y_ref, metric_z, out_ref):
+def layer_fields(ring, slots, rz, low, high, metric_x, metric_y_ref, metric_z, puts):
     cells_y, snaps, cells_z = ring.shape[2:]
     back2, back1, here, fore1, fore2 = slots
 
     def some_rows(step, _):
         at = pl.ds(pl.multiple_of(step * ROWS, ROWS), ROWS)
-        held = {}
 
         def row(comp, y):
-            if (comp, y) not in held:
-                if y < 0:
-                    held[comp, y] = low[comp, y + 2, at, :].astype(F32)
-                elif y >= cells_y:
-                    held[comp, y] = high[comp, y - cells_y, at, :].astype(F32)
-                else:
-                    held[comp, y] = ring[here, comp, y, at, :]
-            return held[comp, y]
-
-        for n, y in enumerate(ys):
+            if y < 0:
+                return low[comp, y + 2, at, :].astype(F32)
+            if y >= cells_y:
+                return high[comp, y - cells_y, at, :].astype(F32)
+            return ring[here, comp, y, at, :]
+
+        window = [[row(c, y) for y in range(-2, 2)] for c in range(3)]
+        for y in range(cells_y):
+            for c in range(3):
+                window[c].append(row(c, y + 2))
 
             def along_x(c):
                 near = ring[fore1, c, y, at, :] - ring[back1, c, y, at, :]
@@ -217,131 +218,226 @@
                 return (8.0 * near - far) * metric_x
 
             def along_y(c):
-                near = row(c, y + 1) - row(c, y - 1)
-                far = row(c, y + 2) - row(c, y - 2)
-                return (8.0 * near - far) * metric_y_ref[y]
+                w = window[c]
+                return (8.0 * (w[3] - w[1]) - (w[4] - w[0])) * metric_y_ref[y]
 
             def along_z(c):
                 return rz[c, y, at, :] * metric_z
 
-            outs = (
-                along_y(2) - along_z(1),
-                along_z(0) - along_x(2),
-                along_x(1) - along_y(0),
-                along_x(0) + along_y(1) + along_z(2),
+            puts[0](at, y, along_y(2) - along_z(1))
+            puts[1](at, y, along_z(0) - along_x(2))
+            puts[2](at, y, along_x(1) - along_y(0))
+            puts[3](at, y, along_x(0) + along_y(1) + along_z(2))
+            for c in range(3):
+                window[c] = window[c][1:]
+        return 0
+
+    lax.fori_loop(0, snaps // ROWS, some_rows, 0)
+
+
+def inner_kernel(mx_ref, my_ref, mz_ref, taps_ref, cells, low, high, *rest):
+    middle, ends, parts, gram_ref = rest[:4]
+    layers, lows, highs, ring, rz_ring, done, done_ends, done_parts, in_sems, out_sems = rest[4:]
+    comps, cells_y, snaps, cells_z = ring.shape[1:]
+    cells_x = lows.shape[0]
+    width = cells_y * cells_z
+
+    def reads(x):
+        return [
+            pltpu.make_async_copy(cells.at[:, x], layers.at[x % SLOTS], in_sems.at[0, x]),
+            pltpu.make_async_copy(low.at[:, x], lows.at[x], in_sems.at[1, x]),
+            pltpu.make_async_copy(high.at[:, x], highs.at[x], in_sems.at[2, x]),
+        ]
+
+    def put_in(ref, lane):
+        def put(at, y, value):
+            ref[at, lane + y * cells_z : lane + (y + 1) * cells_z] = value.astype(ref.dtype)
+
+        return put
+
+    for x in range(SLOTS):
+        for copy in reads(x):
+            copy.start()
+    gram_ref[...] = jnp.zeros_like(gram_ref)
+    writes, middle_writes = [], []
+
+    def write(src, dst):
+        sem = out_sems.at[len(writes) + len(middle_writes)]
+        writes.append(pltpu.make_async_copy(src, dst, sem))
+        writes[-1].start()
+
+    for i in range(cells_x + 4):
+        if 2 <= i < cells_x + 2:
+            for copy in reads(i - 2):
+                copy.wait()
+            slot = layers.at[(i - 2) % SLOTS]
+            ring[i % 5] = slot[...].astype(F32)
+            flat = slot[...].reshape(comps * cells_y * snaps, cells_z)
+            rz_ring[i % 3] = jnp.dot(flat, taps_ref[...], preferred_element_type=F32).reshape(
+                comps, cells_y, snaps, cells_z
             )
-            for f, value in enumerate(outs):
-                lane = (f * len(ys) + n) * cells_z
-                out_ref[at, lane : lane + cells_z] = value.astype(BF16)
-        return 0
-
-    lax.fori_loop(0, snaps // ROWS, some_rows, 0)
-
-
-def runs(ys):
-    found = []
-    for y in ys:
-        if found and found[-1][1] == y:
-            found[-1][1] = y + 1
+            if i - 2 + SLOTS < cells_x:
+                for copy in reads(i - 2 + SLOTS):
+                    copy.start()
         else:
-            found.append([y, y + 1])
-    return found
-
-
-def fields_kernel(reads, centers, ys, mx_ref, my_ref, mz_ref, taps_ref, *rest):
-    n = len(rest) - 12
-    sources, (low, high, out, gram_ref) = rest[:n], rest[n : n + 4]
-    layers, lows, highs, ring, rz_ring, done, in_sems, out_sems = rest[n + 4 :]
-    comps, cells_y, snaps, cells_z = ring.shape[1:]
-    steps = len(centers)
-    kept = [i for i in range(steps) if centers[i] is not None]
-    lowest, highest = min(ys) < 2, max(ys) >= cells_y - 2
-
-    def whichever(i, start):
-        for m, (src, rows, cond) in enumerate(reads[i](sources)):
-            copy = pltpu.make_async_copy(src, layers.at[i, :, rows], in_sems.at[0, i, m])
-            if cond is None:
-                getattr(copy, "start" if start else "wait")()
-            else:
-                pl.when(cond)(copy.start if start else copy.wait)
-
-    def sides(k):
-        x = centers[kept[k]]
-        copies = []
-        if lowest:
-            copies.append(pltpu.make_async_copy(low.at[:, x], lows.at[k], in_sems.at[1, k, 0]))
-        if highest:
-            copies.append(pltpu.make_async_copy(high.at[:, x], highs.at[k], in_sems.at[2, k, 0]))
-        return copies
-
-    for i in range(steps):
-        whichever(i, True)
-        if centers[i] is not None:
-            for copy in sides(kept.index(i)):
-                copy.start()
-
-    gram_ref[...] = jnp.zeros_like(gram_ref)
-    writes = []
-    for i in range(steps):
-        whichever(i, False)
-        ring[i % 5] = layers[i].astype(F32)
-        if i + 2 < steps and centers[i + 2] is not None:
-            for a, b in runs(ys):
-                flat = layers[i, :, a:b].reshape(comps * (b - a) * snaps, cells_z)
-                rz_ring[i % 3, :, a:b] = jnp.dot(
-                    flat, taps_ref[...], preferred_element_type=F32
-                ).reshape(comps, b - a, snaps, cells_z)
-        if centers[i] is None:
+            ring[i % 5] = jnp.zeros(ring.shape[1:], F32)
+        x = i - 4
+        if x < 0:
             continue
-        k = kept.index(i)
-        for copy in sides(k):
-            copy.wait()
+        is_inner = 2 <= x < cells_x - 2
+        e = x if x < 2 else x - cells_x + 4
+        if is_inner:
+            made = done.at[x % SLOTS]
+            if x - 2 >= SLOTS:
+                middle_writes[x - 2 - SLOTS].wait()
+            puts = [put_in(made, f * width) for f in range(4)]
+        else:
+            made = done_ends.at[e]
+            puts = [put_in(made, 0)]
+            puts += [put_in(done_parts.at[e], f * width) for f in range(3)]
         layer_fields(
-            ys,
             ring,
             [(i + 1 + s) % 5 for s in range(5)],
             rz_ring.at[(i - 2) % 3],
-            lows.at[k],
-            highs.at[k],
-            mx_ref[centers[i]],
+            lows.at[x],
+            highs.at[x],
+            mx_ref[x],
             my_ref,
             mz_ref[...],
-            done.at[k],
+            puts,
         )
-        writes.append(pltpu.make_async_copy(done.at[k], out.at[k], out_sems.at[k]))
+        if is_inner:
+            write(made, middle.at[x - 2])
+            middle_writes.append(writes.pop())
+        else:
+            write(made, ends.at[e])
+            write(done_parts.at[e], parts.at[e])
+        gram_ref[...] += lax.dot_general(
+            made[...], made[...], (((1,), (1,)), ((), ())), preferred_element_type=F32
+        )
+    for w in writes + middle_writes[-SLOTS:]:
+        w.wait()
+
+
+def inner_fields(cells, low, high, metrics):
+    comps, cells_x, cells_y, snaps, cells_z = cells.shape
+    width = cells_y * cells_z
+    return pl.pallas_call(
+        inner_kernel,
+        in_specs=[SMEM, SMEM, VMEM, VMEM] + [HBM] * 3,
+        out_specs=[HBM] * 3 + [VMEM],
+        out_shape=[
+            jax.ShapeDtypeStruct((cells_x - 4, snaps, 4 * width), BF16),
+            jax.ShapeDtypeStruct((4, snaps, width), BF16),
+            jax.ShapeDtypeStruct((4, snaps, 3 * width), F32),
+            jax.ShapeDtypeStruct((snaps, snaps), F32),
+        ],
+        scratch_shapes=[
+            pltpu.VMEM((SLOTS, comps, cells_y, snaps, cells_z), BF16),
+            pltpu.VMEM((cells_x, comps, 2, snaps, cells_z), BF16),
+            pltpu.VMEM((cells_x, comps, 2, snaps, cells_z), BF16),
+            pltpu.VMEM((5, comps, cells_y, snaps, cells_z), F32),
+            pltpu.VMEM((3, comps, cells_y, snaps, cells_z), F32),
+            pltpu.VMEM((SLOTS, snaps, 4 * width), BF16),
+            pltpu.VMEM((4, snaps, width), BF16),
+            pltpu.VMEM((4, snaps, 3 * width), F32),
+            DMA((3, cells_x)),
+            DMA((cells_x + 4,)),
+        ],
+        compiler_params=limit(36),
+    )(*metrics, cells, low, high)
+
+
+def outer_kernel(near, far1, far2, parts, mx_ref, gram_ref, out, total_ref, *rest):
+    taken, halos, done, part_sems, halo_sems, out_sems = rest
+    _, comps, _, cells_y, snaps, cells_z = halos.shape
+    half = cells_y // 2
+    width = cells_y * cells_z
+    cells_x = mx_ref.shape[0]
+    odd = lax.rem(lax.axis_index("stream"), 2)
+
+    def part_read(e):
+        return pltpu.make_async_copy(parts.at[e], taken.at[e], part_sems.at[e])
+
+    def halo_reads(side, run):
+        sem = halo_sems.at[side]
+        is_near = (odd == 1) == (side == 0)
+        first, second = pl.ds(0, half), pl.ds(half, half)
+
+        @pl.when(is_near)
+        def _():
+            run(pltpu.make_async_copy(near, halos.at[side], sem.at[0]))
+
+        @pl.when(jnp.logical_not(is_near))
+        def _():
+            run(pltpu.make_async_copy(far1, halos.at[side, :, :, first], sem.at[0]))
+            run(pltpu.make_async_copy(far2, halos.at[side, :, :, second], sem.at[1]))
+
+    for side in range(2):
+        halo_reads(side, lambda copy: copy.start())
+        for e in (2 * side, 2 * side + 1):
+            part_read(e).start()
+    total = gram_ref[...]
+    writes = []
+    last = cells_x - 1
+    plan = (
+        (0, 0, 0, (1.0, -8.0)),
+        (1, 1, 0, (0.0, 1.0)),
+        (2, last - 1, 1, (-1.0, 0.0)),
+        (3, last, 1, (8.0, -1.0)),
+    )
+    for e, x, side, weights in plan:
+        if e % 2 == 0:
+            halo_reads(side, lambda copy: copy.wait())
+        part_read(e).wait()
+        metric_x = mx_ref[x]
+
+        def some_rows(step, _):
+            at = pl.ds(pl.multiple_of(step * ROWS, ROWS), ROWS)
+            for f, (comp, sign) in enumerate(((2, -1.0), (1, 1.0), (0, 1.0))):
+                for y in range(cells_y):
+                    lanes = slice(f * width + y * cells_z, f * width + (y + 1) * cells_z)
+                    sums = [
+                        (sign * w) * halos[side, comp, k, y, at, :].astype(F32)
+                        for k, w in enumerate(weights)
+                        if w
+                    ]
+                    value = taken[e, at, lanes] + functools.reduce(jnp.add, sums) * metric_x
+                    done[e, at, lanes] = value.astype(BF16)
+            return 0
+
+        lax.fori_loop(0, snaps // ROWS, some_rows, 0)
+        writes.append(pltpu.make_async_copy(done.at[e], out.at[e], out_sems.at[e]))
         writes[-1].start()
-        gram_ref[...] += lax.dot_general(
-            done[k], done[k], (((1,), (1,)), ((), ())), preferred_element_type=F32
+        total += lax.dot_general(
+            done[e], done[e], (((1,), (1,)), ((), ())), preferred_element_type=F32
         )
+    total_ref[...] = total
     for w in writes:
         w.wait()
 
 
-def fields(sources, reads, centers, ys, low, high, metrics):
-    comps, _, cells_y, snaps, cells_z = sources[0].shape
-    steps = len(centers)
-    kept = sum(c is not None for c in centers)
-    lanes = 4 * len(ys) * cells_z
+def outer_fields(metric_x, gram, parts, near, far1, far2):
+    comps, _, cells_y, snaps, cells_z = near.shape
+    lanes = parts.shape[2]
     return pl.pallas_call(
-        functools.partial(fields_kernel, reads, centers, ys),
-        in_specs=[SMEM, SMEM, VMEM, VMEM] + [HBM] * (len(sources) + 2),
+        outer_kernel,
+        in_specs=[HBM] * 4 + [SMEM, VMEM],
         out_specs=[HBM, VMEM],
         out_shape=[
-            jax.ShapeDtypeStruct((kept, snaps, lanes), BF16),
+            jax.ShapeDtypeStruct(parts.shape, BF16),
             jax.ShapeDtypeStruct((snaps, snaps), F32),
         ],
         scratch_shapes=[
-            pltpu.VMEM((steps, comps, cells_y, snaps, cells_z), BF16),
-            pltpu.VMEM((kept, comps, 2, snaps, cells_z), BF16),
-            pltpu.VMEM((kept, comps, 2, snaps, cells_z), BF16),
-            pltpu.VMEM((5, comps, cells_y, snaps, cells_z), F32),
-            pltpu.VMEM((3, comps, cells_y, snaps, cells_z), F32),
-            pltpu.VMEM((kept, snaps, lanes), BF16),
-            DMA((3, steps, 3)),
-            DMA((kept,)),
-        ],
-        compiler_params=PARAMS,
-    )(*metrics, *sources, low, high)
+            pltpu.VMEM(parts.shape, F32),
+            pltpu.VMEM((2, comps, 2, cells_y, snaps, cells_z), BF16),
+            pltpu.VMEM(parts.shape, BF16),
+            DMA((4,)),
+            DMA((2, 2)),
+            DMA((4,)),
+        ],
+        compiler_params=limit(20),
+    )(near, far1, far2, parts, metric_x, gram)
 
 
 def factorize(rows, panel):
@@ -412,12 +508,13 @@
     n = len(rest) - 7
     sources, (out, lower_ref, held, made, rows, in_sems, out_sems) = rest[:n], rest[n:]
     snaps, comps, _, cells_y, cells_z = out.shape
+    width = cells_y * cells_z
 
     def reads(x):
         copies, lane = [], 0
-        for m, (source, layer, ys) in enumerate(places[x]):
-            lanes = pl.ds(lane, comps * len(ys) * cells_z)
-            lane += comps * len(ys) * cells_z
+        for m, (source, layer, count) in enumerate(places[x]):
+            lanes = pl.ds(lane, count * width)
+            lane += count * width
             copies.append(
                 pltpu.make_async_copy(
                     sources[source].at[layer], held.at[x, :, lanes], in_sems.at[x, m]
@@ -446,16 +543,12 @@
         for copy in reads(x):
             copy.wait()
         for f in range(comps):
-            lane = 0
-            for _, _, ys in places[x]:
-                width = len(ys) * cells_z
-                at = lane + f * width
-                lane += comps * width
-                whole = jnp.dot(inverse, held[x, :, at : at + width], preferred_element_type=F32)
-                for k, y in enumerate(ys):
-                    rows[f % 2, pl.ds(y, snaps, stride=PITCH), :] = whole[
-                        :, k * cells_z : (k + 1) * cells_z
-                    ]
+            lanes = slice(f * width, (f + 1) * width)
+            whole = jnp.dot(inverse, held[x, :, lanes], preferred_element_type=F32)
+            for y in range(cells_y):
+                rows[f % 2, pl.ds(y, snaps, stride=PITCH), :] = whole[
+                    :, y * cells_z : (y + 1) * cells_z
+                ]
             for s in range(snaps):
                 made[x, s, f] = rows[f % 2, pl.ds(s * PITCH, cells_y), :].astype(BF16)
         writes.append(pltpu.make_async_copy(made.at[x], out.at[:, :, x], out_sems.at[x]))
@@ -482,7 +575,7 @@
             DMA((cells_x, 2)),
             DMA((cells_x,)),
         ],
-        compiler_params=PARAMS,
+        compiler_params=limit(32),
     )(gram, more, *sources)
 
 
@@ -535,51 +628,18 @@
     for step, weight in ((1, 8.0), (-1, -8.0), (2, -1.0), (-2, 1.0)):
         taps = taps + weight * jnp.eye(cells_z, k=-step, dtype=F32)
     metrics = (metric_x / 12.0, metric_y / 12.0, metric_z[None, :] / 12.0, taps.astype(BF16))
-    whole, half = slice(0, cells_y), cells_y // 2
-
-    def local(layer):
-        return lambda refs: [(refs[0].at[:, layer], whole, None)]
-
-    def halo(layer, of_near):
-        def read(refs):
-            odd = lax.rem(lax.axis_index("stream"), 2)
-            is_near = (odd == 1) == of_near
-            is_far = jnp.logical_not(is_near)
-            return [
-                (refs[1].at[:, layer], whole, is_near),
-                (refs[2].at[:, layer], slice(0, half), is_far),
-                (refs[3].at[:, layer], slice(half, cells_y), is_far),
-            ]
-
-        return read
-
-    rows = tuple(range(cells_y))
-    rows_in, rows_out = rows[2:-2], rows[:2] + rows[-2:]
-    walk = ([local(i) for i in range(cells_x)], [None] * 4 + list(range(2, cells_x - 2)))
-    middle, middle_gram = fields([cells], *walk, rows_in, first, last, metrics)
-    sides, sides_gram = fields([cells], *walk, rows_out, low, high, metrics)
-    outer, outer_gram = fields(
-        [cells, near, far1, far2],
-        [halo(0, True), halo(1, True)]
-        + [local(i) for i in (*range(4), *range(cells_x - 4, cells_x))]
-        + [halo(0, False), halo(1, False)],
-        [None] * 4 + [0, 1] + [None] * 4 + [cells_x - 2, cells_x - 1],
-        rows,
-        low,
-        high,
-        metrics,
-    )
+    middle, ends, parts, gram = inner_fields(cells, low, high, metrics)
+    outer, gram = outer_fields(metrics[0], gram, parts, near, far1, far2)
     everywhere = (
         4.0 * cells_x * lax.axis_size("stream") * cells_y * lax.axis_size("cross") * cells_z
     )
-    gram, more = total(middle_gram + sides_gram + outer_gram)
+    gram, more = total(gram)
+    end = lambda x: x if x < 2 else x - cells_x + 4
     places = [
-        [(2, x if x < 2 else x - cells_x + 4, rows)]
-        if x < 2 or x >= cells_x - 2
-        else [(0, x - 2, rows_in), (1, x - 2, rows_out)]
+        [(0, x - 2, 4)] if 2 <= x < cells_x - 2 else [(1, end(x), 1), (2, end(x), 3)]
         for x in range(cells_x)
     ]
-    sources = [middle, sides, outer]
+    sources = [middle, ends, outer]
     return tuple(modes(gram, more, 1.0 / everywhere, sources, places, cells_y, cells_z))
 
 

time: 126 us -> 111 us (0.88)
  Pallas kernels: 73.8 us -> 61.1 us
  local copies, waits for them, and re-layouts: 5.68 us -> 0.01 us
  starting transfers between devices: 22 us -> 27.3 us
  other arithmetic: 3.28 us -> 0.19 us
  waiting for transfers between devices: 19.7 us -> 21.6 us
    pallas_call x3 -> x2, Pallas kernels: 42 us -> 31.4 us  [the longest x1 25.8 us: inner_fields(): pl.pallas_call(inner_kernel, in_specs=[SMEM, SMEM, VMEM, VMEM] + [HBM] *...]
    ppermute x1, waiting for transfers between devices: 0.01 us -> 6.95 us  [far_exchange(): lax.ppermute(cells, 'stream', [(3, 2), (0, 1)])]
    ppermute x5, starting transfers between devices: 4.96 us -> 11.4 us  [total(): more = lax.ppermute(local, axis, [(i, i ^ step) for i in range(count)])]
    unnamed x24 -> x8, local copies, waits for them, and re-layouts: 5.68 us -> 0.01 us
    ppermute x5, waiting for transfers between devices: 14.6 us -> 10.6 us  [total(): more = lax.ppermute(local, axis, [(i, i ^ step) for i in range(count)])]
    pallas_call x1, Pallas kernels: 15.6 us -> 13.5 us  [modes(): pl.pallas_call(functools.partial(modes_kernel, places, scale), in_specs=[...]
  transfers between devices with their start and end apart: 11 -> 11, of which waited for: 6 -> 7; matrix products, arithmetic and copies ran while one was open for 2% -> 0% of each run, Pallas kernels for 29% -> 30%
where the time goes in v4:
time: 111 us
  Pallas kernels  61.1 us (55%)
  starting transfers between devices  27.3 us (25%)
  waiting for transfers between devices  21.6 us (19%)
    pallas_call x1, Pallas kernels, inner_fields(): pl.pallas_call(inner_kernel, in_specs=[SMEM, SMEM, VMEM, VMEM] + [HBM] *...  25.8 us
    pallas_call x1, Pallas kernels, modes(): pl.pallas_call(functools.partial(modes_kernel, places, scale), in_specs=[...  13.5 us
    ppermute x5, starting transfers between devices, total(): more = lax.ppermute(local, axis, [(i, i ^ step) for i in range(count)])  11.4 us
    ppermute x5, waiting for transfers between devices, total(): more = lax.ppermute(local, axis, [(i, i ^ step) for i in range(count)])  10.6 us
    pallas_call x1, Pallas kernels, edges(): pl.pallas_call(edges_kernel, in_specs=[HBM], out_specs=[HBM] * 5, out_sha...  8.11 us
    pallas_call x1, Pallas kernels, planes(): pl.pallas_call(planes_kernel, in_specs=[HBM], out_specs=HBM, out_shape=ja...  8.04 us
    ppermute x1, waiting for transfers between devices, far_exchange(): lax.ppermute(cells, 'stream', [(3, 2), (0, 1)])  6.95 us
    pallas_call x1, Pallas kernels, outer_fields(): pl.pallas_call(outer_kernel, in_specs=[HBM] * 4 + [SMEM, VMEM], out_specs...  5.67 us
  transfers between devices with their start and end apart: 11, of which 7 were waited for; matrix products, arithmetic and copies ran while one was open for 0% of the time, Pallas kernels for 30%

profile of v4, /device:TPU:0, one launch (start us, length us, event | category | flops | bytes accessed | tf_op | source)
XLA Modules:
  0.0 111.2 jit_solution(6326803064750575782)
XLA Ops:
  0.6 8.1 %shard_map.59 = (bf16[3,2,8,128,128]{4,3,2,1,0:T(8,128)(2,1)}, bf16[3,2,4,128,128]{4,3,2,1,0:T(8,128)(2,1)}, bf16[3,2,4,128,128]{4,3,2,1,0:T(8,128)(2,1)}, bf16[...) custom-call(bf16[128,3,12,8,128]{4,3,2,1,0:T(8,128)(2,1)} %velocity.2), custom_call_target="tpu_custom_call" | custom-call | tf_op jit(solution)/shard_map/pallas_call | solution.py:128
  8.7 2.5 %collective-permute-start.4 = (bf16[3,12,2,128,128]{4,3,2,1,0:T(8,128)(2,1)}, bf16[3,12,2,128,128]{4,3,2,1,0:T(8,128)(2,1)S(1)}, u32[]{:S(2)}, u32[]{:S(2)}) collective-permute-start(bf16[3,12,2,128,128]{4,3,2,1,0:T(8,128)(2,1)} %get-tuple-element.22), channel_id=1, source_target_pairs={{0,1},{1,2},{2,3},{3,4},{4,5},{5,6},{6,7},{8,9},{9,10},{10,11},{11... | collective-permute-start | bytes 7077896 | tf_op jit(solution)/shard_map/ppermute | solution.py:597
  11.3 1.3 %collective-permute-start.5 = (bf16[3,12,2,128,128]{4,3,2,1,0:T(8,128)(2,1)}, bf16[3,12,2,128,128]{4,3,2,1,0:T(8,128)(2,1)}, u32[]{:S(2)}, u32[]{:S(2)}) collective-permute-start(bf16[3,12,2,128,128]{4,3,2,1,0:T(8,128)(2,1)} %get-tuple-element.23), channel_id=1, source_target_pairs={{1,0},{2,1},{3,2},{4,3},{5,4},{6,5},{7,6},{9,8},{10,9},{11,10},{12... | collective-permute-start | bytes 7077896 | tf_op jit(solution)/shard_map/ppermute | solution.py:597
  12.6 1.3 %collective-permute-start.2 = (bf16[3,2,4,128,128]{4,3,2,1,0:T(8,128)(2,1)}, bf16[3,2,4,128,128]{4,3,2,1,0:T(8,128)(2,1)}, u32[]{:S(2)}, u32[]{:S(2)}) collective-permute-start(bf16[3,2,4,128,128]{4,3,2,1,0:T(8,128)(2,1)} %get-tuple-element.18), channel_id=1, source_target_pairs={{8,24},{16,0},{9,25},{17,1},{10,26},{18,2},{11,27},{19,3},{12,28},... | collective-permute-start | bytes 2359304 | tf_op jit(solution)/shard_map/ppermute | solution.py:608
  13.9 5.2 %collective-permute-start = (bf16[3,2,8,128,128]{4,3,2,1,0:T(8,128)(2,1)}, bf16[3,2,8,128,128]{4,3,2,1,0:T(8,128)(2,1)S(1)}, u32[]{:S(2)}, u32[]{:S(2)}) collective-permute-start(bf16[3,2,8,128,128]{4,3,2,1,0:T(8,128)(2,1)} %get-tuple-element.16), channel_id=1, source_target_pairs={{0,8},{8,0},{16,24},{24,16},{1,9},{9,1},{17,25},{25,17},{2,10},{10... | collective-permute-start | bytes 4718600 | tf_op jit(solution)/shard_map/ppermute | solution.py:619
  19.1 1.7 %collective-permute-start.1 = (bf16[3,2,4,128,128]{4,3,2,1,0:T(8,128)(2,1)}, bf16[3,2,4,128,128]{4,3,2,1,0:T(8,128)(2,1)}, u32[]{:S(2)}, u32[]{:S(2)}) collective-permute-start(bf16[3,2,4,128,128]{4,3,2,1,0:T(8,128)(2,1)} %get-tuple-element.17), channel_id=1, source_target_pairs={{8,16},{16,8},{9,17},{17,9},{10,18},{18,10},{11,19},{19,11},{12,20... | collective-permute-start | bytes 2359304 | tf_op jit(solution)/shard_map/ppermute | solution.py:620
  20.7 8.0 %shard_map.60.cells = bf16[3,12,8,128,128]{4,3,2,1,0:T(8,128)(2,1)} custom-call(bf16[128,3,12,8,128]{4,3,2,1,0:T(8,128)(2,1)} %velocity.2), custom_call_target="tpu_custom_call" | custom-call | tf_op jit(solution)/shard_map/pallas_call | solution.py:180
  28.8 0.0 copy-done.1
  28.8 4.1 %collective-permute-done.2 = bf16[3,2,4,128,128]{4,3,2,1,0:T(8,128)(2,1)} collective-permute-done((bf16[3,2,4,128,128]{4,3,2,1,0:T(8,128)(2,1)}, bf16[3,2,4,128,128]{4,3,2,1,0:T(8,128)(2,1)}, u32[]{:S(2)}, u32[]{:S(2)}) %collective-permute-start.2) | collective-permute-done | bytes 786464 | tf_op jit(solution)/shard_map/ppermute | solution.py:608
  32.9 4.0 %collective-permute-start.3 = (bf16[3,2,4,128,128]{4,3,2,1,0:T(8,128)(2,1)}, bf16[3,2,4,128,128]{4,3,2,1,0:T(8,128)(2,1)S(1)}, u32[]{:S(2)}, u32[]{:S(2)}) collective-permute-start(bf16[3,2,4,128,128]{4,3,2,1,0:T(8,128)(2,1)} %collective-permute-done.2), channel_id=1, source_target_pairs={{24,16},{0,8},{25,17},{1,9},{26,18},{2,10},{27,19},{3,11},{28,20},... | collective-permute-start | bytes 2359304 | tf_op jit(solution)/shard_map/ppermute | solution.py:609
  37.0 0.0 copy-done.2
  37.0 0.0 copy-done.3
  37.0 0.1 add_convert_fusion.taps_ref
  37.1 0.0 collective-permute-done.4.low
  37.1 0.0 collective-permute-done.5.high
  37.2 25.8 %shard_map.61 = (bf16[8,128,4096]{2,1,0:T(8,128)(2,1)}, bf16[4,128,1024]{2,1,0:T(8,128)(2,1)S(1)}, f32[4,128,3072]{2,1,0:T(8,128)S(1)}, f32[128,128]{1,0:T(8,128)S(1)}) custom-call(f32[12]{0:T(128)S(1)} %broadcast_multiply_fusion.1.mx_ref, f32[8]{0:T(128)S(1)} %broadcast_multiply_fusion.my_ref, f32[1,128]{1,0:T(1,128)S(1)} %multiply_bitcast_fusion.mz_ref, ...), custom_call_target="tpu_custom_call" | custom-call | tf_op jit(solution)/shard_map/pallas_call | solution.py:325
  62.9 0.0 collective-permute-done.1.far1
  62.9 0.0 collective-permute-done.near
  63.0 7.0 %collective-permute-done.3.far2 = bf16[3,2,4,128,128]{4,3,2,1,0:T(8,128)(2,1)S(1)} collective-permute-done((bf16[3,2,4,128,128]{4,3,2,1,0:T(8,128)(2,1)}, bf16[3,2,4,128,128]{4,3,2,1,0:T(8,128)(2,1)S(1)}, u32[]{:S(2)}, u32[]{:S(2)}) %collective-permute-start.3) | collective-permute-done | bytes 786464 | tf_op jit(solution)/shard_map/ppermute | solution.py:609
  69.9 5.7 %shard_map.62 = (bf16[4,128,3072]{2,1,0:T(8,128)(2,1)S(1)}, f32[128,128]{1,0:T(8,128)S(1)}) custom-call(bf16[3,2,8,128,128]{4,3,2,1,0:T(8,128)(2,1)S(1)} %collective-permute-done.near, bf16[3,2,4,128,128]{4,3,2,1,0:T(8,128)(2,1)} %collective-permute-done.1.far1, bf16[3,2,4,128,128]{4,3,2,1,0:T(8,128)(2,1)S(1)} %collective-permute-done.3.far2, ...), custom_call_target="tpu_custom_call" | custom-call | tf_op jit(solution)/shard_map/pallas_call | solution.py:423
  75.6 1.3 %collective-permute-start.6 = (f32[128,128]{1,0:T(8,128)S(1)}, f32[128,128]{1,0:T(8,128)S(1)}, u32[]{:S(2)}, u32[]{:S(2)}) collective-permute-start(f32[128,128]{1,0:T(8,128)S(1)} %get-tuple-element.26), channel_id=1, source_target_pairs={{0,1},{1,0},{2,3},{3,2},{4,5},{5,4},{6,7},{7,6},{8,9},{9,8},{10,11... | collective-permute-start | bytes 196616 | tf_op jit(solution)/shard_map/ppermute | solution.py:590
  76.9 0.9 collective-permute-done.6
  77.8 3.0 %collective-permute-start.7 = (f32[128,128]{1,0:T(8,128)S(1)}, f32[128,128]{1,0:T(8,128)S(1)}, u32[]{:S(2)}, u32[]{:S(2)}) collective-permute-start(f32[128,128]{1,0:T(8,128)S(1)} %add.60), channel_id=1, source_target_pairs={{0,2},{1,3},{2,0},{3,1},{4,6},{5,7},{6,4},{7,5},{8,10},{9,11},{10,... | collective-permute-start | bytes 196616 | tf_op jit(solution)/shard_map/ppermute | solution.py:590
  80.8 2.4 %collective-permute-done.7 = f32[128,128]{1,0:T(8,128)S(1)} collective-permute-done((f32[128,128]{1,0:T(8,128)S(1)}, f32[128,128]{1,0:T(8,128)S(1)}, u32[]{:S(2)}, u32[]{:S(2)}) %collective-permute-start.7) | collective-permute-done | bytes 65568 | tf_op jit(solution)/shard_map/ppermute | solution.py:590
  83.2 2.9 %collective-permute-start.8 = (f32[128,128]{1,0:T(8,128)S(1)}, f32[128,128]{1,0:T(8,128)S(1)}, u32[]{:S(2)}, u32[]{:S(2)}) collective-permute-start(f32[128,128]{1,0:T(8,128)S(1)} %add.61), channel_id=1, source_target_pairs={{0,4},{1,5},{2,6},{3,7},{4,0},{5,1},{6,2},{7,3},{8,12},{9,13},{10,... | collective-permute-start | bytes 196616 | tf_op jit(solution)/shard_map/ppermute | solution.py:590
  86.1 2.6 %collective-permute-done.8 = f32[128,128]{1,0:T(8,128)S(1)} collective-permute-done((f32[128,128]{1,0:T(8,128)S(1)}, f32[128,128]{1,0:T(8,128)S(1)}, u32[]{:S(2)}, u32[]{:S(2)}) %collective-permute-start.8) | collective-permute-done | bytes 65568 | tf_op jit(solution)/shard_map/ppermute | solution.py:590
  88.7 1.9 %collective-permute-start.9 = (f32[128,128]{1,0:T(8,128)S(1)}, f32[128,128]{1,0:T(8,128)S(1)}, u32[]{:S(2)}, u32[]{:S(2)}) collective-permute-start(f32[128,128]{1,0:T(8,128)S(1)} %add.62), channel_id=1, source_target_pairs={{0,8},{8,0},{16,24},{24,16},{1,9},{9,1},{17,25},{25,17},{2,10},{10... | collective-permute-start | bytes 196616 | tf_op jit(solution)/shard_map/ppermute | solution.py:590
  90.6 2.4 %collective-permute-done.9 = f32[128,128]{1,0:T(8,128)S(1)} collective-permute-done((f32[128,128]{1,0:T(8,128)S(1)}, f32[128,128]{1,0:T(8,128)S(1)}, u32[]{:S(2)}, u32[]{:S(2)}) %collective-permute-start.9) | collective-permute-done | bytes 65568 | tf_op jit(solution)/shard_map/ppermute | solution.py:590
  93.0 2.3 %collective-permute-start.10 = (f32[128,128]{1,0:T(8,128)S(1)}, f32[128,128]{1,0:T(8,128)S(1)}, u32[]{:S(2)}, u32[]{:S(2)}) collective-permute-start(f32[128,128]{1,0:T(8,128)S(1)} %add.63.gram_ref), channel_id=1, source_target_pairs={{0,16},{8,24},{16,0},{24,8},{1,17},{9,25},{17,1},{25,9},{2,18},{10... | collective-permute-start | bytes 196616 | tf_op jit(solution)/shard_map/ppermute | solution.py:590
  95.3 2.2 %collective-permute-done.10.more_ref = f32[128,128]{1,0:T(8,128)S(1)} collective-permute-done((f32[128,128]{1,0:T(8,128)S(1)}, f32[128,128]{1,0:T(8,128)S(1)}, u32[]{:S(2)}, u32[]{:S(2)}) %collective-permute-start.10) | collective-permute-done | bytes 65568 | tf_op jit(solution)/shard_map/ppermute | solution.py:590
  97.6 0.0 copy-done
  97.6 13.5 %shard_map.63 = (bf16[128,4,12,8,128]{4,3,2,1,0:T(8,128)(2,1)}, f32[128,128]{1,0:T(8,128)}) custom-call(f32[128,128]{1,0:T(8,128)S(1)} %add.63.gram_ref, f32[128,128]{1,0:T(8,128)S(1)} %collective-permute-done.10.more_ref, bf16[8,128,4096]{2,1,0:T(8,128)(2,1)S(1)} %copy-done, bf16[4,128,1024]{2,1,0:T(8,128)(2,1)S(1)} %get-tuple-element.28.rest_1_, ...), custom_call_target="tpu_custom_call" | custom-call | tf_op jit(solution)/shard_map/pallas_call | solution.py:563
  (13 shorter events, 0.1 us)
Async XLA Ops:
  8.7 28.4 %collective-permute-start.4 = (bf16[3,12,2,128,128]{4,3,2,1,0:T(8,128)(2,1)}, bf16[3,12,2,128,128]{4,3,2,1,0:T(8,128)(2,1)S(1)}, u32[]{:S(2)}, u32[]{:S(2)}) collective-permute-start(bf16[3,12,2,128,128]{4,3,2,1,0:T(8,128)(2,1)} %get-tuple-element.22), channel_id=1, source_target_pairs={{0,1},{1,2},{2,3},{3,4},{4,5},{5,6},{6,7},{8,9},{9,10},{10,11},{11... | collective-permute-start | bytes 7077896 | tf_op jit(solution)/shard_map/ppermute | solution.py:597
  11.3 25.9 %collective-permute-start.5 = (bf16[3,12,2,128,128]{4,3,2,1,0:T(8,128)(2,1)}, bf16[3,12,2,128,128]{4,3,2,1,0:T(8,128)(2,1)}, u32[]{:S(2)}, u32[]{:S(2)}) collective-permute-start(bf16[3,12,2,128,128]{4,3,2,1,0:T(8,128)(2,1)} %get-tuple-element.23), channel_id=1, source_target_pairs={{1,0},{2,1},{3,2},{4,3},{5,4},{6,5},{7,6},{9,8},{10,9},{11,10},{12... | collective-permute-start | bytes 7077896 | tf_op jit(solution)/shard_map/ppermute | solution.py:597
  12.6 20.4 %collective-permute-start.2 = (bf16[3,2,4,128,128]{4,3,2,1,0:T(8,128)(2,1)}, bf16[3,2,4,128,128]{4,3,2,1,0:T(8,128)(2,1)}, u32[]{:S(2)}, u32[]{:S(2)}) collective-permute-start(bf16[3,2,4,128,128]{4,3,2,1,0:T(8,128)(2,1)} %get-tuple-element.18), channel_id=1, source_target_pairs={{8,24},{16,0},{9,25},{17,1},{10,26},{18,2},{11,27},{19,3},{12,28},... | collective-permute-start | bytes 2359304 | tf_op jit(solution)/shard_map/ppermute | solution.py:608
  13.9 49.1 %collective-permute-start = (bf16[3,2,8,128,128]{4,3,2,1,0:T(8,128)(2,1)}, bf16[3,2,8,128,128]{4,3,2,1,0:T(8,128)(2,1)S(1)}, u32[]{:S(2)}, u32[]{:S(2)}) collective-permute-start(bf16[3,2,8,128,128]{4,3,2,1,0:T(8,128)(2,1)} %get-tuple-element.16), channel_id=1, source_target_pairs={{0,8},{8,0},{16,24},{24,16},{1,9},{9,1},{17,25},{25,17},{2,10},{10... | collective-permute-start | bytes 4718600 | tf_op jit(solution)/shard_map/ppermute | solution.py:619
  19.1 9.7 %copy-start.1 = (f32[12]{0:T(128)S(1)}, f32[12]{0:T(128)}, u32[]{:S(2)}) copy-start(f32[12]{0:T(128)} %param.5) | copy-start | bytes 148
  19.1 17.9 %copy-start.2 = (f32[8]{0:T(128)S(1)}, f32[8]{0:T(128)}, u32[]{:S(2)}) copy-start(f32[8]{0:T(128)} %param.6) | copy-start | bytes 100
  19.1 17.9 %copy-start.3 = (f32[128]{0:T(128)S(1)}, f32[128]{0:T(128)}, u32[]{:S(2)}) copy-start(f32[128]{0:T(128)} %param.7) | copy-start | bytes 1540
  19.1 43.9 %collective-permute-start.1 = (bf16[3,2,4,128,128]{4,3,2,1,0:T(8,128)(2,1)}, bf16[3,2,4,128,128]{4,3,2,1,0:T(8,128)(2,1)}, u32[]{:S(2)}, u32[]{:S(2)}) collective-permute-start(bf16[3,2,4,128,128]{4,3,2,1,0:T(8,128)(2,1)} %get-tuple-element.17), channel_id=1, source_target_pairs={{8,16},{16,8},{9,17},{17,9},{10,18},{18,10},{11,19},{19,11},{12,20... | collective-permute-start | bytes 2359304 | tf_op jit(solution)/shard_map/ppermute | solution.py:620
  32.9 37.0 %collective-permute-start.3 = (bf16[3,2,4,128,128]{4,3,2,1,0:T(8,128)(2,1)}, bf16[3,2,4,128,128]{4,3,2,1,0:T(8,128)(2,1)S(1)}, u32[]{:S(2)}, u32[]{:S(2)}) collective-permute-start(bf16[3,2,4,128,128]{4,3,2,1,0:T(8,128)(2,1)} %collective-permute-done.2), channel_id=1, source_target_pairs={{24,16},{0,8},{25,17},{1,9},{26,18},{2,10},{27,19},{3,11},{28,20},... | collective-permute-start | bytes 2359304 | tf_op jit(solution)/shard_map/ppermute | solution.py:609
  69.9 27.7 %copy-start = (bf16[8,128,4096]{2,1,0:T(8,128)(2,1)S(1)}, bf16[8,128,4096]{2,1,0:T(8,128)(2,1)}, u32[]{:S(2)}) copy-start(bf16[8,128,4096]{2,1,0:T(8,128)(2,1)} %get-tuple-element.27.rest_0_) | copy-start | bytes 25165828
  75.6 2.2 %collective-permute-start.6 = (f32[128,128]{1,0:T(8,128)S(1)}, f32[128,128]{1,0:T(8,128)S(1)}, u32[]{:S(2)}, u32[]{:S(2)}) collective-permute-start(f32[128,128]{1,0:T(8,128)S(1)} %get-tuple-element.26), channel_id=1, source_target_pairs={{0,1},{1,0},{2,3},{3,2},{4,5},{5,4},{6,7},{7,6},{8,9},{9,8},{10,11... | collective-permute-start | bytes 196616 | tf_op jit(solution)/shard_map/ppermute | solution.py:590
  77.8 5.4 %collective-permute-start.7 = (f32[128,128]{1,0:T(8,128)S(1)}, f32[128,128]{1,0:T(8,128)S(1)}, u32[]{:S(2)}, u32[]{:S(2)}) collective-permute-start(f32[128,128]{1,0:T(8,128)S(1)} %add.60), channel_id=1, source_target_pairs={{0,2},{1,3},{2,0},{3,1},{4,6},{5,7},{6,4},{7,5},{8,10},{9,11},{10,... | collective-permute-start | bytes 196616 | tf_op jit(solution)/shard_map/ppermute | solution.py:590
  83.2 5.5 %collective-permute-start.8 = (f32[128,128]{1,0:T(8,128)S(1)}, f32[128,128]{1,0:T(8,128)S(1)}, u32[]{:S(2)}, u32[]{:S(2)}) collective-permute-start(f32[128,128]{1,0:T(8,128)S(1)} %add.61), channel_id=1, source_target_pairs={{0,4},{1,5},{2,6},{3,7},{4,0},{5,1},{6,2},{7,3},{8,12},{9,13},{10,... | collective-permute-start | bytes 196616 | tf_op jit(solution)/shard_map/ppermute | solution.py:590
  88.7 4.3 %collective-permute-start.9 = (f32[128,128]{1,0:T(8,128)S(1)}, f32[128,128]{1,0:T(8,128)S(1)}, u32[]{:S(2)}, u32[]{:S(2)}) collective-permute-start(f32[128,128]{1,0:T(8,128)S(1)} %add.62), channel_id=1, source_target_pairs={{0,8},{8,0},{16,24},{24,16},{1,9},{9,1},{17,25},{25,17},{2,10},{10... | collective-permute-start | bytes 196616 | tf_op jit(solution)/shard_map/ppermute | solution.py:590
  93.0 4.5 %collective-permute-start.10 = (f32[128,128]{1,0:T(8,128)S(1)}, f32[128,128]{1,0:T(8,128)S(1)}, u32[]{:S(2)}, u32[]{:S(2)}) collective-permute-start(f32[128,128]{1,0:T(8,128)S(1)} %add.63.gram_ref), channel_id=1, source_target_pairs={{0,16},{8,24},{16,0},{24,8},{1,17},{9,25},{17,1},{25,9},{2,18},{10... | collective-permute-start | bytes 196616 | tf_op jit(solution)/shard_map/ppermute | solution.py:590

commit v5 on v4

--- a/solution.py
+++ b/solution.py
@@ -232,7 +232,7 @@
                 window[c] = window[c][1:]
         return 0
 
-    lax.fori_loop(0, snaps // ROWS, some_rows, 0)
+    lax.fori_loop(0, snaps // ROWS, some_rows, 0, unroll=2)
 
 
 def inner_kernel(mx_ref, my_ref, mz_ref, taps_ref, cells, low, high, *rest):
@@ -348,6 +348,31 @@
     )(*metrics, cells, low, high)
 
 
+def triangle(whole):
+    n = whole.shape[0]
+    half = n // 2
+    r = lax.broadcasted_iota(jnp.int32, (half, n), 0)
+    c = lax.broadcasted_iota(jnp.int32, (half, n), 1)
+    top, bottom = whole[:half], whole[half:]
+    packed = jnp.where(c - half <= r, bottom, pltpu.roll(top, half, 1))
+    diagonal = jnp.sum(jnp.where(r == c, top, 0.0), axis=0, keepdims=True)
+    return packed, jnp.broadcast_to(diagonal, (8, n))
+
+
+def symmetric(packed):
+    n = packed.shape[1]
+    half = n // 2
+    r = lax.broadcasted_iota(jnp.int32, (half, n), 0)
+    c = lax.broadcasted_iota(jnp.int32, (half, n), 1)
+    rows, diagonal = packed[:half], packed[half : half + 1]
+    top = jnp.where((c > r) & (c < half), pltpu.roll(rows, half, 1), 0.0)
+    top = jnp.where(r == c, jnp.broadcast_to(diagonal, (half, n)), top)
+    one = jnp.concatenate([top, jnp.where(c - half <= r, rows, 0.0)], axis=0)
+    r = lax.broadcasted_iota(jnp.int32, (n, n), 0)
+    c = lax.broadcasted_iota(jnp.int32, (n, n), 1)
+    return jnp.where(r == c, one, one + one.T)
+
+
 def outer_kernel(near, far1, far2, parts, mx_ref, gram_ref, out, total_ref, *rest):
     taken, halos, done, part_sems, halo_sems, out_sems = rest
     _, comps, _, cells_y, snaps, cells_z = halos.shape
@@ -412,7 +437,8 @@
         total += lax.dot_general(
             done[e], done[e], (((1,), (1,)), ((), ())), preferred_element_type=F32
         )
-    total_ref[...] = total
+    half = snaps // 2
+    total_ref[:half], total_ref[half:] = triangle(total)
     for w in writes:
         w.wait()
 
@@ -426,7 +452,7 @@
         out_specs=[HBM, VMEM],
         out_shape=[
             jax.ShapeDtypeStruct(parts.shape, BF16),
-            jax.ShapeDtypeStruct((snaps, snaps), F32),
+            jax.ShapeDtypeStruct((snaps // 2 + 8, snaps), F32),
         ],
         scratch_shapes=[
             pltpu.VMEM(parts.shape, F32),
@@ -504,7 +530,8 @@
     return jnp.concatenate(uppers, axis=0), jnp.concatenate(inverses, axis=0)
 
 
-def modes_kernel(places, scale, gram_ref, more_ref, *rest):
+def modes_kernel(places, scale, n_terms, *rest):
+    terms, rest = rest[:n_terms], rest[n_terms:]
     n = len(rest) - 7
     sources, (out, lower_ref, held, made, rows, in_sems, out_sems) = rest[:n], rest[n:]
     snaps, comps, _, cells_y, cells_z = out.shape
@@ -526,13 +553,8 @@
         for copy in reads(x):
             copy.start()
 
-    upper, inverse = factorize(
-        [
-            (gram_ref[r : r + 8, :] + more_ref[r : r + 8, :]) * scale
-            for r in range(0, snaps, 8)
-        ],
-        4,
-    )
+    gram = symmetric(tree_sum([term[...] for term in terms]) * scale)
+    upper, inverse = factorize([gram[r : r + 8] for r in range(0, snaps, 8)], 4)
     r = lax.broadcasted_iota(jnp.int32, (snaps, snaps), 0)
     c = lax.broadcasted_iota(jnp.int32, (snaps, snaps), 1)
     lower_ref[...] = jnp.where(r >= c, upper.T, 0.0)
@@ -557,12 +579,12 @@
         w.wait()
 
 
-def modes(gram, more, scale, sources, places, cells_y, cells_z):
-    snaps = gram.shape[0]
+def modes(terms, scale, sources, places, cells_y, cells_z):
+    snaps = terms[0].shape[1]
     cells_x = len(places)
     return pl.pallas_call(
-        functools.partial(modes_kernel, places, scale),
-        in_specs=[VMEM, VMEM] + [HBM] * len(sources),
+        functools.partial(modes_kernel, places, scale, len(terms)),
+        in_specs=[VMEM] * len(terms) + [HBM] * len(sources),
         out_specs=[HBM, VMEM],
         out_shape=[
             jax.ShapeDtypeStruct((snaps, 4, cells_x, cells_y, cells_z), BF16),
@@ -576,19 +598,31 @@
             DMA((cells_x,)),
         ],
         compiler_params=limit(32),
-    )(gram, more, *sources)
-
-
-def total(local):
-    steps = []
+    )(*terms, *sources)
+
+
+def tree_sum(terms):
+    while len(terms) > 1:
+        terms = [terms[i] + terms[i + 1] for i in range(0, len(terms), 2)]
+    return terms[0]
+
+
+def exchange(local):
+    groups = []
     for axis in ("cross", "stream"):
         count = lax.axis_size(axis)
-        steps += [(axis, count, 1 << k) for k in range((count - 1).bit_length())]
-    more = jnp.zeros_like(local)
-    for axis, count, step in steps:
-        local = local + more
-        more = lax.ppermute(local, axis, [(i, i ^ step) for i in range(count)])
-    return local, more
+        bits = [1 << k for k in range((count - 1).bit_length())]
+        if axis == "cross":
+            groups, bits = groups + [(axis, count, bits[:1])], bits[1:]
+        groups += [(axis, count, bits[k : k + 2]) for k in range(0, len(bits), 2)]
+    terms = [local]
+    for axis, count, bits in groups:
+        local = tree_sum(terms)
+        steps = [sum(b for k, b in enumerate(bits) if n >> k & 1) for n in range(1 << len(bits))]
+        terms = [local] + [
+            lax.ppermute(local, axis, [(i, i ^ step) for i in range(count)]) for step in steps[1:]
+        ]
+    return terms
 
 
 def shift(cells, axis, way):
@@ -633,14 +667,14 @@
     everywhere = (
         4.0 * cells_x * lax.axis_size("stream") * cells_y * lax.axis_size("cross") * cells_z
     )
-    gram, more = total(gram)
+    terms = exchange(gram)
     end = lambda x: x if x < 2 else x - cells_x + 4
     places = [
         [(0, x - 2, 4)] if 2 <= x < cells_x - 2 else [(1, end(x), 1), (2, end(x), 3)]
         for x in range(cells_x)
     ]
     sources = [middle, ends, outer]
-    return tuple(modes(gram, more, 1.0 / everywhere, sources, places, cells_y, cells_z))
+    return tuple(modes(terms, 1.0 / everywhere, sources, places, cells_y, cells_z))
 
 
 def solution(mesh):

time: 111 us -> 109 us (0.982)
  waiting for transfers between devices: 21.6 us -> 20 us
    ppermute x5 -> x7, waiting for transfers between devices: 10.6 us -> 8.64 us  [exchange(): lax.ppermute(local, axis, [(i, i ^ step) for i in range(count)])]
    ppermute x5 -> x7, starting transfers between devices: 11.4 us -> 10.9 us  [exchange(): lax.ppermute(local, axis, [(i, i ^ step) for i in range(count)])]
  transfers between devices with their start and end apart: 11 -> 13, of which waited for: 7 -> 8; matrix products, arithmetic and copies ran while one was open for 0% -> 0% of each run, Pallas kernels for 30% -> 31%
where the time goes in v5:
time: 109 us
  Pallas kernels  61.1 us (56%)
  starting transfers between devices  26.9 us (25%)
  waiting for transfers between devices  20 us (18%)
    pallas_call x1, Pallas kernels, inner_fields(): pl.pallas_call(inner_kernel, in_specs=[SMEM, SMEM, VMEM, VMEM] + [HBM] *...  25.5 us
    pallas_call x1, Pallas kernels, modes(): pl.pallas_call(functools.partial(modes_kernel, places, scale, len(terms))...  13.7 us
    ppermute x7, starting transfers between devices, exchange(): lax.ppermute(local, axis, [(i, i ^ step) for i in range(count)])  10.9 us
    ppermute x7, waiting for transfers between devices, exchange(): lax.ppermute(local, axis, [(i, i ^ step) for i in range(count)])  8.64 us
    pallas_call x1, Pallas kernels, edges(): pl.pallas_call(edges_kernel, in_specs=[HBM], out_specs=[HBM] * 5, out_sha...  8.11 us
    pallas_call x1, Pallas kernels, planes(): pl.pallas_call(planes_kernel, in_specs=[HBM], out_specs=HBM, out_shape=ja...  8.04 us
    ppermute x1, waiting for transfers between devices, far_exchange(): lax.ppermute(cells, 'stream', [(3, 2), (0, 1)])  7.23 us
    pallas_call x1, Pallas kernels, outer_fields(): pl.pallas_call(outer_kernel, in_specs=[HBM] * 4 + [SMEM, VMEM], out_specs...  5.72 us
  transfers between devices with their start and end apart: 13, of which 8 were waited for; matrix products, arithmetic and copies ran while one was open for 0% of the time, Pallas kernels for 31%

profile of v5, /device:TPU:0, one launch (start us, length us, event | category | flops | bytes accessed | tf_op | source)
XLA Modules:
  0.0 109.1 jit_solution(11123579940409600705)
XLA Ops:
  0.6 8.1 %shard_map.59 = (bf16[3,2,8,128,128]{4,3,2,1,0:T(8,128)(2,1)}, bf16[3,2,4,128,128]{4,3,2,1,0:T(8,128)(2,1)}, bf16[3,2,4,128,128]{4,3,2,1,0:T(8,128)(2,1)}, bf16[...) custom-call(bf16[128,3,12,8,128]{4,3,2,1,0:T(8,128)(2,1)} %velocity.2), custom_call_target="tpu_custom_call" | custom-call | tf_op jit(solution)/shard_map/pallas_call | solution.py:128
  8.7 2.5 %collective-permute-start.4 = (bf16[3,12,2,128,128]{4,3,2,1,0:T(8,128)(2,1)}, bf16[3,12,2,128,128]{4,3,2,1,0:T(8,128)(2,1)S(1)}, u32[]{:S(2)}, u32[]{:S(2)}) collective-permute-start(bf16[3,12,2,128,128]{4,3,2,1,0:T(8,128)(2,1)} %get-tuple-element.22), channel_id=1, source_target_pairs={{0,1},{1,2},{2,3},{3,4},{4,5},{5,6},{6,7},{8,9},{9,10},{10,11},{11... | collective-permute-start | bytes 7077896 | tf_op jit(solution)/shard_map/ppermute | solution.py:631
  11.3 1.3 %collective-permute-start.5 = (bf16[3,12,2,128,128]{4,3,2,1,0:T(8,128)(2,1)}, bf16[3,12,2,128,128]{4,3,2,1,0:T(8,128)(2,1)}, u32[]{:S(2)}, u32[]{:S(2)}) collective-permute-start(bf16[3,12,2,128,128]{4,3,2,1,0:T(8,128)(2,1)} %get-tuple-element.23), channel_id=1, source_target_pairs={{1,0},{2,1},{3,2},{4,3},{5,4},{6,5},{7,6},{9,8},{10,9},{11,10},{12... | collective-permute-start | bytes 7077896 | tf_op jit(solution)/shard_map/ppermute | solution.py:631
  12.6 1.3 %collective-permute-start.2 = (bf16[3,2,4,128,128]{4,3,2,1,0:T(8,128)(2,1)}, bf16[3,2,4,128,128]{4,3,2,1,0:T(8,128)(2,1)}, u32[]{:S(2)}, u32[]{:S(2)}) collective-permute-start(bf16[3,2,4,128,128]{4,3,2,1,0:T(8,128)(2,1)} %get-tuple-element.18), channel_id=1, source_target_pairs={{8,24},{16,0},{9,25},{17,1},{10,26},{18,2},{11,27},{19,3},{12,28},... | collective-permute-start | bytes 2359304 | tf_op jit(solution)/shard_map/ppermute | solution.py:642
  13.9 5.2 %collective-permute-start = (bf16[3,2,8,128,128]{4,3,2,1,0:T(8,128)(2,1)}, bf16[3,2,8,128,128]{4,3,2,1,0:T(8,128)(2,1)S(1)}, u32[]{:S(2)}, u32[]{:S(2)}) collective-permute-start(bf16[3,2,8,128,128]{4,3,2,1,0:T(8,128)(2,1)} %get-tuple-element.16), channel_id=1, source_target_pairs={{0,8},{8,0},{16,24},{24,16},{1,9},{9,1},{17,25},{25,17},{2,10},{10... | collective-permute-start | bytes 4718600 | tf_op jit(solution)/shard_map/ppermute | solution.py:653
  19.1 1.7 %collective-permute-start.1 = (bf16[3,2,4,128,128]{4,3,2,1,0:T(8,128)(2,1)}, bf16[3,2,4,128,128]{4,3,2,1,0:T(8,128)(2,1)}, u32[]{:S(2)}, u32[]{:S(2)}) collective-permute-start(bf16[3,2,4,128,128]{4,3,2,1,0:T(8,128)(2,1)} %get-tuple-element.17), channel_id=1, source_target_pairs={{8,16},{16,8},{9,17},{17,9},{10,18},{18,10},{11,19},{19,11},{12,20... | collective-permute-start | bytes 2359304 | tf_op jit(solution)/shard_map/ppermute | solution.py:654
  20.7 8.0 %shard_map.60.cells = bf16[3,12,8,128,128]{4,3,2,1,0:T(8,128)(2,1)} custom-call(bf16[128,3,12,8,128]{4,3,2,1,0:T(8,128)(2,1)} %velocity.2), custom_call_target="tpu_custom_call" | custom-call | tf_op jit(solution)/shard_map/pallas_call | solution.py:180
  28.8 4.1 %collective-permute-done.2 = bf16[3,2,4,128,128]{4,3,2,1,0:T(8,128)(2,1)} collective-permute-done((bf16[3,2,4,128,128]{4,3,2,1,0:T(8,128)(2,1)}, bf16[3,2,4,128,128]{4,3,2,1,0:T(8,128)(2,1)}, u32[]{:S(2)}, u32[]{:S(2)}) %collective-permute-start.2) | collective-permute-done | bytes 786464 | tf_op jit(solution)/shard_map/ppermute | solution.py:642
  32.9 4.0 %collective-permute-start.3 = (bf16[3,2,4,128,128]{4,3,2,1,0:T(8,128)(2,1)}, bf16[3,2,4,128,128]{4,3,2,1,0:T(8,128)(2,1)S(1)}, u32[]{:S(2)}, u32[]{:S(2)}) collective-permute-start(bf16[3,2,4,128,128]{4,3,2,1,0:T(8,128)(2,1)} %collective-permute-done.2), channel_id=1, source_target_pairs={{24,16},{0,8},{25,17},{1,9},{26,18},{2,10},{27,19},{3,11},{28,20},... | collective-permute-start | bytes 2359304 | tf_op jit(solution)/shard_map/ppermute | solution.py:643
  37.0 0.1 add_convert_fusion.taps_ref
  37.1 0.0 collective-permute-done.4.low
  37.1 0.0 collective-permute-done.5.high
  37.2 25.5 %shard_map.61 = (bf16[8,128,4096]{2,1,0:T(8,128)(2,1)}, bf16[4,128,1024]{2,1,0:T(8,128)(2,1)S(1)}, f32[4,128,3072]{2,1,0:T(8,128)S(1)}, f32[128,128]{1,0:T(8,128)S(1)}) custom-call(f32[12]{0:T(128)S(1)} %broadcast_multiply_fusion.1.mx_ref, f32[8]{0:T(128)S(1)} %broadcast_multiply_fusion.my_ref, f32[1,128]{1,0:T(1,128)S(1)} %multiply_bitcast_fusion.mz_ref, ...), custom_call_target="tpu_custom_call" | custom-call | tf_op jit(solution)/shard_map/pallas_call | solution.py:325
  62.7 0.0 collective-permute-done.1.far1
  62.7 0.0 collective-permute-done.near
  62.7 7.2 %collective-permute-done.3.far2 = bf16[3,2,4,128,128]{4,3,2,1,0:T(8,128)(2,1)S(1)} collective-permute-done((bf16[3,2,4,128,128]{4,3,2,1,0:T(8,128)(2,1)}, bf16[3,2,4,128,128]{4,3,2,1,0:T(8,128)(2,1)S(1)}, u32[]{:S(2)}, u32[]{:S(2)}) %collective-permute-start.3) | collective-permute-done | bytes 786464 | tf_op jit(solution)/shard_map/ppermute | solution.py:643
  69.9 5.7 %shard_map.62 = (bf16[4,128,3072]{2,1,0:T(8,128)(2,1)S(1)}, f32[72,128]{1,0:T(8,128)S(1)}) custom-call(bf16[3,2,8,128,128]{4,3,2,1,0:T(8,128)(2,1)S(1)} %collective-permute-done.near, bf16[3,2,4,128,128]{4,3,2,1,0:T(8,128)(2,1)} %collective-permute-done.1.far1, bf16[3,2,4,128,128]{4,3,2,1,0:T(8,128)(2,1)S(1)} %collective-permute-done.3.far2, ...), custom_call_target="tpu_custom_call" | custom-call | tf_op jit(solution)/shard_map/pallas_call | solution.py:449
  75.7 1.3 %collective-permute-start.6 = (f32[72,128]{1,0:T(8,128)S(1)}, f32[72,128]{1,0:T(8,128)S(1)}, u32[]{:S(2)}, u32[]{:S(2)}) collective-permute-start(f32[72,128]{1,0:T(8,128)S(1)} %get-tuple-element.26), channel_id=1, source_target_pairs={{0,1},{1,0},{2,3},{3,2},{4,5},{5,4},{6,7},{7,6},{8,9},{9,8},{10,11... | collective-permute-start | bytes 110600 | tf_op jit(solution)/shard_map/ppermute | solution.py:623
  76.9 0.9 collective-permute-done.6
  77.8 5.2 %collective-permute-start.9 = (f32[72,128]{1,0:T(8,128)S(1)}, f32[72,128]{1,0:T(8,128)S(1)}, u32[]{:S(2)}, u32[]{:S(2)}) collective-permute-start(f32[72,128]{1,0:T(8,128)S(1)} %add.60), channel_id=1, source_target_pairs={{0,6},{1,7},{2,4},{3,5},{4,2},{5,3},{6,0},{7,1},{8,14},{9,15},{10,... | collective-permute-start | bytes 110600 | tf_op jit(solution)/shard_map/ppermute | solution.py:623
  83.0 0.0 collective-permute-start.8
  83.0 0.6 collective-permute-start.7
  83.7 1.3 %collective-permute-done.9 = f32[72,128]{1,0:T(8,128)S(1)} collective-permute-done((f32[72,128]{1,0:T(8,128)S(1)}, f32[72,128]{1,0:T(8,128)S(1)}, u32[]{:S(2)}, u32[]{:S(2)}) %collective-permute-start.9) | collective-permute-done | bytes 36896 | tf_op jit(solution)/shard_map/ppermute | solution.py:623
  85.0 2.9 %collective-permute-done.8 = f32[72,128]{1,0:T(8,128)S(1)} collective-permute-done((f32[72,128]{1,0:T(8,128)S(1)}, f32[72,128]{1,0:T(8,128)S(1)}, u32[]{:S(2)}, u32[]{:S(2)}) %collective-permute-start.8) | collective-permute-done | bytes 36896 | tf_op jit(solution)/shard_map/ppermute | solution.py:623
  87.9 0.0 collective-permute-done.7
  87.9 0.1 collective-permute-start.12
  88.0 3.2 %collective-permute-start.11 = (f32[72,128]{1,0:T(8,128)S(1)}, f32[72,128]{1,0:T(8,128)S(1)}, u32[]{:S(2)}, u32[]{:S(2)}) collective-permute-start(f32[72,128]{1,0:T(8,128)S(1)} %add_add_fusion.rest_0_), channel_id=1, source_target_pairs={{0,16},{8,24},{16,0},{24,8},{1,17},{9,25},{17,1},{25,9},{2,18},{10... | collective-permute-start | bytes 110600 | tf_op jit(solution)/shard_map/ppermute | solution.py:623
  91.3 0.4 collective-permute-start.10
  91.7 1.6 %collective-permute-done.12.rest_3_ = f32[72,128]{1,0:T(8,128)S(1)} collective-permute-done((f32[72,128]{1,0:T(8,128)S(1)}, f32[72,128]{1,0:T(8,128)S(1)}, u32[]{:S(2)}, u32[]{:S(2)}) %collective-permute-start.12) | collective-permute-done | bytes 36896 | tf_op jit(solution)/shard_map/ppermute | solution.py:623
  93.2 0.2 collective-permute-done.11.rest_2_
  93.4 1.8 %collective-permute-done.10.rest_1_ = f32[72,128]{1,0:T(8,128)S(1)} collective-permute-done((f32[72,128]{1,0:T(8,128)S(1)}, f32[72,128]{1,0:T(8,128)S(1)}, u32[]{:S(2)}, u32[]{:S(2)}) %collective-permute-start.10) | collective-permute-done | bytes 36896 | tf_op jit(solution)/shard_map/ppermute | solution.py:623
  95.2 13.7 %shard_map.63 = (bf16[128,4,12,8,128]{4,3,2,1,0:T(8,128)(2,1)}, f32[128,128]{1,0:T(8,128)}) custom-call(f32[72,128]{1,0:T(8,128)S(1)} %add_add_fusion.rest_0_, f32[72,128]{1,0:T(8,128)S(1)} %collective-permute-done.10.rest_1_, f32[72,128]{1,0:T(8,128)S(1)} %collective-permute-done.11.rest_2_, f32[72,128]{1,0:T(8,128)S(1)} %collective-permute-done.12.rest_3_, ...), custom_call_target="tpu_custom_call" | custom-call | tf_op jit(solution)/shard_map/pallas_call | solution.py:585
  (15 shorter events, 0.0 us)
Async XLA Ops:
  8.7 28.4 %collective-permute-start.4 = (bf16[3,12,2,128,128]{4,3,2,1,0:T(8,128)(2,1)}, bf16[3,12,2,128,128]{4,3,2,1,0:T(8,128)(2,1)S(1)}, u32[]{:S(2)}, u32[]{:S(2)}) collective-permute-start(bf16[3,12,2,128,128]{4,3,2,1,0:T(8,128)(2,1)} %get-tuple-element.22), channel_id=1, source_target_pairs={{0,1},{1,2},{2,3},{3,4},{4,5},{5,6},{6,7},{8,9},{9,10},{10,11},{11... | collective-permute-start | bytes 7077896 | tf_op jit(solution)/shard_map/ppermute | solution.py:631
  11.3 25.9 %collective-permute-start.5 = (bf16[3,12,2,128,128]{4,3,2,1,0:T(8,128)(2,1)}, bf16[3,12,2,128,128]{4,3,2,1,0:T(8,128)(2,1)}, u32[]{:S(2)}, u32[]{:S(2)}) collective-permute-start(bf16[3,12,2,128,128]{4,3,2,1,0:T(8,128)(2,1)} %get-tuple-element.23), channel_id=1, source_target_pairs={{1,0},{2,1},{3,2},{4,3},{5,4},{6,5},{7,6},{9,8},{10,9},{11,10},{12... | collective-permute-start | bytes 7077896 | tf_op jit(solution)/shard_map/ppermute | solution.py:631
  12.6 20.4 %collective-permute-start.2 = (bf16[3,2,4,128,128]{4,3,2,1,0:T(8,128)(2,1)}, bf16[3,2,4,128,128]{4,3,2,1,0:T(8,128)(2,1)}, u32[]{:S(2)}, u32[]{:S(2)}) collective-permute-start(bf16[3,2,4,128,128]{4,3,2,1,0:T(8,128)(2,1)} %get-tuple-element.18), channel_id=1, source_target_pairs={{8,24},{16,0},{9,25},{17,1},{10,26},{18,2},{11,27},{19,3},{12,28},... | collective-permute-start | bytes 2359304 | tf_op jit(solution)/shard_map/ppermute | solution.py:642
  13.9 48.8 %collective-permute-start = (bf16[3,2,8,128,128]{4,3,2,1,0:T(8,128)(2,1)}, bf16[3,2,8,128,128]{4,3,2,1,0:T(8,128)(2,1)S(1)}, u32[]{:S(2)}, u32[]{:S(2)}) collective-permute-start(bf16[3,2,8,128,128]{4,3,2,1,0:T(8,128)(2,1)} %get-tuple-element.16), channel_id=1, source_target_pairs={{0,8},{8,0},{16,24},{24,16},{1,9},{9,1},{17,25},{25,17},{2,10},{10... | collective-permute-start | bytes 4718600 | tf_op jit(solution)/shard_map/ppermute | solution.py:653
  19.1 9.7 %copy-start.1 = (f32[12]{0:T(128)S(1)}, f32[12]{0:T(128)}, u32[]{:S(2)}) copy-start(f32[12]{0:T(128)} %param.5) | copy-start | bytes 148
  19.1 17.9 %copy-start.2 = (f32[8]{0:T(128)S(1)}, f32[8]{0:T(128)}, u32[]{:S(2)}) copy-start(f32[8]{0:T(128)} %param.6) | copy-start | bytes 100
  19.1 17.9 %copy-start.3 = (f32[128]{0:T(128)S(1)}, f32[128]{0:T(128)}, u32[]{:S(2)}) copy-start(f32[128]{0:T(128)} %param.7) | copy-start | bytes 1540
  19.1 43.6 %collective-permute-start.1 = (bf16[3,2,4,128,128]{4,3,2,1,0:T(8,128)(2,1)}, bf16[3,2,4,128,128]{4,3,2,1,0:T(8,128)(2,1)}, u32[]{:S(2)}, u32[]{:S(2)}) collective-permute-start(bf16[3,2,4,128,128]{4,3,2,1,0:T(8,128)(2,1)} %get-tuple-element.17), channel_id=1, source_target_pairs={{8,16},{16,8},{9,17},{17,9},{10,18},{18,10},{11,19},{19,11},{12,20... | collective-permute-start | bytes 2359304 | tf_op jit(solution)/shard_map/ppermute | solution.py:654
  32.9 37.0 %collective-permute-start.3 = (bf16[3,2,4,128,128]{4,3,2,1,0:T(8,128)(2,1)}, bf16[3,2,4,128,128]{4,3,2,1,0:T(8,128)(2,1)S(1)}, u32[]{:S(2)}, u32[]{:S(2)}) collective-permute-start(bf16[3,2,4,128,128]{4,3,2,1,0:T(8,128)(2,1)} %collective-permute-done.2), channel_id=1, source_target_pairs={{24,16},{0,8},{25,17},{1,9},{26,18},{2,10},{27,19},{3,11},{28,20},... | collective-permute-start | bytes 2359304 | tf_op jit(solution)/shard_map/ppermute | solution.py:643
  69.9 25.3 %copy-start = (bf16[8,128,4096]{2,1,0:T(8,128)(2,1)S(1)}, bf16[8,128,4096]{2,1,0:T(8,128)(2,1)}, u32[]{:S(2)}) copy-start(bf16[8,128,4096]{2,1,0:T(8,128)(2,1)} %get-tuple-element.27.rest_4_) | copy-start | bytes 25165828
  75.7 2.1 %collective-permute-start.6 = (f32[72,128]{1,0:T(8,128)S(1)}, f32[72,128]{1,0:T(8,128)S(1)}, u32[]{:S(2)}, u32[]{:S(2)}) collective-permute-start(f32[72,128]{1,0:T(8,128)S(1)} %get-tuple-element.26), channel_id=1, source_target_pairs={{0,1},{1,0},{2,3},{3,2},{4,5},{5,4},{6,7},{7,6},{8,9},{9,8},{10,11... | collective-permute-start | bytes 110600 | tf_op jit(solution)/shard_map/ppermute | solution.py:623
  77.8 7.1 %collective-permute-start.9 = (f32[72,128]{1,0:T(8,128)S(1)}, f32[72,128]{1,0:T(8,128)S(1)}, u32[]{:S(2)}, u32[]{:S(2)}) collective-permute-start(f32[72,128]{1,0:T(8,128)S(1)} %add.60), channel_id=1, source_target_pairs={{0,6},{1,7},{2,4},{3,5},{4,2},{5,3},{6,0},{7,1},{8,14},{9,15},{10,... | collective-permute-start | bytes 110600 | tf_op jit(solution)/shard_map/ppermute | solution.py:623
  83.0 4.9 %collective-permute-start.8 = (f32[72,128]{1,0:T(8,128)S(1)}, f32[72,128]{1,0:T(8,128)S(1)}, u32[]{:S(2)}, u32[]{:S(2)}) collective-permute-start(f32[72,128]{1,0:T(8,128)S(1)} %add.60), channel_id=1, source_target_pairs={{0,4},{1,5},{2,6},{3,7},{4,0},{5,1},{6,2},{7,3},{8,12},{9,13},{10,... | collective-permute-start | bytes 110600 | tf_op jit(solution)/shard_map/ppermute | solution.py:623
  83.0 4.9 %collective-permute-start.7 = (f32[72,128]{1,0:T(8,128)S(1)}, f32[72,128]{1,0:T(8,128)S(1)}, u32[]{:S(2)}, u32[]{:S(2)}) collective-permute-start(f32[72,128]{1,0:T(8,128)S(1)} %add.60), channel_id=1, source_target_pairs={{0,2},{1,3},{2,0},{3,1},{4,6},{5,7},{6,4},{7,5},{8,10},{9,11},{10,... | collective-permute-start | bytes 110600 | tf_op jit(solution)/shard_map/ppermute | solution.py:623
  87.9 5.3 %collective-permute-start.12 = (f32[72,128]{1,0:T(8,128)S(1)}, f32[72,128]{1,0:T(8,128)S(1)}, u32[]{:S(2)}, u32[]{:S(2)}) collective-permute-start(f32[72,128]{1,0:T(8,128)S(1)} %add_add_fusion.rest_0_), channel_id=1, source_target_pairs={{0,24},{8,16},{16,8},{24,0},{1,25},{9,17},{17,9},{25,1},{2,26},{10... | collective-permute-start | bytes 110600 | tf_op jit(solution)/shard_map/ppermute | solution.py:623
  88.0 5.4 %collective-permute-start.11 = (f32[72,128]{1,0:T(8,128)S(1)}, f32[72,128]{1,0:T(8,128)S(1)}, u32[]{:S(2)}, u32[]{:S(2)}) collective-permute-start(f32[72,128]{1,0:T(8,128)S(1)} %add_add_fusion.rest_0_), channel_id=1, source_target_pairs={{0,16},{8,24},{16,0},{24,8},{1,17},{9,25},{17,1},{25,9},{2,18},{10... | collective-permute-start | bytes 110600 | tf_op jit(solution)/shard_map/ppermute | solution.py:623
  91.3 4.0 %collective-permute-start.10 = (f32[72,128]{1,0:T(8,128)S(1)}, f32[72,128]{1,0:T(8,128)S(1)}, u32[]{:S(2)}, u32[]{:S(2)}) collective-permute-start(f32[72,128]{1,0:T(8,128)S(1)} %add_add_fusion.rest_0_), channel_id=1, source_target_pairs={{0,8},{8,0},{16,24},{24,16},{1,9},{9,1},{17,25},{25,17},{2,10},{10... | collective-permute-start | bytes 110600 | tf_op jit(solution)/shard_map/ppermute | solution.py:623

commit v6 on v5

--- a/solution.py
+++ b/solution.py
@@ -554,7 +554,7 @@
             copy.start()
 
     gram = symmetric(tree_sum([term[...] for term in terms]) * scale)
-    upper, inverse = factorize([gram[r : r + 8] for r in range(0, snaps, 8)], 4)
+    upper, inverse = factorize([gram[r : r + 8] for r in range(0, snaps, 8)], 8)
     r = lax.broadcasted_iota(jnp.int32, (snaps, snaps), 0)
     c = lax.broadcasted_iota(jnp.int32, (snaps, snaps), 1)
     lower_ref[...] = jnp.where(r >= c, upper.T, 0.0)

time: 109 us -> 109 us (level)
  no operation moved by 1% of the time
where the time goes in v6:
time: 109 us
  Pallas kernels  60.6 us (56%)
  starting transfers between devices  26.9 us (25%)
  waiting for transfers between devices  20 us (18%)
    pallas_call x1, Pallas kernels, inner_fields(): pl.pallas_call(inner_kernel, in_specs=[SMEM, SMEM, VMEM, VMEM] + [HBM] *...  25.5 us
    pallas_call x1, Pallas kernels, modes(): pl.pallas_call(functools.partial(modes_kernel, places, scale, len(terms))...  13.2 us
    ppermute x7, starting transfers between devices, exchange(): lax.ppermute(local, axis, [(i, i ^ step) for i in range(count)])  10.9 us
    ppermute x7, waiting for transfers between devices, exchange(): lax.ppermute(local, axis, [(i, i ^ step) for i in range(count)])  8.64 us
    pallas_call x1, Pallas kernels, edges(): pl.pallas_call(edges_kernel, in_specs=[HBM], out_specs=[HBM] * 5, out_sha...  8.11 us
    pallas_call x1, Pallas kernels, planes(): pl.pallas_call(planes_kernel, in_specs=[HBM], out_specs=HBM, out_shape=ja...  8.04 us
    ppermute x1, waiting for transfers between devices, far_exchange(): lax.ppermute(cells, 'stream', [(3, 2), (0, 1)])  7.23 us
    pallas_call x1, Pallas kernels, outer_fields(): pl.pallas_call(outer_kernel, in_specs=[HBM] * 4 + [SMEM, VMEM], out_specs...  5.72 us
  transfers between devices with their start and end apart: 13, of which 8 were waited for; matrix products, arithmetic and copies ran while one was open for 0% of the time, Pallas kernels for 31%

profile of v6, /device:TPU:0, one launch (start us, length us, event | category | flops | bytes accessed | tf_op | source)
XLA Modules:
  0.0 108.6 jit_solution(9081255701609547224)
XLA Ops:
  0.6 8.1 %shard_map.59 = (bf16[3,2,8,128,128]{4,3,2,1,0:T(8,128)(2,1)}, bf16[3,2,4,128,128]{4,3,2,1,0:T(8,128)(2,1)}, bf16[3,2,4,128,128]{4,3,2,1,0:T(8,128)(2,1)}, bf16[...) custom-call(bf16[128,3,12,8,128]{4,3,2,1,0:T(8,128)(2,1)} %velocity.2), custom_call_target="tpu_custom_call" | custom-call | tf_op jit(solution)/shard_map/pallas_call | solution.py:128
  8.7 2.5 %collective-permute-start.4 = (bf16[3,12,2,128,128]{4,3,2,1,0:T(8,128)(2,1)}, bf16[3,12,2,128,128]{4,3,2,1,0:T(8,128)(2,1)S(1)}, u32[]{:S(2)}, u32[]{:S(2)}) collective-permute-start(bf16[3,12,2,128,128]{4,3,2,1,0:T(8,128)(2,1)} %get-tuple-element.22), channel_id=1, source_target_pairs={{0,1},{1,2},{2,3},{3,4},{4,5},{5,6},{6,7},{8,9},{9,10},{10,11},{11... | collective-permute-start | bytes 7077896 | tf_op jit(solution)/shard_map/ppermute | solution.py:631
  11.3 1.3 %collective-permute-start.5 = (bf16[3,12,2,128,128]{4,3,2,1,0:T(8,128)(2,1)}, bf16[3,12,2,128,128]{4,3,2,1,0:T(8,128)(2,1)}, u32[]{:S(2)}, u32[]{:S(2)}) collective-permute-start(bf16[3,12,2,128,128]{4,3,2,1,0:T(8,128)(2,1)} %get-tuple-element.23), channel_id=1, source_target_pairs={{1,0},{2,1},{3,2},{4,3},{5,4},{6,5},{7,6},{9,8},{10,9},{11,10},{12... | collective-permute-start | bytes 7077896 | tf_op jit(solution)/shard_map/ppermute | solution.py:631
  12.6 1.3 %collective-permute-start.2 = (bf16[3,2,4,128,128]{4,3,2,1,0:T(8,128)(2,1)}, bf16[3,2,4,128,128]{4,3,2,1,0:T(8,128)(2,1)}, u32[]{:S(2)}, u32[]{:S(2)}) collective-permute-start(bf16[3,2,4,128,128]{4,3,2,1,0:T(8,128)(2,1)} %get-tuple-element.18), channel_id=1, source_target_pairs={{8,24},{16,0},{9,25},{17,1},{10,26},{18,2},{11,27},{19,3},{12,28},... | collective-permute-start | bytes 2359304 | tf_op jit(solution)/shard_map/ppermute | solution.py:642
  13.9 5.2 %collective-permute-start = (bf16[3,2,8,128,128]{4,3,2,1,0:T(8,128)(2,1)}, bf16[3,2,8,128,128]{4,3,2,1,0:T(8,128)(2,1)S(1)}, u32[]{:S(2)}, u32[]{:S(2)}) collective-permute-start(bf16[3,2,8,128,128]{4,3,2,1,0:T(8,128)(2,1)} %get-tuple-element.16), channel_id=1, source_target_pairs={{0,8},{8,0},{16,24},{24,16},{1,9},{9,1},{17,25},{25,17},{2,10},{10... | collective-permute-start | bytes 4718600 | tf_op jit(solution)/shard_map/ppermute | solution.py:653
  19.1 1.7 %collective-permute-start.1 = (bf16[3,2,4,128,128]{4,3,2,1,0:T(8,128)(2,1)}, bf16[3,2,4,128,128]{4,3,2,1,0:T(8,128)(2,1)}, u32[]{:S(2)}, u32[]{:S(2)}) collective-permute-start(bf16[3,2,4,128,128]{4,3,2,1,0:T(8,128)(2,1)} %get-tuple-element.17), channel_id=1, source_target_pairs={{8,16},{16,8},{9,17},{17,9},{10,18},{18,10},{11,19},{19,11},{12,20... | collective-permute-start | bytes 2359304 | tf_op jit(solution)/shard_map/ppermute | solution.py:654
  20.7 8.0 %shard_map.60.cells = bf16[3,12,8,128,128]{4,3,2,1,0:T(8,128)(2,1)} custom-call(bf16[128,3,12,8,128]{4,3,2,1,0:T(8,128)(2,1)} %velocity.2), custom_call_target="tpu_custom_call" | custom-call | tf_op jit(solution)/shard_map/pallas_call | solution.py:180
  28.8 4.1 %collective-permute-done.2 = bf16[3,2,4,128,128]{4,3,2,1,0:T(8,128)(2,1)} collective-permute-done((bf16[3,2,4,128,128]{4,3,2,1,0:T(8,128)(2,1)}, bf16[3,2,4,128,128]{4,3,2,1,0:T(8,128)(2,1)}, u32[]{:S(2)}, u32[]{:S(2)}) %collective-permute-start.2) | collective-permute-done | bytes 786464 | tf_op jit(solution)/shard_map/ppermute | solution.py:642
  32.9 4.0 %collective-permute-start.3 = (bf16[3,2,4,128,128]{4,3,2,1,0:T(8,128)(2,1)}, bf16[3,2,4,128,128]{4,3,2,1,0:T(8,128)(2,1)S(1)}, u32[]{:S(2)}, u32[]{:S(2)}) collective-permute-start(bf16[3,2,4,128,128]{4,3,2,1,0:T(8,128)(2,1)} %collective-permute-done.2), channel_id=1, source_target_pairs={{24,16},{0,8},{25,17},{1,9},{26,18},{2,10},{27,19},{3,11},{28,20},... | collective-permute-start | bytes 2359304 | tf_op jit(solution)/shard_map/ppermute | solution.py:643
  37.0 0.1 add_convert_fusion.taps_ref
  37.1 0.0 collective-permute-done.4.low
  37.1 0.0 collective-permute-done.5.high
  37.2 25.5 %shard_map.61 = (bf16[8,128,4096]{2,1,0:T(8,128)(2,1)}, bf16[4,128,1024]{2,1,0:T(8,128)(2,1)S(1)}, f32[4,128,3072]{2,1,0:T(8,128)S(1)}, f32[128,128]{1,0:T(8,128)S(1)}) custom-call(f32[12]{0:T(128)S(1)} %broadcast_multiply_fusion.1.mx_ref, f32[8]{0:T(128)S(1)} %broadcast_multiply_fusion.my_ref, f32[1,128]{1,0:T(1,128)S(1)} %multiply_bitcast_fusion.mz_ref, ...), custom_call_target="tpu_custom_call" | custom-call | tf_op jit(solution)/shard_map/pallas_call | solution.py:325
  62.7 0.0 collective-permute-done.1.far1
  62.7 0.0 collective-permute-done.near
  62.7 7.2 %collective-permute-done.3.far2 = bf16[3,2,4,128,128]{4,3,2,1,0:T(8,128)(2,1)S(1)} collective-permute-done((bf16[3,2,4,128,128]{4,3,2,1,0:T(8,128)(2,1)}, bf16[3,2,4,128,128]{4,3,2,1,0:T(8,128)(2,1)S(1)}, u32[]{:S(2)}, u32[]{:S(2)}) %collective-permute-start.3) | collective-permute-done | bytes 786464 | tf_op jit(solution)/shard_map/ppermute | solution.py:643
  69.9 5.7 %shard_map.62 = (bf16[4,128,3072]{2,1,0:T(8,128)(2,1)S(1)}, f32[72,128]{1,0:T(8,128)S(1)}) custom-call(bf16[3,2,8,128,128]{4,3,2,1,0:T(8,128)(2,1)S(1)} %collective-permute-done.near, bf16[3,2,4,128,128]{4,3,2,1,0:T(8,128)(2,1)} %collective-permute-done.1.far1, bf16[3,2,4,128,128]{4,3,2,1,0:T(8,128)(2,1)S(1)} %collective-permute-done.3.far2, ...), custom_call_target="tpu_custom_call" | custom-call | tf_op jit(solution)/shard_map/pallas_call | solution.py:449
  75.7 1.3 %collective-permute-start.6 = (f32[72,128]{1,0:T(8,128)S(1)}, f32[72,128]{1,0:T(8,128)S(1)}, u32[]{:S(2)}, u32[]{:S(2)}) collective-permute-start(f32[72,128]{1,0:T(8,128)S(1)} %get-tuple-element.26), channel_id=1, source_target_pairs={{0,1},{1,0},{2,3},{3,2},{4,5},{5,4},{6,7},{7,6},{8,9},{9,8},{10,11... | collective-permute-start | bytes 110600 | tf_op jit(solution)/shard_map/ppermute | solution.py:623
  76.9 0.9 collective-permute-done.6
  77.8 5.2 %collective-permute-start.9 = (f32[72,128]{1,0:T(8,128)S(1)}, f32[72,128]{1,0:T(8,128)S(1)}, u32[]{:S(2)}, u32[]{:S(2)}) collective-permute-start(f32[72,128]{1,0:T(8,128)S(1)} %add.60), channel_id=1, source_target_pairs={{0,6},{1,7},{2,4},{3,5},{4,2},{5,3},{6,0},{7,1},{8,14},{9,15},{10,... | collective-permute-start | bytes 110600 | tf_op jit(solution)/shard_map/ppermute | solution.py:623
  83.0 0.0 collective-permute-start.8
  83.0 0.6 collective-permute-start.7
  83.7 1.3 %collective-permute-done.9 = f32[72,128]{1,0:T(8,128)S(1)} collective-permute-done((f32[72,128]{1,0:T(8,128)S(1)}, f32[72,128]{1,0:T(8,128)S(1)}, u32[]{:S(2)}, u32[]{:S(2)}) %collective-permute-start.9) | collective-permute-done | bytes 36896 | tf_op jit(solution)/shard_map/ppermute | solution.py:623
  85.0 2.9 %collective-permute-done.8 = f32[72,128]{1,0:T(8,128)S(1)} collective-permute-done((f32[72,128]{1,0:T(8,128)S(1)}, f32[72,128]{1,0:T(8,128)S(1)}, u32[]{:S(2)}, u32[]{:S(2)}) %collective-permute-start.8) | collective-permute-done | bytes 36896 | tf_op jit(solution)/shard_map/ppermute | solution.py:623
  87.9 0.0 collective-permute-done.7
  87.9 0.1 collective-permute-start.12
  88.0 3.2 %collective-permute-start.11 = (f32[72,128]{1,0:T(8,128)S(1)}, f32[72,128]{1,0:T(8,128)S(1)}, u32[]{:S(2)}, u32[]{:S(2)}) collective-permute-start(f32[72,128]{1,0:T(8,128)S(1)} %add_add_fusion.rest_0_), channel_id=1, source_target_pairs={{0,16},{8,24},{16,0},{24,8},{1,17},{9,25},{17,1},{25,9},{2,18},{10... | collective-permute-start | bytes 110600 | tf_op jit(solution)/shard_map/ppermute | solution.py:623
  91.3 0.4 collective-permute-start.10
  91.7 1.6 %collective-permute-done.12.rest_3_ = f32[72,128]{1,0:T(8,128)S(1)} collective-permute-done((f32[72,128]{1,0:T(8,128)S(1)}, f32[72,128]{1,0:T(8,128)S(1)}, u32[]{:S(2)}, u32[]{:S(2)}) %collective-permute-start.12) | collective-permute-done | bytes 36896 | tf_op jit(solution)/shard_map/ppermute | solution.py:623
  93.2 0.2 collective-permute-done.11.rest_2_
  93.4 1.8 %collective-permute-done.10.rest_1_ = f32[72,128]{1,0:T(8,128)S(1)} collective-permute-done((f32[72,128]{1,0:T(8,128)S(1)}, f32[72,128]{1,0:T(8,128)S(1)}, u32[]{:S(2)}, u32[]{:S(2)}) %collective-permute-start.10) | collective-permute-done | bytes 36896 | tf_op jit(solution)/shard_map/ppermute | solution.py:623
  95.2 13.2 %shard_map.63 = (bf16[128,4,12,8,128]{4,3,2,1,0:T(8,128)(2,1)}, f32[128,128]{1,0:T(8,128)}) custom-call(f32[72,128]{1,0:T(8,128)S(1)} %add_add_fusion.rest_0_, f32[72,128]{1,0:T(8,128)S(1)} %collective-permute-done.10.rest_1_, f32[72,128]{1,0:T(8,128)S(1)} %collective-permute-done.11.rest_2_, f32[72,128]{1,0:T(8,128)S(1)} %collective-permute-done.12.rest_3_, ...), custom_call_target="tpu_custom_call" | custom-call | tf_op jit(solution)/shard_map/pallas_call | solution.py:585
  (15 shorter events, 0.0 us)
Async XLA Ops:
  8.7 28.4 %collective-permute-start.4 = (bf16[3,12,2,128,128]{4,3,2,1,0:T(8,128)(2,1)}, bf16[3,12,2,128,128]{4,3,2,1,0:T(8,128)(2,1)S(1)}, u32[]{:S(2)}, u32[]{:S(2)}) collective-permute-start(bf16[3,12,2,128,128]{4,3,2,1,0:T(8,128)(2,1)} %get-tuple-element.22), channel_id=1, source_target_pairs={{0,1},{1,2},{2,3},{3,4},{4,5},{5,6},{6,7},{8,9},{9,10},{10,11},{11... | collective-permute-start | bytes 7077896 | tf_op jit(solution)/shard_map/ppermute | solution.py:631
  11.3 25.9 %collective-permute-start.5 = (bf16[3,12,2,128,128]{4,3,2,1,0:T(8,128)(2,1)}, bf16[3,12,2,128,128]{4,3,2,1,0:T(8,128)(2,1)}, u32[]{:S(2)}, u32[]{:S(2)}) collective-permute-start(bf16[3,12,2,128,128]{4,3,2,1,0:T(8,128)(2,1)} %get-tuple-element.23), channel_id=1, source_target_pairs={{1,0},{2,1},{3,2},{4,3},{5,4},{6,5},{7,6},{9,8},{10,9},{11,10},{12... | collective-permute-start | bytes 7077896 | tf_op jit(solution)/shard_map/ppermute | solution.py:631
  12.6 20.4 %collective-permute-start.2 = (bf16[3,2,4,128,128]{4,3,2,1,0:T(8,128)(2,1)}, bf16[3,2,4,128,128]{4,3,2,1,0:T(8,128)(2,1)}, u32[]{:S(2)}, u32[]{:S(2)}) collective-permute-start(bf16[3,2,4,128,128]{4,3,2,1,0:T(8,128)(2,1)} %get-tuple-element.18), channel_id=1, source_target_pairs={{8,24},{16,0},{9,25},{17,1},{10,26},{18,2},{11,27},{19,3},{12,28},... | collective-permute-start | bytes 2359304 | tf_op jit(solution)/shard_map/ppermute | solution.py:642
  13.9 48.8 %collective-permute-start = (bf16[3,2,8,128,128]{4,3,2,1,0:T(8,128)(2,1)}, bf16[3,2,8,128,128]{4,3,2,1,0:T(8,128)(2,1)S(1)}, u32[]{:S(2)}, u32[]{:S(2)}) collective-permute-start(bf16[3,2,8,128,128]{4,3,2,1,0:T(8,128)(2,1)} %get-tuple-element.16), channel_id=1, source_target_pairs={{0,8},{8,0},{16,24},{24,16},{1,9},{9,1},{17,25},{25,17},{2,10},{10... | collective-permute-start | bytes 4718600 | tf_op jit(solution)/shard_map/ppermute | solution.py:653
  19.1 9.7 %copy-start.1 = (f32[12]{0:T(128)S(1)}, f32[12]{0:T(128)}, u32[]{:S(2)}) copy-start(f32[12]{0:T(128)} %param.5) | copy-start | bytes 148
  19.1 17.9 %copy-start.2 = (f32[8]{0:T(128)S(1)}, f32[8]{0:T(128)}, u32[]{:S(2)}) copy-start(f32[8]{0:T(128)} %param.6) | copy-start | bytes 100
  19.1 17.9 %copy-start.3 = (f32[128]{0:T(128)S(1)}, f32[128]{0:T(128)}, u32[]{:S(2)}) copy-start(f32[128]{0:T(128)} %param.7) | copy-start | bytes 1540
  19.1 43.6 %collective-permute-start.1 = (bf16[3,2,4,128,128]{4,3,2,1,0:T(8,128)(2,1)}, bf16[3,2,4,128,128]{4,3,2,1,0:T(8,128)(2,1)}, u32[]{:S(2)}, u32[]{:S(2)}) collective-permute-start(bf16[3,2,4,128,128]{4,3,2,1,0:T(8,128)(2,1)} %get-tuple-element.17), channel_id=1, source_target_pairs={{8,16},{16,8},{9,17},{17,9},{10,18},{18,10},{11,19},{19,11},{12,20... | collective-permute-start | bytes 2359304 | tf_op jit(solution)/shard_map/ppermute | solution.py:654
  32.9 37.0 %collective-permute-start.3 = (bf16[3,2,4,128,128]{4,3,2,1,0:T(8,128)(2,1)}, bf16[3,2,4,128,128]{4,3,2,1,0:T(8,128)(2,1)S(1)}, u32[]{:S(2)}, u32[]{:S(2)}) collective-permute-start(bf16[3,2,4,128,128]{4,3,2,1,0:T(8,128)(2,1)} %collective-permute-done.2), channel_id=1, source_target_pairs={{24,16},{0,8},{25,17},{1,9},{26,18},{2,10},{27,19},{3,11},{28,20},... | collective-permute-start | bytes 2359304 | tf_op jit(solution)/shard_map/ppermute | solution.py:643
  69.9 25.3 %copy-start = (bf16[8,128,4096]{2,1,0:T(8,128)(2,1)S(1)}, bf16[8,128,4096]{2,1,0:T(8,128)(2,1)}, u32[]{:S(2)}) copy-start(bf16[8,128,4096]{2,1,0:T(8,128)(2,1)} %get-tuple-element.27.rest_4_) | copy-start | bytes 25165828
  75.7 2.1 %collective-permute-start.6 = (f32[72,128]{1,0:T(8,128)S(1)}, f32[72,128]{1,0:T(8,128)S(1)}, u32[]{:S(2)}, u32[]{:S(2)}) collective-permute-start(f32[72,128]{1,0:T(8,128)S(1)} %get-tuple-element.26), channel_id=1, source_target_pairs={{0,1},{1,0},{2,3},{3,2},{4,5},{5,4},{6,7},{7,6},{8,9},{9,8},{10,11... | collective-permute-start | bytes 110600 | tf_op jit(solution)/shard_map/ppermute | solution.py:623
  77.8 7.1 %collective-permute-start.9 = (f32[72,128]{1,0:T(8,128)S(1)}, f32[72,128]{1,0:T(8,128)S(1)}, u32[]{:S(2)}, u32[]{:S(2)}) collective-permute-start(f32[72,128]{1,0:T(8,128)S(1)} %add.60), channel_id=1, source_target_pairs={{0,6},{1,7},{2,4},{3,5},{4,2},{5,3},{6,0},{7,1},{8,14},{9,15},{10,... | collective-permute-start | bytes 110600 | tf_op jit(solution)/shard_map/ppermute | solution.py:623
  83.0 4.9 %collective-permute-start.8 = (f32[72,128]{1,0:T(8,128)S(1)}, f32[72,128]{1,0:T(8,128)S(1)}, u32[]{:S(2)}, u32[]{:S(2)}) collective-permute-start(f32[72,128]{1,0:T(8,128)S(1)} %add.60), channel_id=1, source_target_pairs={{0,4},{1,5},{2,6},{3,7},{4,0},{5,1},{6,2},{7,3},{8,12},{9,13},{10,... | collective-permute-start | bytes 110600 | tf_op jit(solution)/shard_map/ppermute | solution.py:623
  83.0 4.9 %collective-permute-start.7 = (f32[72,128]{1,0:T(8,128)S(1)}, f32[72,128]{1,0:T(8,128)S(1)}, u32[]{:S(2)}, u32[]{:S(2)}) collective-permute-start(f32[72,128]{1,0:T(8,128)S(1)} %add.60), channel_id=1, source_target_pairs={{0,2},{1,3},{2,0},{3,1},{4,6},{5,7},{6,4},{7,5},{8,10},{9,11},{10,... | collective-permute-start | bytes 110600 | tf_op jit(solution)/shard_map/ppermute | solution.py:623
  87.9 5.3 %collective-permute-start.12 = (f32[72,128]{1,0:T(8,128)S(1)}, f32[72,128]{1,0:T(8,128)S(1)}, u32[]{:S(2)}, u32[]{:S(2)}) collective-permute-start(f32[72,128]{1,0:T(8,128)S(1)} %add_add_fusion.rest_0_), channel_id=1, source_target_pairs={{0,24},{8,16},{16,8},{24,0},{1,25},{9,17},{17,9},{25,1},{2,26},{10... | collective-permute-start | bytes 110600 | tf_op jit(solution)/shard_map/ppermute | solution.py:623
  88.0 5.4 %collective-permute-start.11 = (f32[72,128]{1,0:T(8,128)S(1)}, f32[72,128]{1,0:T(8,128)S(1)}, u32[]{:S(2)}, u32[]{:S(2)}) collective-permute-start(f32[72,128]{1,0:T(8,128)S(1)} %add_add_fusion.rest_0_), channel_id=1, source_target_pairs={{0,16},{8,24},{16,0},{24,8},{1,17},{9,25},{17,1},{25,9},{2,18},{10... | collective-permute-start | bytes 110600 | tf_op jit(solution)/shard_map/ppermute | solution.py:623
  91.3 4.0 %collective-permute-start.10 = (f32[72,128]{1,0:T(8,128)S(1)}, f32[72,128]{1,0:T(8,128)S(1)}, u32[]{:S(2)}, u32[]{:S(2)}) collective-permute-start(f32[72,128]{1,0:T(8,128)S(1)} %add_add_fusion.rest_0_), channel_id=1, source_target_pairs={{0,8},{8,0},{16,24},{24,16},{1,9},{9,1},{17,25},{25,17},{2,10},{10... | collective-permute-start | bytes 110600 | tf_op jit(solution)/shard_map/ppermute | solution.py:623

commit v7 on v6

--- a/solution.py
+++ b/solution.py
@@ -51,9 +51,9 @@
             velocity.at[:, c, pl.ds(2, between)], inner.at[c], inner_in.at[c]
         )
 
-    def side_writes(c, x):
+    def side_writes(c):
         return [
-            pltpu.make_async_copy(sides.at[k, c, x], ref.at[c, x], side_out.at[k, c, x])
+            pltpu.make_async_copy(sides.at[k, c], ref.at[c], side_out.at[k, c])
             for k, ref in enumerate((first, last))
         ]
 
@@ -79,8 +79,6 @@
                 put_side(c, x, y, plane)
 
             turn(tiles[side, c, :, layer], rows, range(cells_y), put)
-            for w in side_writes(c, x):
-                w.start()
             return 0
 
         lax.fori_loop(0, 2, one_end, 0)
@@ -105,21 +103,17 @@
                 (0, 1, cells_y - 2, cells_y - 1),
                 functools.partial(put_side, c, n + 2),
             )
-            for w in side_writes(c, n + 2):
-                w.start()
             return 0
 
         lax.fori_loop(0, between, one_inner, 0)
+        for w in side_writes(c):
+            w.start()
 
     for w in writes:
         w.wait()
-
-    def finish(n, _):
-        for w in side_writes(n // cells_x, lax.rem(n, cells_x)):
+    for c in range(comps):
+        for w in side_writes(c):
             w.wait()
-        return 0
-
-    lax.fori_loop(0, comps * cells_x, finish, 0)
 
 
 def edges(velocity):
@@ -139,7 +133,7 @@
             DMA((2, comps)),
             DMA((comps,)),
             DMA((3 * comps,)),
-            DMA((2, comps, cells_x)),
+            DMA((2, comps)),
         ],
         compiler_params=limit(60),
     )(velocity)

time: 109 us -> 109 us (level)
  no operation moved by 1% of the time
where the time goes in v7:
time: 109 us; the launch traced here: 108 us
  Pallas kernels  60.3 us (55%)
  starting transfers between devices  27 us (25%)
  waiting for transfers between devices  19.9 us (18%)
    pallas_call x1, Pallas kernels, inner_fields(): pl.pallas_call(inner_kernel, in_specs=[SMEM, SMEM, VMEM, VMEM] + [HBM] *...  25.5 us
    pallas_call x1, Pallas kernels, modes(): pl.pallas_call(functools.partial(modes_kernel, places, scale, len(terms))...  13.3 us
    ppermute x7, starting transfers between devices, exchange(): lax.ppermute(local, axis, [(i, i ^ step) for i in range(count)])  10.9 us
    ppermute x7, waiting for transfers between devices, exchange(): lax.ppermute(local, axis, [(i, i ^ step) for i in range(count)])  8.65 us
    pallas_call x1, Pallas kernels, planes(): pl.pallas_call(planes_kernel, in_specs=[HBM], out_specs=HBM, out_shape=ja...  8.04 us
    pallas_call x1, Pallas kernels, edges(): pl.pallas_call(edges_kernel, in_specs=[HBM], out_specs=[HBM] * 5, out_sha...  7.73 us
    ppermute x1, waiting for transfers between devices, far_exchange(): lax.ppermute(cells, 'stream', [(3, 2), (0, 1)])  7.23 us
    pallas_call x1, Pallas kernels, outer_fields(): pl.pallas_call(outer_kernel, in_specs=[HBM] * 4 + [SMEM, VMEM], out_specs...  5.72 us
  transfers between devices with their start and end apart: 13, of which 8 were waited for; matrix products, arithmetic and copies ran while one was open for 0% of the time, Pallas kernels for 31%

profile of v7, /device:TPU:0, one launch (start us, length us, event | category | flops | bytes accessed | tf_op | source)
XLA Modules:
  0.0 108.3 jit_solution(1955195591342301736)
XLA Ops:
  0.6 7.7 %shard_map.59 = (bf16[3,2,8,128,128]{4,3,2,1,0:T(8,128)(2,1)}, bf16[3,2,4,128,128]{4,3,2,1,0:T(8,128)(2,1)}, bf16[3,2,4,128,128]{4,3,2,1,0:T(8,128)(2,1)}, bf16[...) custom-call(bf16[128,3,12,8,128]{4,3,2,1,0:T(8,128)(2,1)} %velocity.2), custom_call_target="tpu_custom_call" | custom-call | tf_op jit(solution)/shard_map/pallas_call | solution.py:122
  8.4 2.5 %collective-permute-start.4 = (bf16[3,12,2,128,128]{4,3,2,1,0:T(8,128)(2,1)}, bf16[3,12,2,128,128]{4,3,2,1,0:T(8,128)(2,1)S(1)}, u32[]{:S(2)}, u32[]{:S(2)}) collective-permute-start(bf16[3,12,2,128,128]{4,3,2,1,0:T(8,128)(2,1)} %get-tuple-element.22), channel_id=1, source_target_pairs={{0,1},{1,2},{2,3},{3,4},{4,5},{5,6},{6,7},{8,9},{9,10},{10,11},{11... | collective-permute-start | bytes 7077896 | tf_op jit(solution)/shard_map/ppermute | solution.py:625
  10.9 1.3 %collective-permute-start.5 = (bf16[3,12,2,128,128]{4,3,2,1,0:T(8,128)(2,1)}, bf16[3,12,2,128,128]{4,3,2,1,0:T(8,128)(2,1)}, u32[]{:S(2)}, u32[]{:S(2)}) collective-permute-start(bf16[3,12,2,128,128]{4,3,2,1,0:T(8,128)(2,1)} %get-tuple-element.23), channel_id=1, source_target_pairs={{1,0},{2,1},{3,2},{4,3},{5,4},{6,5},{7,6},{9,8},{10,9},{11,10},{12... | collective-permute-start | bytes 7077896 | tf_op jit(solution)/shard_map/ppermute | solution.py:625
  12.2 1.3 %collective-permute-start.2 = (bf16[3,2,4,128,128]{4,3,2,1,0:T(8,128)(2,1)}, bf16[3,2,4,128,128]{4,3,2,1,0:T(8,128)(2,1)}, u32[]{:S(2)}, u32[]{:S(2)}) collective-permute-start(bf16[3,2,4,128,128]{4,3,2,1,0:T(8,128)(2,1)} %get-tuple-element.18), channel_id=1, source_target_pairs={{8,24},{16,0},{9,25},{17,1},{10,26},{18,2},{11,27},{19,3},{12,28},... | collective-permute-start | bytes 2359304 | tf_op jit(solution)/shard_map/ppermute | solution.py:636
  13.5 5.3 %collective-permute-start = (bf16[3,2,8,128,128]{4,3,2,1,0:T(8,128)(2,1)}, bf16[3,2,8,128,128]{4,3,2,1,0:T(8,128)(2,1)S(1)}, u32[]{:S(2)}, u32[]{:S(2)}) collective-permute-start(bf16[3,2,8,128,128]{4,3,2,1,0:T(8,128)(2,1)} %get-tuple-element.16), channel_id=1, source_target_pairs={{0,8},{8,0},{16,24},{24,16},{1,9},{9,1},{17,25},{25,17},{2,10},{10... | collective-permute-start | bytes 4718600 | tf_op jit(solution)/shard_map/ppermute | solution.py:647
  18.8 1.7 %collective-permute-start.1 = (bf16[3,2,4,128,128]{4,3,2,1,0:T(8,128)(2,1)}, bf16[3,2,4,128,128]{4,3,2,1,0:T(8,128)(2,1)}, u32[]{:S(2)}, u32[]{:S(2)}) collective-permute-start(bf16[3,2,4,128,128]{4,3,2,1,0:T(8,128)(2,1)} %get-tuple-element.17), channel_id=1, source_target_pairs={{8,16},{16,8},{9,17},{17,9},{10,18},{18,10},{11,19},{19,11},{12,20... | collective-permute-start | bytes 2359304 | tf_op jit(solution)/shard_map/ppermute | solution.py:648
  20.4 8.0 %shard_map.60.cells = bf16[3,12,8,128,128]{4,3,2,1,0:T(8,128)(2,1)} custom-call(bf16[128,3,12,8,128]{4,3,2,1,0:T(8,128)(2,1)} %velocity.2), custom_call_target="tpu_custom_call" | custom-call | tf_op jit(solution)/shard_map/pallas_call | solution.py:174
  28.5 4.1 %collective-permute-done.2 = bf16[3,2,4,128,128]{4,3,2,1,0:T(8,128)(2,1)} collective-permute-done((bf16[3,2,4,128,128]{4,3,2,1,0:T(8,128)(2,1)}, bf16[3,2,4,128,128]{4,3,2,1,0:T(8,128)(2,1)}, u32[]{:S(2)}, u32[]{:S(2)}) %collective-permute-start.2) | collective-permute-done | bytes 786464 | tf_op jit(solution)/shard_map/ppermute | solution.py:636
  32.5 4.1 %collective-permute-start.3 = (bf16[3,2,4,128,128]{4,3,2,1,0:T(8,128)(2,1)}, bf16[3,2,4,128,128]{4,3,2,1,0:T(8,128)(2,1)S(1)}, u32[]{:S(2)}, u32[]{:S(2)}) collective-permute-start(bf16[3,2,4,128,128]{4,3,2,1,0:T(8,128)(2,1)} %collective-permute-done.2), channel_id=1, source_target_pairs={{24,16},{0,8},{25,17},{1,9},{26,18},{2,10},{27,19},{3,11},{28,20},... | collective-permute-start | bytes 2359304 | tf_op jit(solution)/shard_map/ppermute | solution.py:637
  36.7 0.1 add_convert_fusion.taps_ref
  36.8 0.0 collective-permute-done.4.low
  36.8 0.0 collective-permute-done.5.high
  36.8 25.5 %shard_map.61 = (bf16[8,128,4096]{2,1,0:T(8,128)(2,1)}, bf16[4,128,1024]{2,1,0:T(8,128)(2,1)S(1)}, f32[4,128,3072]{2,1,0:T(8,128)S(1)}, f32[128,128]{1,0:T(8,128)S(1)}) custom-call(f32[12]{0:T(128)S(1)} %broadcast_multiply_fusion.1.mx_ref, f32[8]{0:T(128)S(1)} %broadcast_multiply_fusion.my_ref, f32[1,128]{1,0:T(1,128)S(1)} %multiply_bitcast_fusion.mz_ref, ...), custom_call_target="tpu_custom_call" | custom-call | tf_op jit(solution)/shard_map/pallas_call | solution.py:319
  62.4 0.0 collective-permute-done.1.far1
  62.4 0.0 collective-permute-done.near
  62.4 7.2 %collective-permute-done.3.far2 = bf16[3,2,4,128,128]{4,3,2,1,0:T(8,128)(2,1)S(1)} collective-permute-done((bf16[3,2,4,128,128]{4,3,2,1,0:T(8,128)(2,1)}, bf16[3,2,4,128,128]{4,3,2,1,0:T(8,128)(2,1)S(1)}, u32[]{:S(2)}, u32[]{:S(2)}) %collective-permute-start.3) | collective-permute-done | bytes 786464 | tf_op jit(solution)/shard_map/ppermute | solution.py:637
  69.6 5.7 %shard_map.62 = (bf16[4,128,3072]{2,1,0:T(8,128)(2,1)S(1)}, f32[72,128]{1,0:T(8,128)S(1)}) custom-call(bf16[3,2,8,128,128]{4,3,2,1,0:T(8,128)(2,1)S(1)} %collective-permute-done.near, bf16[3,2,4,128,128]{4,3,2,1,0:T(8,128)(2,1)} %collective-permute-done.1.far1, bf16[3,2,4,128,128]{4,3,2,1,0:T(8,128)(2,1)S(1)} %collective-permute-done.3.far2, ...), custom_call_target="tpu_custom_call" | custom-call | tf_op jit(solution)/shard_map/pallas_call | solution.py:443
  75.3 1.3 %collective-permute-start.6 = (f32[72,128]{1,0:T(8,128)S(1)}, f32[72,128]{1,0:T(8,128)S(1)}, u32[]{:S(2)}, u32[]{:S(2)}) collective-permute-start(f32[72,128]{1,0:T(8,128)S(1)} %get-tuple-element.26), channel_id=1, source_target_pairs={{0,1},{1,0},{2,3},{3,2},{4,5},{5,4},{6,7},{7,6},{8,9},{9,8},{10,11... | collective-permute-start | bytes 110600 | tf_op jit(solution)/shard_map/ppermute | solution.py:617
  76.6 0.9 collective-permute-done.6
  77.5 5.2 %collective-permute-start.9 = (f32[72,128]{1,0:T(8,128)S(1)}, f32[72,128]{1,0:T(8,128)S(1)}, u32[]{:S(2)}, u32[]{:S(2)}) collective-permute-start(f32[72,128]{1,0:T(8,128)S(1)} %add.60), channel_id=1, source_target_pairs={{0,6},{1,7},{2,4},{3,5},{4,2},{5,3},{6,0},{7,1},{8,14},{9,15},{10,... | collective-permute-start | bytes 110600 | tf_op jit(solution)/shard_map/ppermute | solution.py:617
  82.7 0.0 collective-permute-start.8
  82.7 0.6 collective-permute-start.7
  83.3 1.3 %collective-permute-done.9 = f32[72,128]{1,0:T(8,128)S(1)} collective-permute-done((f32[72,128]{1,0:T(8,128)S(1)}, f32[72,128]{1,0:T(8,128)S(1)}, u32[]{:S(2)}, u32[]{:S(2)}) %collective-permute-start.9) | collective-permute-done | bytes 36896 | tf_op jit(solution)/shard_map/ppermute | solution.py:617
  84.6 2.9 %collective-permute-done.8 = f32[72,128]{1,0:T(8,128)S(1)} collective-permute-done((f32[72,128]{1,0:T(8,128)S(1)}, f32[72,128]{1,0:T(8,128)S(1)}, u32[]{:S(2)}, u32[]{:S(2)}) %collective-permute-start.8) | collective-permute-done | bytes 36896 | tf_op jit(solution)/shard_map/ppermute | solution.py:617
  87.6 0.0 collective-permute-done.7
  87.6 0.1 collective-permute-start.12
  87.7 3.3 %collective-permute-start.11 = (f32[72,128]{1,0:T(8,128)S(1)}, f32[72,128]{1,0:T(8,128)S(1)}, u32[]{:S(2)}, u32[]{:S(2)}) collective-permute-start(f32[72,128]{1,0:T(8,128)S(1)} %add_add_fusion.rest_0_), channel_id=1, source_target_pairs={{0,16},{8,24},{16,0},{24,8},{1,17},{9,25},{17,1},{25,9},{2,18},{10... | collective-permute-start | bytes 110600 | tf_op jit(solution)/shard_map/ppermute | solution.py:617
  90.9 0.4 collective-permute-start.10
  91.3 1.6 %collective-permute-done.12.rest_3_ = f32[72,128]{1,0:T(8,128)S(1)} collective-permute-done((f32[72,128]{1,0:T(8,128)S(1)}, f32[72,128]{1,0:T(8,128)S(1)}, u32[]{:S(2)}, u32[]{:S(2)}) %collective-permute-start.12) | collective-permute-done | bytes 36896 | tf_op jit(solution)/shard_map/ppermute | solution.py:617
  92.9 0.2 collective-permute-done.11.rest_2_
  93.1 1.8 %collective-permute-done.10.rest_1_ = f32[72,128]{1,0:T(8,128)S(1)} collective-permute-done((f32[72,128]{1,0:T(8,128)S(1)}, f32[72,128]{1,0:T(8,128)S(1)}, u32[]{:S(2)}, u32[]{:S(2)}) %collective-permute-start.10) | collective-permute-done | bytes 36896 | tf_op jit(solution)/shard_map/ppermute | solution.py:617
  94.9 13.3 %shard_map.63 = (bf16[128,4,12,8,128]{4,3,2,1,0:T(8,128)(2,1)}, f32[128,128]{1,0:T(8,128)}) custom-call(f32[72,128]{1,0:T(8,128)S(1)} %add_add_fusion.rest_0_, f32[72,128]{1,0:T(8,128)S(1)} %collective-permute-done.10.rest_1_, f32[72,128]{1,0:T(8,128)S(1)} %collective-permute-done.11.rest_2_, f32[72,128]{1,0:T(8,128)S(1)} %collective-permute-done.12.rest_3_, ...), custom_call_target="tpu_custom_call" | custom-call | tf_op jit(solution)/shard_map/pallas_call | solution.py:579
  (15 shorter events, 0.0 us)
Async XLA Ops:
  8.4 28.4 %collective-permute-start.4 = (bf16[3,12,2,128,128]{4,3,2,1,0:T(8,128)(2,1)}, bf16[3,12,2,128,128]{4,3,2,1,0:T(8,128)(2,1)S(1)}, u32[]{:S(2)}, u32[]{:S(2)}) collective-permute-start(bf16[3,12,2,128,128]{4,3,2,1,0:T(8,128)(2,1)} %get-tuple-element.22), channel_id=1, source_target_pairs={{0,1},{1,2},{2,3},{3,4},{4,5},{5,6},{6,7},{8,9},{9,10},{10,11},{11... | collective-permute-start | bytes 7077896 | tf_op jit(solution)/shard_map/ppermute | solution.py:625
  10.9 25.9 %collective-permute-start.5 = (bf16[3,12,2,128,128]{4,3,2,1,0:T(8,128)(2,1)}, bf16[3,12,2,128,128]{4,3,2,1,0:T(8,128)(2,1)}, u32[]{:S(2)}, u32[]{:S(2)}) collective-permute-start(bf16[3,12,2,128,128]{4,3,2,1,0:T(8,128)(2,1)} %get-tuple-element.23), channel_id=1, source_target_pairs={{1,0},{2,1},{3,2},{4,3},{5,4},{6,5},{7,6},{9,8},{10,9},{11,10},{12... | collective-permute-start | bytes 7077896 | tf_op jit(solution)/shard_map/ppermute | solution.py:625
  12.2 20.4 %collective-permute-start.2 = (bf16[3,2,4,128,128]{4,3,2,1,0:T(8,128)(2,1)}, bf16[3,2,4,128,128]{4,3,2,1,0:T(8,128)(2,1)}, u32[]{:S(2)}, u32[]{:S(2)}) collective-permute-start(bf16[3,2,4,128,128]{4,3,2,1,0:T(8,128)(2,1)} %get-tuple-element.18), channel_id=1, source_target_pairs={{8,24},{16,0},{9,25},{17,1},{10,26},{18,2},{11,27},{19,3},{12,28},... | collective-permute-start | bytes 2359304 | tf_op jit(solution)/shard_map/ppermute | solution.py:636
  13.5 48.9 %collective-permute-start = (bf16[3,2,8,128,128]{4,3,2,1,0:T(8,128)(2,1)}, bf16[3,2,8,128,128]{4,3,2,1,0:T(8,128)(2,1)S(1)}, u32[]{:S(2)}, u32[]{:S(2)}) collective-permute-start(bf16[3,2,8,128,128]{4,3,2,1,0:T(8,128)(2,1)} %get-tuple-element.16), channel_id=1, source_target_pairs={{0,8},{8,0},{16,24},{24,16},{1,9},{9,1},{17,25},{25,17},{2,10},{10... | collective-permute-start | bytes 4718600 | tf_op jit(solution)/shard_map/ppermute | solution.py:647
  18.8 9.7 %copy-start.1 = (f32[12]{0:T(128)S(1)}, f32[12]{0:T(128)}, u32[]{:S(2)}) copy-start(f32[12]{0:T(128)} %param.5) | copy-start | bytes 148
  18.8 17.9 %copy-start.2 = (f32[8]{0:T(128)S(1)}, f32[8]{0:T(128)}, u32[]{:S(2)}) copy-start(f32[8]{0:T(128)} %param.6) | copy-start | bytes 100
  18.8 17.9 %copy-start.3 = (f32[128]{0:T(128)S(1)}, f32[128]{0:T(128)}, u32[]{:S(2)}) copy-start(f32[128]{0:T(128)} %param.7) | copy-start | bytes 1540
  18.8 43.6 %collective-permute-start.1 = (bf16[3,2,4,128,128]{4,3,2,1,0:T(8,128)(2,1)}, bf16[3,2,4,128,128]{4,3,2,1,0:T(8,128)(2,1)}, u32[]{:S(2)}, u32[]{:S(2)}) collective-permute-start(bf16[3,2,4,128,128]{4,3,2,1,0:T(8,128)(2,1)} %get-tuple-element.17), channel_id=1, source_target_pairs={{8,16},{16,8},{9,17},{17,9},{10,18},{18,10},{11,19},{19,11},{12,20... | collective-permute-start | bytes 2359304 | tf_op jit(solution)/shard_map/ppermute | solution.py:648
  32.5 37.1 %collective-permute-start.3 = (bf16[3,2,4,128,128]{4,3,2,1,0:T(8,128)(2,1)}, bf16[3,2,4,128,128]{4,3,2,1,0:T(8,128)(2,1)S(1)}, u32[]{:S(2)}, u32[]{:S(2)}) collective-permute-start(bf16[3,2,4,128,128]{4,3,2,1,0:T(8,128)(2,1)} %collective-permute-done.2), channel_id=1, source_target_pairs={{24,16},{0,8},{25,17},{1,9},{26,18},{2,10},{27,19},{3,11},{28,20},... | collective-permute-start | bytes 2359304 | tf_op jit(solution)/shard_map/ppermute | solution.py:637
  69.6 25.3 %copy-start = (bf16[8,128,4096]{2,1,0:T(8,128)(2,1)S(1)}, bf16[8,128,4096]{2,1,0:T(8,128)(2,1)}, u32[]{:S(2)}) copy-start(bf16[8,128,4096]{2,1,0:T(8,128)(2,1)} %get-tuple-element.27.rest_4_) | copy-start | bytes 25165828
  75.3 2.1 %collective-permute-start.6 = (f32[72,128]{1,0:T(8,128)S(1)}, f32[72,128]{1,0:T(8,128)S(1)}, u32[]{:S(2)}, u32[]{:S(2)}) collective-permute-start(f32[72,128]{1,0:T(8,128)S(1)} %get-tuple-element.26), channel_id=1, source_target_pairs={{0,1},{1,0},{2,3},{3,2},{4,5},{5,4},{6,7},{7,6},{8,9},{9,8},{10,11... | collective-permute-start | bytes 110600 | tf_op jit(solution)/shard_map/ppermute | solution.py:617
  77.5 7.1 %collective-permute-start.9 = (f32[72,128]{1,0:T(8,128)S(1)}, f32[72,128]{1,0:T(8,128)S(1)}, u32[]{:S(2)}, u32[]{:S(2)}) collective-permute-start(f32[72,128]{1,0:T(8,128)S(1)} %add.60), channel_id=1, source_target_pairs={{0,6},{1,7},{2,4},{3,5},{4,2},{5,3},{6,0},{7,1},{8,14},{9,15},{10,... | collective-permute-start | bytes 110600 | tf_op jit(solution)/shard_map/ppermute | solution.py:617
  82.7 4.9 %collective-permute-start.8 = (f32[72,128]{1,0:T(8,128)S(1)}, f32[72,128]{1,0:T(8,128)S(1)}, u32[]{:S(2)}, u32[]{:S(2)}) collective-permute-start(f32[72,128]{1,0:T(8,128)S(1)} %add.60), channel_id=1, source_target_pairs={{0,4},{1,5},{2,6},{3,7},{4,0},{5,1},{6,2},{7,3},{8,12},{9,13},{10,... | collective-permute-start | bytes 110600 | tf_op jit(solution)/shard_map/ppermute | solution.py:617
  82.7 4.9 %collective-permute-start.7 = (f32[72,128]{1,0:T(8,128)S(1)}, f32[72,128]{1,0:T(8,128)S(1)}, u32[]{:S(2)}, u32[]{:S(2)}) collective-permute-start(f32[72,128]{1,0:T(8,128)S(1)} %add.60), channel_id=1, source_target_pairs={{0,2},{1,3},{2,0},{3,1},{4,6},{5,7},{6,4},{7,5},{8,10},{9,11},{10,... | collective-permute-start | bytes 110600 | tf_op jit(solution)/shard_map/ppermute | solution.py:617
  87.6 5.3 %collective-permute-start.12 = (f32[72,128]{1,0:T(8,128)S(1)}, f32[72,128]{1,0:T(8,128)S(1)}, u32[]{:S(2)}, u32[]{:S(2)}) collective-permute-start(f32[72,128]{1,0:T(8,128)S(1)} %add_add_fusion.rest_0_), channel_id=1, source_target_pairs={{0,24},{8,16},{16,8},{24,0},{1,25},{9,17},{17,9},{25,1},{2,26},{10... | collective-permute-start | bytes 110600 | tf_op jit(solution)/shard_map/ppermute | solution.py:617
  87.7 5.4 %collective-permute-start.11 = (f32[72,128]{1,0:T(8,128)S(1)}, f32[72,128]{1,0:T(8,128)S(1)}, u32[]{:S(2)}, u32[]{:S(2)}) collective-permute-start(f32[72,128]{1,0:T(8,128)S(1)} %add_add_fusion.rest_0_), channel_id=1, source_target_pairs={{0,16},{8,24},{16,0},{24,8},{1,17},{9,25},{17,1},{25,9},{2,18},{10... | collective-permute-start | bytes 110600 | tf_op jit(solution)/shard_map/ppermute | solution.py:617
  90.9 4.0 %collective-permute-start.10 = (f32[72,128]{1,0:T(8,128)S(1)}, f32[72,128]{1,0:T(8,128)S(1)}, u32[]{:S(2)}, u32[]{:S(2)}) collective-permute-start(f32[72,128]{1,0:T(8,128)S(1)} %add_add_fusion.rest_0_), channel_id=1, source_target_pairs={{0,8},{8,0},{16,24},{24,16},{1,9},{9,1},{17,25},{25,17},{2,10},{10... | collective-permute-start | bytes 110600 | tf_op jit(solution)/shard_map/ppermute | solution.py:617
